TPU v7x, 512 devices: a whole 4x4x16 slice. The times are simulated.
512 devices in a mesh: gx: 32 (over y, x, core), gy: 16 (over z).
Axes of the slice: x: 4, y: 4, z: 16, core: 2. Of those that a mesh axis runs over, the one named last changes fastest.
Arguments:
- phi_start: float32 [256, 128, 512], P('gx', 'gy'), may hold values from -6 to 6
- right_side: float32 [256, 128, 512], P('gx', 'gy'), may hold values from -8 to 8
- coefficient: float32 [256, 128, 512], P('gx', 'gy'), may hold values from 0.25 to 4
Outputs:
- phi_fine: float32 [256, 128, 512], P('gx', 'gy')
- correction: float32 [128, 64, 256], P('gx', 'gy')
All inputs are finite; a program needn't handle non-finite values.
Results may differ from a plain program's by a relative error of at most 0.0003.
Values sent between devices are 32-bit elements; how exact they have to be, the bound alone decides.
No kernel may reach another device: no remote copies, remote signals or barrier semaphores. Data moves between devices by JAX's collectives and lax.ppermute only.
A program may use at most 64 MiB of HBM per device.

v0:
```python
import jax
import jax.numpy as jnp
from jax import lax
from jax.sharding import PartitionSpec as P

BOTTOM = 6


RELAX_WEIGHT = 0.8


def extended(shard, sides, width):
    for axis, dim in sides:
        devices, length = (lax.axis_size(axis), shard.shape[dim])
        up = [(i, (i + 1) % devices) for i in range(devices - 1)]
        down = [(j, i) for i, j in up]
        last = lax.slice_in_dim(shard, length - width, length, axis=dim)
        leading = lax.slice_in_dim(shard, 0, width, axis=dim)
        before = lax.ppermute(last, axis, up)
        after = lax.ppermute(leading, axis, down)
        shard = jnp.concatenate([before, shard, after], axis=dim)
    return shard


def neighbour_views(padded):
    return [
        padded[2:, 1:-1, 1:-1],
        padded[:-2, 1:-1, 1:-1],
        padded[1:-1, 2:, 1:-1],
        padded[1:-1, :-2, 1:-1],
        padded[1:-1, 1:-1, 2:],
        padded[1:-1, 1:-1, :-2],
    ]


def face_weights(padded_coef):
    centre = padded_coef[1:-1, 1:-1, 1:-1]
    weights = []
    for neighbour in neighbour_views(padded_coef):
        weights.append(
            jnp.where(neighbour > 0.0, 2.0 * centre * neighbour / (centre + neighbour), centre)
        )
    diagonal = weights[0] + weights[1] + weights[2] + weights[3] + weights[4] + weights[5]
    return (weights, diagonal)


def apply_operator(padded, weights, diagonal):
    result = diagonal * padded[1:-1, 1:-1, 1:-1]
    for weight, neighbour in zip(weights, neighbour_views(padded)):
        result = result - weight * neighbour
    return result


def relax_once(current, padded, source, weights, diagonal):
    return current + RELAX_WEIGHT * (source - apply_operator(padded, weights, diagonal)) / diagonal


def descend(source, coef_level, start, extend):
    weights, diagonal = face_weights(extend(coef_level))
    if start is None:
        current = RELAX_WEIGHT * source / diagonal
    else:
        current = relax_once(start, extend(start), source, weights, diagonal)
    current = relax_once(current, extend(current), source, weights, diagonal)
    residual = source - apply_operator(extend(current), weights, diagonal)
    return (current, residual)


def restrict(values, scale):
    size_x, size_y, size_z = values.shape
    blocks = values.reshape(size_x // 2, 2, size_y // 2, 2, size_z // 2, 2)
    return scale * jnp.mean(blocks, axis=(1, 3, 5))


def prolong(values):
    return jnp.repeat(jnp.repeat(jnp.repeat(values, 2, axis=0), 2, axis=1), 2, axis=2)


def pad_zero(values):
    return jnp.pad(values, 1)


def bottom_solve(source, coef_level):
    weights, diagonal = face_weights(pad_zero(coef_level))
    solution = jnp.zeros_like(source)
    residual = source
    direction = source
    norm_now = jnp.sum(residual * residual)
    for iteration in range(BOTTOM):
        image = apply_operator(pad_zero(direction), weights, diagonal)
        step_size = norm_now / jnp.sum(direction * image)
        solution = solution + step_size * direction
        residual = residual - step_size * image
        norm_next = jnp.sum(residual * residual)
        direction = residual + norm_next / norm_now * direction
        norm_now = norm_next
    return solution


def shards(phi_start, right_side, coefficient):

    def extend_fine(values):
        padded = extended(values, (("gx", 0), ("gy", 1)), 1)
        return jnp.pad(padded, ((0, 0), (0, 0), (1, 1)))

    def extend_mid(values):
        padded = extended(values, (("gx", 0), ("gy", 1)), 1)
        return jnp.pad(padded, ((0, 0), (0, 0), (1, 1)))

    phi_fine, residual = descend(right_side, coefficient, phi_start, extend_fine)
    source_mid = restrict(residual, 4.0)
    coef_mid = restrict(coefficient, 1.0)
    error_mid, residual_mid = descend(source_mid, coef_mid, None, extend_mid)
    source_low = restrict(residual_mid, 4.0)
    coef_low = restrict(coef_mid, 1.0)
    column_x = lax.axis_index("gx")
    column_y = lax.axis_index("gy")

    def extend_column(values):
        padded = extended(values, (("gx", 0),), 1)
        return jnp.pad(padded, ((0, 0), (1, 1), (1, 1)))

    source_col, coef_col = (
        lax.all_gather(source_low, "gy", axis=1, tiled=True),
        lax.all_gather(coef_low, "gy", axis=1, tiled=True),
    )
    error_low, residual_low = descend(source_col, coef_col, None, extend_column)
    source_bottom = restrict(residual_low, 4.0)
    coef_bottom = restrict(coef_col, 1.0)
    slab_rows = source_bottom.shape[0]
    stacked = jnp.stack([source_bottom, coef_bottom])
    collected = lax.all_gather(stacked, "gx", axis=1, tiled=True)
    error_bottom = bottom_solve(collected[0], collected[1])
    slab = lax.dynamic_slice_in_dim(error_bottom, column_x * slab_rows, slab_rows, 0)
    total_low = error_low + prolong(slab)
    span_y = error_mid.shape[1] // 2
    correction = error_mid + prolong(
        lax.dynamic_slice_in_dim(total_low, column_y * span_y, span_y, 1)
    )
    return (phi_fine, correction)


def solution(mesh):
    return jax.shard_map(
        shards,
        mesh=mesh,
        in_specs=(P("gx", "gy", None), P("gx", "gy", None), P("gx", "gy", None)),
        out_specs=(P("gx", "gy", None), P("gx", "gy", None)),
        check_vma=False,
    )
```

profile of v0, /device:TPU:1, one launch (start us, length us, event | category | flops | bytes accessed | tf_op | source)
XLA Modules:
  0.0 285.9 jit_solution(14458566404459489684)
XLA Ops:
  0.6 0.7 fusion.192
  1.4 4.5 %collective-permute-start.1 = (f32[1,8,512]{2,1,0:T(8,128)S(1)}, f32[1,8,512]{2,1,0:T(8,128)S(1)}, u32[]{:S(2)}, u32[]{:S(2)}) collective-permute-start(f32[1,8,512]{2,1,0:T(8,128)S(1)} %get-tuple-element.50), channel_id=1, source_target_pairs={{0,16},{16,32},{32,48},{48,64},{64,80},{80,96},{96,112},{112,128},... | collective-permute-start | bytes 49160 | tf_op jit(solution)/shard_map/ppermute | solution.py:19
  5.9 5.6 %collective-permute-start = (f32[1,8,512]{2,1,0:T(8,128)S(1)}, f32[1,8,512]{2,1,0:T(8,128)S(1)}, u32[]{:S(2)}, u32[]{:S(2)}) collective-permute-start(f32[1,8,512]{2,1,0:T(8,128)S(1)} %get-tuple-element.49), channel_id=1, source_target_pairs={{16,0},{32,16},{48,32},{64,48},{80,64},{96,80},{112,96},{128,112},... | collective-permute-start | bytes 49160 | tf_op jit(solution)/shard_map/ppermute | solution.py:20
  11.5 0.7 fusion.193
  12.2 1.9 collective-permute-start.5
  14.1 2.5 collective-permute-start.4
  16.7 10.5 %reshape.63 = f32[4,2,4,2,256,2]{5,4,3,2,1,0:T(8,128)} reshape(f32[8,8,512]{2,1,0:T(8,128)} %param.5) | data formatting | bytes 262144 | tf_op jit(solution)/shard_map/reshape | solution.py:71
  27.2 4.0 %reduce_sum.177 = f32[4,4,256]{2,1,0:T(4,128)S(1)} reduce(f32[4,2,4,2,256,2]{5,4,3,2,1,0:T(8,128)} %reshape.63, f32[]{:T(128)} %constant.15.clone.1), dimensions={1,3,5}, to_apply=%region_1.2 | reduce | flops 28672 | bytes 147460 | tf_op jit(solution)/shard_map/reduce_sum | solution.py:72
  31.3 1.3 collective-permute-start.2
  32.6 4.0 %collective-permute-start.3 = (f32[10,1,512]{2,1,0:T(1,128)S(1)}, f32[10,1,512]{2,1,0:T(1,128)S(1)}, u32[]{:S(2)}, u32[]{:S(2)}) collective-permute-start(f32[10,1,512]{2,1,0:T(1,128)S(1)} %get-tuple-element.41), channel_id=1, source_target_pairs={{0,1},{1,2},{2,3},{3,4},{4,5},{5,6},{6,7},{7,8},{8,9},{9,10},{10,1... | collective-permute-start | bytes 61448 | tf_op jit(solution)/shard_map/ppermute | solution.py:19
  36.7 1.3 collective-permute-start.6
  38.0 4.0 %collective-permute-start.7 = (f32[10,1,512]{2,1,0:T(1,128)S(1)}, f32[10,1,512]{2,1,0:T(1,128)S(1)}, u32[]{:S(2)}, u32[]{:S(2)}) collective-permute-start(f32[10,1,512]{2,1,0:T(1,128)S(1)} %get-tuple-element.43), channel_id=1, source_target_pairs={{0,1},{1,2},{2,3},{3,4},{4,5},{5,6},{6,7},{7,8},{8,9},{9,10},{10,1... | collective-permute-start | bytes 61448 | tf_op jit(solution)/shard_map/ppermute | solution.py:19
  43.6 3.0 %collective-permute-start.8 = (f32[1,8,512]{2,1,0:T(8,128)S(1)}, f32[1,8,512]{2,1,0:T(8,128)S(1)}, u32[]{:S(2)}, u32[]{:S(2)}) collective-permute-start(f32[1,8,512]{2,1,0:T(8,128)S(1)} %get-tuple-element.48), channel_id=1, source_target_pairs={{16,0},{32,16},{48,32},{64,48},{80,64},{96,80},{112,96},{128,112},... | collective-permute-start | bytes 49160 | tf_op jit(solution)/shard_map/ppermute | solution.py:20
  46.6 3.8 %collective-permute-start.9 = (f32[1,8,512]{2,1,0:T(8,128)S(1)}, f32[1,8,512]{2,1,0:T(8,128)S(1)}, u32[]{:S(2)}, u32[]{:S(2)}) collective-permute-start(f32[1,8,512]{2,1,0:T(8,128)S(1)} %get-tuple-element.47), channel_id=1, source_target_pairs={{0,16},{16,32},{32,48},{48,64},{64,80},{80,96},{96,112},{112,128},... | collective-permute-start | bytes 49160 | tf_op jit(solution)/shard_map/ppermute | solution.py:19
  50.5 0.8 collective-permute-done.9
  51.3 1.3 collective-permute-start.10
  52.6 4.6 %collective-permute-start.11 = (f32[10,1,512]{2,1,0:T(1,128)S(1)}, f32[10,1,512]{2,1,0:T(1,128)S(1)}, u32[]{:S(2)}, u32[]{:S(2)}) collective-permute-start(f32[10,1,512]{2,1,0:T(1,128)S(1)} %get-tuple-element.39), channel_id=1, source_target_pairs={{0,1},{1,2},{2,3},{3,4},{4,5},{5,6},{6,7},{7,8},{8,9},{9,10},{10,1... | collective-permute-start | bytes 61448 | tf_op jit(solution)/shard_map/ppermute | solution.py:19
  57.2 1.9 collective-permute-start.16
  59.1 4.5 %collective-permute-start.17 = (f32[1,4,256]{2,1,0:T(4,128)S(1)}, f32[1,4,256]{2,1,0:T(4,128)S(1)}, u32[]{:S(2)}, u32[]{:S(2)}) collective-permute-start(f32[1,4,256]{2,1,0:T(4,128)S(1)} %get-tuple-element.71), channel_id=1, source_target_pairs={{0,16},{16,32},{32,48},{48,64},{64,80},{80,96},{96,112},{112,128},... | collective-permute-start | bytes 12296 | tf_op jit(solution)/shard_map/ppermute | solution.py:19
  63.6 1.0 div.156
  65.5 1.9 collective-permute-start.12
  67.4 3.6 %collective-permute-start.13 = (f32[1,8,512]{2,1,0:T(8,128)S(1)}, f32[1,8,512]{2,1,0:T(8,128)S(1)}, u32[]{:S(2)}, u32[]{:S(2)}) collective-permute-start(f32[1,8,512]{2,1,0:T(8,128)S(1)} %get-tuple-element.45), channel_id=1, source_target_pairs={{0,16},{16,32},{32,48},{48,64},{64,80},{80,96},{96,112},{112,128},... | collective-permute-start | bytes 49160 | tf_op jit(solution)/shard_map/ppermute | solution.py:19
  71.1 1.3 collective-permute-start.18
  72.4 4.3 %collective-permute-start.19 = (f32[6,1,256]{2,1,0:T(1,128)S(1)}, f32[6,1,256]{2,1,0:T(1,128)S(1)}, u32[]{:S(2)}, u32[]{:S(2)}) collective-permute-start(f32[6,1,256]{2,1,0:T(1,128)S(1)} %get-tuple-element.65), channel_id=1, source_target_pairs={{0,1},{1,2},{2,3},{3,4},{4,5},{5,6},{6,7},{7,8},{8,9},{9,10},{10,1... | collective-permute-start | bytes 18440 | tf_op jit(solution)/shard_map/ppermute | solution.py:19
  76.7 1.3 collective-permute-start.14
  78.0 4.2 %collective-permute-start.15 = (f32[10,1,512]{2,1,0:T(1,128)S(1)}, f32[10,1,512]{2,1,0:T(1,128)S(1)}, u32[]{:S(2)}, u32[]{:S(2)}) collective-permute-start(f32[10,1,512]{2,1,0:T(1,128)S(1)} %get-tuple-element.37), channel_id=1, source_target_pairs={{0,1},{1,2},{2,3},{3,4},{4,5},{5,6},{6,7},{7,8},{8,9},{9,10},{10,1... | collective-permute-start | bytes 61448 | tf_op jit(solution)/shard_map/ppermute | solution.py:19
  82.4 0.7 collective-permute-done.15
  83.7 9.7 %reshape.62 = f32[4,2,4,2,256,2]{5,4,3,2,1,0:T(8,128)} reshape(f32[8,8,512]{2,1,0:T(8,128)S(1)} %fusion.79) | data formatting | bytes 262144 | tf_op jit(solution)/shard_map/reshape | solution.py:71
  93.5 4.0 %reduce_sum.176 = f32[4,4,256]{2,1,0:T(4,128)S(1)} reduce(f32[4,2,4,2,256,2]{5,4,3,2,1,0:T(8,128)} %reshape.62, f32[]{:T(128)} %constant.15.clone.1), dimensions={1,3,5}, to_apply=%region_0.1 | reduce | flops 28672 | bytes 147460 | tf_op jit(solution)/shard_map/reduce_sum | solution.py:72
  97.6 1.9 collective-permute-start.20
  99.5 3.6 %collective-permute-start.21 = (f32[1,4,256]{2,1,0:T(4,128)S(1)}, f32[1,4,256]{2,1,0:T(4,128)S(1)}, u32[]{:S(2)}, u32[]{:S(2)}) collective-permute-start(f32[1,4,256]{2,1,0:T(4,128)S(1)} %get-tuple-element.69), channel_id=1, source_target_pairs={{0,16},{16,32},{32,48},{48,64},{64,80},{80,96},{96,112},{112,128},... | collective-permute-start | bytes 12296 | tf_op jit(solution)/shard_map/ppermute | solution.py:19
  103.2 0.7 collective-permute-done.21
  103.9 1.3 collective-permute-start.22
  105.2 5.8 %collective-permute-start.23 = (f32[6,1,256]{2,1,0:T(1,128)S(1)}, f32[6,1,256]{2,1,0:T(1,128)S(1)}, u32[]{:S(2)}, u32[]{:S(2)}) collective-permute-start(f32[6,1,256]{2,1,0:T(1,128)S(1)} %get-tuple-element.63), channel_id=1, source_target_pairs={{0,1},{1,2},{2,3},{3,4},{4,5},{5,6},{6,7},{7,8},{8,9},{9,10},{10,1... | collective-permute-start | bytes 18440 | tf_op jit(solution)/shard_map/ppermute | solution.py:19
  111.0 31.3 %all_gather.10 = f32[2,32,128]{2,0,1:T(2,128)S(1)} all-gather(f32[2,2,128]{2,0,1:T(2,128)S(1)} %copy.63), channel_id=1, replica_groups=mesh['gx'=32,'gy'=16] {'gy'}, dimensions={1}, use_global_device_ids=true | all-gather | bytes 34816 | tf_op jit(solution)/shard_map/all_gather | solution.py:125
  142.6 8.3 %collective-permute-start.24 = (f32[1,4,256]{2,1,0:T(4,128)S(1)}, f32[1,4,256]{2,1,0:T(4,128)S(1)}, u32[]{:S(2)}, u32[]{:S(2)}) collective-permute-start(f32[1,4,256]{2,1,0:T(4,128)S(1)} %get-tuple-element.68), channel_id=1, source_target_pairs={{16,0},{32,16},{48,32},{64,48},{80,64},{96,80},{112,96},{128,112},... | collective-permute-start | bytes 12296 | tf_op jit(solution)/shard_map/ppermute | solution.py:20
  150.9 4.9 %collective-permute-start.25 = (f32[1,4,256]{2,1,0:T(4,128)S(1)}, f32[1,4,256]{2,1,0:T(4,128)S(1)}, u32[]{:S(2)}, u32[]{:S(2)}) collective-permute-start(f32[1,4,256]{2,1,0:T(4,128)S(1)} %get-tuple-element.67), channel_id=1, source_target_pairs={{0,16},{16,32},{32,48},{48,64},{64,80},{80,96},{96,112},{112,128},... | collective-permute-start | bytes 12296 | tf_op jit(solution)/shard_map/ppermute | solution.py:19
  155.8 1.9 collective-permute-start.28
  157.7 3.6 %collective-permute-start.29 = (f32[1,32,128]{2,0,1:T(1,128)S(1)}, f32[1,32,128]{2,0,1:T(1,128)S(1)}, u32[]{:S(2)}, u32[]{:S(2)}) collective-permute-start(f32[1,32,128]{2,0,1:T(1,128)S(1)} %get-tuple-element.59), channel_id=1, source_target_pairs={{0,16},{16,32},{32,48},{48,64},{64,80},{80,96},{96,112},{112,128},... | collective-permute-start | bytes 49160 | tf_op jit(solution)/shard_map/ppermute | solution.py:19
  161.4 1.3 collective-permute-start.26
  162.7 4.0 %collective-permute-start.27 = (f32[6,1,256]{2,1,0:T(1,128)S(1)}, f32[6,1,256]{2,1,0:T(1,128)S(1)}, u32[]{:S(2)}, u32[]{:S(2)}) collective-permute-start(f32[6,1,256]{2,1,0:T(1,128)S(1)} %get-tuple-element.61), channel_id=1, source_target_pairs={{0,1},{1,2},{2,3},{3,4},{4,5},{5,6},{6,7},{7,8},{8,9},{9,10},{10,1... | collective-permute-start | bytes 18440 | tf_op jit(solution)/shard_map/ppermute | solution.py:19
  167.7 1.0 reshape.64
  168.9 22.3 %all_gather.9 = f32[2,32,128]{2,0,1:T(2,128)S(1)} all-gather(f32[2,2,128]{2,0,1:T(2,128)S(1)} %copy.62), channel_id=1, replica_groups=mesh['gx'=32,'gy'=16] {'gy'}, dimensions={1}, use_global_device_ids=true | all-gather | bytes 34816 | tf_op jit(solution)/shard_map/all_gather | solution.py:124
  191.6 9.1 %collective-permute-start.30 = (f32[1,32,128]{2,0,1:T(1,128)S(1)}, f32[1,32,128]{2,0,1:T(1,128)S(1)}, u32[]{:S(2)}, u32[]{:S(2)}) collective-permute-start(f32[1,32,128]{2,0,1:T(1,128)S(1)} %get-tuple-element.58), channel_id=1, source_target_pairs={{16,0},{32,16},{48,32},{64,48},{80,64},{96,80},{112,96},{128,112},... | collective-permute-start | bytes 49160 | tf_op jit(solution)/shard_map/ppermute | solution.py:20
  200.7 3.3 %collective-permute-start.31 = (f32[1,32,128]{2,0,1:T(1,128)S(1)}, f32[1,32,128]{2,0,1:T(1,128)S(1)}, u32[]{:S(2)}, u32[]{:S(2)}) collective-permute-start(f32[1,32,128]{2,0,1:T(1,128)S(1)} %get-tuple-element.57), channel_id=1, source_target_pairs={{0,16},{16,32},{32,48},{48,64},{64,80},{80,96},{96,112},{112,128},... | collective-permute-start | bytes 49160 | tf_op jit(solution)/shard_map/ppermute | solution.py:19
  204.1 0.7 collective-permute-done.31
  205.5 1.9 collective-permute-start.32
  207.4 4.2 %collective-permute-start.33 = (f32[1,32,128]{2,0,1:T(1,128)S(1)}, f32[1,32,128]{2,0,1:T(1,128)S(1)}, u32[]{:S(2)}, u32[]{:S(2)}) collective-permute-start(f32[1,32,128]{2,0,1:T(1,128)S(1)} %get-tuple-element.53), channel_id=1, source_target_pairs={{0,16},{16,32},{32,48},{48,64},{64,80},{80,96},{96,112},{112,128},... | collective-permute-start | bytes 49160 | tf_op jit(solution)/shard_map/ppermute | solution.py:19
  211.6 1.0 reduce_sum.184
  213.7 1.0 reduce_sum.181
  214.9 44.0 %all_gather.11 = f32[2,32,16,64]{3,2,1,0:T(8,128)S(1)} all-gather(f32[2,1,16,64]{3,2,1,0:T(8,128)S(1)} %pad_maximum_fusion.60), channel_id=1, replica_groups=mesh['gx'=32,'gy'=16] {'gx'}, dimensions={1}, use_global_device_ids=true | all-gather | bytes 270336 | tf_op jit(solution)/shard_map/all_gather | solution.py:132
  258.9 1.4 multiply_reduce_fusion.9
  261.6 0.7 multiply_reduce_fusion.8
  263.7 0.9 multiply_reduce_fusion.7
  265.9 0.7 multiply_reduce_fusion.6
  268.0 0.9 multiply_reduce_fusion.5
  270.2 0.7 multiply_reduce_fusion.4
  272.2 0.9 multiply_reduce_fusion.3
  274.4 0.7 multiply_reduce_fusion.2
  276.5 0.9 multiply_reduce_fusion.1
  278.7 0.7 multiply_reduce_fusion
  280.7 0.7 copy-done.3
  281.4 1.0 fusion.74
  283.8 0.7 fusion.178
  (109 shorter events, 8.8 us)
Async XLA Ops:
  1.4 29.8 %collective-permute-start.1 = (f32[1,8,512]{2,1,0:T(8,128)S(1)}, f32[1,8,512]{2,1,0:T(8,128)S(1)}, u32[]{:S(2)}, u32[]{:S(2)}) collective-permute-start(f32[1,8,512]{2,1,0:T(8,128)S(1)} %get-tuple-element.50), channel_id=1, source_target_pairs={{0,16},{16,32},{32,48},{48,64},{64,80},{80,96},{96,112},{112,128},... | collective-permute-start | bytes 49160 | tf_op jit(solution)/shard_map/ppermute | solution.py:19
  5.9 25.4 %collective-permute-start = (f32[1,8,512]{2,1,0:T(8,128)S(1)}, f32[1,8,512]{2,1,0:T(8,128)S(1)}, u32[]{:S(2)}, u32[]{:S(2)}) collective-permute-start(f32[1,8,512]{2,1,0:T(8,128)S(1)} %get-tuple-element.49), channel_id=1, source_target_pairs={{16,0},{32,16},{48,32},{64,48},{80,64},{96,80},{112,96},{128,112},... | collective-permute-start | bytes 49160 | tf_op jit(solution)/shard_map/ppermute | solution.py:20
  12.2 24.4 %collective-permute-start.5 = (f32[1,8,512]{2,1,0:T(8,128)S(1)}, f32[1,8,512]{2,1,0:T(8,128)S(1)}, u32[]{:S(2)}, u32[]{:S(2)}) collective-permute-start(f32[1,8,512]{2,1,0:T(8,128)S(1)} %get-tuple-element.52), channel_id=1, source_target_pairs={{0,16},{16,32},{32,48},{48,64},{64,80},{80,96},{96,112},{112,128},... | collective-permute-start | bytes 49160 | tf_op jit(solution)/shard_map/ppermute | solution.py:19
  14.1 17.1 %copy-start = (f32[8,8,512]{2,1,0:T(8,128)S(1)}, f32[8,8,512]{2,1,0:T(8,128)}, u32[]{:S(2)}) copy-start(f32[8,8,512]{2,1,0:T(8,128)} %param.5) | copy-start | bytes 393220
  14.1 22.5 %copy-start.4 = (f32[8,8,512]{2,1,0:T(8,128)S(1)}, f32[8,8,512]{2,1,0:T(8,128)}, u32[]{:S(2)}) copy-start(f32[8,8,512]{2,1,0:T(8,128)} %param.3) | copy-start | bytes 393220
  14.1 29.1 %copy-start.2 = (f32[8,8,512]{2,1,0:T(8,128)S(1)}, f32[8,8,512]{2,1,0:T(8,128)}, u32[]{:S(2)}) copy-start(f32[8,8,512]{2,1,0:T(8,128)} %param.4) | copy-start | bytes 393220
  14.1 22.5 %collective-permute-start.4 = (f32[1,8,512]{2,1,0:T(8,128)S(1)}, f32[1,8,512]{2,1,0:T(8,128)S(1)}, u32[]{:S(2)}, u32[]{:S(2)}) collective-permute-start(f32[1,8,512]{2,1,0:T(8,128)S(1)} %get-tuple-element.51), channel_id=1, source_target_pairs={{16,0},{32,16},{48,32},{64,48},{80,64},{96,80},{112,96},{128,112},... | collective-permute-start | bytes 49160 | tf_op jit(solution)/shard_map/ppermute | solution.py:20
  31.3 10.7 %collective-permute-start.2 = (f32[10,1,512]{2,1,0:T(1,128)S(1)}, f32[10,1,512]{2,1,0:T(1,128)S(1)}, u32[]{:S(2)}, u32[]{:S(2)}) collective-permute-start(f32[10,1,512]{2,1,0:T(1,128)S(1)} %get-tuple-element.42), channel_id=1, source_target_pairs={{1,0},{2,1},{3,2},{4,3},{5,4},{6,5},{7,6},{8,7},{9,8},{10,9},{11,1... | collective-permute-start | bytes 61448 | tf_op jit(solution)/shard_map/ppermute | solution.py:20
  32.6 9.4 %collective-permute-start.3 = (f32[10,1,512]{2,1,0:T(1,128)S(1)}, f32[10,1,512]{2,1,0:T(1,128)S(1)}, u32[]{:S(2)}, u32[]{:S(2)}) collective-permute-start(f32[10,1,512]{2,1,0:T(1,128)S(1)} %get-tuple-element.41), channel_id=1, source_target_pairs={{0,1},{1,2},{2,3},{3,4},{4,5},{5,6},{6,7},{7,8},{8,9},{9,10},{10,1... | collective-permute-start | bytes 61448 | tf_op jit(solution)/shard_map/ppermute | solution.py:19
  36.7 5.6 %collective-permute-start.6 = (f32[10,1,512]{2,1,0:T(1,128)S(1)}, f32[10,1,512]{2,1,0:T(1,128)S(1)}, u32[]{:S(2)}, u32[]{:S(2)}) collective-permute-start(f32[10,1,512]{2,1,0:T(1,128)S(1)} %get-tuple-element.44), channel_id=1, source_target_pairs={{1,0},{2,1},{3,2},{4,3},{5,4},{6,5},{7,6},{8,7},{9,8},{10,9},{11,1... | collective-permute-start | bytes 61448 | tf_op jit(solution)/shard_map/ppermute | solution.py:20
  38.0 4.9 %collective-permute-start.7 = (f32[10,1,512]{2,1,0:T(1,128)S(1)}, f32[10,1,512]{2,1,0:T(1,128)S(1)}, u32[]{:S(2)}, u32[]{:S(2)}) collective-permute-start(f32[10,1,512]{2,1,0:T(1,128)S(1)} %get-tuple-element.43), channel_id=1, source_target_pairs={{0,1},{1,2},{2,3},{3,4},{4,5},{5,6},{6,7},{7,8},{8,9},{9,10},{10,1... | collective-permute-start | bytes 61448 | tf_op jit(solution)/shard_map/ppermute | solution.py:19
  43.6 6.8 %collective-permute-start.8 = (f32[1,8,512]{2,1,0:T(8,128)S(1)}, f32[1,8,512]{2,1,0:T(8,128)S(1)}, u32[]{:S(2)}, u32[]{:S(2)}) collective-permute-start(f32[1,8,512]{2,1,0:T(8,128)S(1)} %get-tuple-element.48), channel_id=1, source_target_pairs={{16,0},{32,16},{48,32},{64,48},{80,64},{96,80},{112,96},{128,112},... | collective-permute-start | bytes 49160 | tf_op jit(solution)/shard_map/ppermute | solution.py:20
  46.6 4.6 %collective-permute-start.9 = (f32[1,8,512]{2,1,0:T(8,128)S(1)}, f32[1,8,512]{2,1,0:T(8,128)S(1)}, u32[]{:S(2)}, u32[]{:S(2)}) collective-permute-start(f32[1,8,512]{2,1,0:T(8,128)S(1)} %get-tuple-element.47), channel_id=1, source_target_pairs={{0,16},{16,32},{32,48},{48,64},{64,80},{80,96},{96,112},{112,128},... | collective-permute-start | bytes 49160 | tf_op jit(solution)/shard_map/ppermute | solution.py:19
  51.3 13.5 %collective-permute-start.10 = (f32[10,1,512]{2,1,0:T(1,128)S(1)}, f32[10,1,512]{2,1,0:T(1,128)S(1)}, u32[]{:S(2)}, u32[]{:S(2)}) collective-permute-start(f32[10,1,512]{2,1,0:T(1,128)S(1)} %get-tuple-element.40), channel_id=1, source_target_pairs={{1,0},{2,1},{3,2},{4,3},{5,4},{6,5},{7,6},{8,7},{9,8},{10,9},{11,1... | collective-permute-start | bytes 61448 | tf_op jit(solution)/shard_map/ppermute | solution.py:20
  52.6 12.2 %collective-permute-start.11 = (f32[10,1,512]{2,1,0:T(1,128)S(1)}, f32[10,1,512]{2,1,0:T(1,128)S(1)}, u32[]{:S(2)}, u32[]{:S(2)}) collective-permute-start(f32[10,1,512]{2,1,0:T(1,128)S(1)} %get-tuple-element.39), channel_id=1, source_target_pairs={{0,1},{1,2},{2,3},{3,4},{4,5},{5,6},{6,7},{7,8},{8,9},{9,10},{10,1... | collective-permute-start | bytes 61448 | tf_op jit(solution)/shard_map/ppermute | solution.py:19
  57.2 13.9 %collective-permute-start.16 = (f32[1,4,256]{2,1,0:T(4,128)S(1)}, f32[1,4,256]{2,1,0:T(4,128)S(1)}, u32[]{:S(2)}, u32[]{:S(2)}) collective-permute-start(f32[1,4,256]{2,1,0:T(4,128)S(1)} %get-tuple-element.72), channel_id=1, source_target_pairs={{16,0},{32,16},{48,32},{64,48},{80,64},{96,80},{112,96},{128,112},... | collective-permute-start | bytes 12296 | tf_op jit(solution)/shard_map/ppermute | solution.py:20
  59.1 11.9 %collective-permute-start.17 = (f32[1,4,256]{2,1,0:T(4,128)S(1)}, f32[1,4,256]{2,1,0:T(4,128)S(1)}, u32[]{:S(2)}, u32[]{:S(2)}) collective-permute-start(f32[1,4,256]{2,1,0:T(4,128)S(1)} %get-tuple-element.71), channel_id=1, source_target_pairs={{0,16},{16,32},{32,48},{48,64},{64,80},{80,96},{96,112},{112,128},... | collective-permute-start | bytes 12296 | tf_op jit(solution)/shard_map/ppermute | solution.py:19
  65.4 32.0 %copy-start.1 = (f32[8,8,512]{2,1,0:T(8,128)}, f32[8,8,512]{2,1,0:T(8,128)S(1)}, u32[]{:S(2)}) copy-start(f32[8,8,512]{2,1,0:T(8,128)S(1)} %fusion.93) | copy-start | bytes 393220
  65.5 11.2 %collective-permute-start.12 = (f32[1,8,512]{2,1,0:T(8,128)S(1)}, f32[1,8,512]{2,1,0:T(8,128)S(1)}, u32[]{:S(2)}, u32[]{:S(2)}) collective-permute-start(f32[1,8,512]{2,1,0:T(8,128)S(1)} %get-tuple-element.46), channel_id=1, source_target_pairs={{16,0},{32,16},{48,32},{64,48},{80,64},{96,80},{112,96},{128,112},... | collective-permute-start | bytes 49160 | tf_op jit(solution)/shard_map/ppermute | solution.py:20
  67.4 9.3 %collective-permute-start.13 = (f32[1,8,512]{2,1,0:T(8,128)S(1)}, f32[1,8,512]{2,1,0:T(8,128)S(1)}, u32[]{:S(2)}, u32[]{:S(2)}) collective-permute-start(f32[1,8,512]{2,1,0:T(8,128)S(1)} %get-tuple-element.45), channel_id=1, source_target_pairs={{0,16},{16,32},{32,48},{48,64},{64,80},{80,96},{96,112},{112,128},... | collective-permute-start | bytes 49160 | tf_op jit(solution)/shard_map/ppermute | solution.py:19
  71.1 11.1 %collective-permute-start.18 = (f32[6,1,256]{2,1,0:T(1,128)S(1)}, f32[6,1,256]{2,1,0:T(1,128)S(1)}, u32[]{:S(2)}, u32[]{:S(2)}) collective-permute-start(f32[6,1,256]{2,1,0:T(1,128)S(1)} %get-tuple-element.66), channel_id=1, source_target_pairs={{1,0},{2,1},{3,2},{4,3},{5,4},{6,5},{7,6},{8,7},{9,8},{10,9},{11,1... | collective-permute-start | bytes 18440 | tf_op jit(solution)/shard_map/ppermute | solution.py:20
  72.4 9.8 %collective-permute-start.19 = (f32[6,1,256]{2,1,0:T(1,128)S(1)}, f32[6,1,256]{2,1,0:T(1,128)S(1)}, u32[]{:S(2)}, u32[]{:S(2)}) collective-permute-start(f32[6,1,256]{2,1,0:T(1,128)S(1)} %get-tuple-element.65), channel_id=1, source_target_pairs={{0,1},{1,2},{2,3},{3,4},{4,5},{5,6},{6,7},{7,8},{8,9},{9,10},{10,1... | collective-permute-start | bytes 18440 | tf_op jit(solution)/shard_map/ppermute | solution.py:19
  76.7 5.7 %collective-permute-start.14 = (f32[10,1,512]{2,1,0:T(1,128)S(1)}, f32[10,1,512]{2,1,0:T(1,128)S(1)}, u32[]{:S(2)}, u32[]{:S(2)}) collective-permute-start(f32[10,1,512]{2,1,0:T(1,128)S(1)} %get-tuple-element.38), channel_id=1, source_target_pairs={{1,0},{2,1},{3,2},{4,3},{5,4},{6,5},{7,6},{8,7},{9,8},{10,9},{11,1... | collective-permute-start | bytes 61448 | tf_op jit(solution)/shard_map/ppermute | solution.py:20
  78.0 5.1 %collective-permute-start.15 = (f32[10,1,512]{2,1,0:T(1,128)S(1)}, f32[10,1,512]{2,1,0:T(1,128)S(1)}, u32[]{:S(2)}, u32[]{:S(2)}) collective-permute-start(f32[10,1,512]{2,1,0:T(1,128)S(1)} %get-tuple-element.37), channel_id=1, source_target_pairs={{0,1},{1,2},{2,3},{3,4},{4,5},{5,6},{6,7},{7,8},{8,9},{9,10},{10,1... | collective-permute-start | bytes 61448 | tf_op jit(solution)/shard_map/ppermute | solution.py:19
  97.6 5.6 %collective-permute-start.20 = (f32[1,4,256]{2,1,0:T(4,128)S(1)}, f32[1,4,256]{2,1,0:T(4,128)S(1)}, u32[]{:S(2)}, u32[]{:S(2)}) collective-permute-start(f32[1,4,256]{2,1,0:T(4,128)S(1)} %get-tuple-element.70), channel_id=1, source_target_pairs={{16,0},{32,16},{48,32},{64,48},{80,64},{96,80},{112,96},{128,112},... | collective-permute-start | bytes 12296 | tf_op jit(solution)/shard_map/ppermute | solution.py:20
  99.5 4.4 %collective-permute-start.21 = (f32[1,4,256]{2,1,0:T(4,128)S(1)}, f32[1,4,256]{2,1,0:T(4,128)S(1)}, u32[]{:S(2)}, u32[]{:S(2)}) collective-permute-start(f32[1,4,256]{2,1,0:T(4,128)S(1)} %get-tuple-element.69), channel_id=1, source_target_pairs={{0,16},{16,32},{32,48},{48,64},{64,80},{80,96},{96,112},{112,128},... | collective-permute-start | bytes 12296 | tf_op jit(solution)/shard_map/ppermute | solution.py:19
  103.9 38.4 %collective-permute-start.22 = (f32[6,1,256]{2,1,0:T(1,128)S(1)}, f32[6,1,256]{2,1,0:T(1,128)S(1)}, u32[]{:S(2)}, u32[]{:S(2)}) collective-permute-start(f32[6,1,256]{2,1,0:T(1,128)S(1)} %get-tuple-element.64), channel_id=1, source_target_pairs={{1,0},{2,1},{3,2},{4,3},{5,4},{6,5},{7,6},{8,7},{9,8},{10,9},{11,1... | collective-permute-start | bytes 18440 | tf_op jit(solution)/shard_map/ppermute | solution.py:20
  105.2 37.1 %collective-permute-start.23 = (f32[6,1,256]{2,1,0:T(1,128)S(1)}, f32[6,1,256]{2,1,0:T(1,128)S(1)}, u32[]{:S(2)}, u32[]{:S(2)}) collective-permute-start(f32[6,1,256]{2,1,0:T(1,128)S(1)} %get-tuple-element.63), channel_id=1, source_target_pairs={{0,1},{1,2},{2,3},{3,4},{4,5},{5,6},{6,7},{7,8},{8,9},{9,10},{10,1... | collective-permute-start | bytes 18440 | tf_op jit(solution)/shard_map/ppermute | solution.py:19
  142.6 18.8 %collective-permute-start.24 = (f32[1,4,256]{2,1,0:T(4,128)S(1)}, f32[1,4,256]{2,1,0:T(4,128)S(1)}, u32[]{:S(2)}, u32[]{:S(2)}) collective-permute-start(f32[1,4,256]{2,1,0:T(4,128)S(1)} %get-tuple-element.68), channel_id=1, source_target_pairs={{16,0},{32,16},{48,32},{64,48},{80,64},{96,80},{112,96},{128,112},... | collective-permute-start | bytes 12296 | tf_op jit(solution)/shard_map/ppermute | solution.py:20
  150.9 10.5 %collective-permute-start.25 = (f32[1,4,256]{2,1,0:T(4,128)S(1)}, f32[1,4,256]{2,1,0:T(4,128)S(1)}, u32[]{:S(2)}, u32[]{:S(2)}) collective-permute-start(f32[1,4,256]{2,1,0:T(4,128)S(1)} %get-tuple-element.67), channel_id=1, source_target_pairs={{0,16},{16,32},{32,48},{48,64},{64,80},{80,96},{96,112},{112,128},... | collective-permute-start | bytes 12296 | tf_op jit(solution)/shard_map/ppermute | solution.py:19
  155.8 10.9 %collective-permute-start.28 = (f32[1,32,128]{2,0,1:T(1,128)S(1)}, f32[1,32,128]{2,0,1:T(1,128)S(1)}, u32[]{:S(2)}, u32[]{:S(2)}) collective-permute-start(f32[1,32,128]{2,0,1:T(1,128)S(1)} %get-tuple-element.60), channel_id=1, source_target_pairs={{16,0},{32,16},{48,32},{64,48},{80,64},{96,80},{112,96},{128,112},... | collective-permute-start | bytes 49160 | tf_op jit(solution)/shard_map/ppermute | solution.py:20
  157.7 9.0 %collective-permute-start.29 = (f32[1,32,128]{2,0,1:T(1,128)S(1)}, f32[1,32,128]{2,0,1:T(1,128)S(1)}, u32[]{:S(2)}, u32[]{:S(2)}) collective-permute-start(f32[1,32,128]{2,0,1:T(1,128)S(1)} %get-tuple-element.59), channel_id=1, source_target_pairs={{0,16},{16,32},{32,48},{48,64},{64,80},{80,96},{96,112},{112,128},... | collective-permute-start | bytes 49160 | tf_op jit(solution)/shard_map/ppermute | solution.py:19
  161.4 5.6 %collective-permute-start.26 = (f32[6,1,256]{2,1,0:T(1,128)S(1)}, f32[6,1,256]{2,1,0:T(1,128)S(1)}, u32[]{:S(2)}, u32[]{:S(2)}) collective-permute-start(f32[6,1,256]{2,1,0:T(1,128)S(1)} %get-tuple-element.62), channel_id=1, source_target_pairs={{1,0},{2,1},{3,2},{4,3},{5,4},{6,5},{7,6},{8,7},{9,8},{10,9},{11,1... | collective-permute-start | bytes 18440 | tf_op jit(solution)/shard_map/ppermute | solution.py:20
  162.7 4.8 %collective-permute-start.27 = (f32[6,1,256]{2,1,0:T(1,128)S(1)}, f32[6,1,256]{2,1,0:T(1,128)S(1)}, u32[]{:S(2)}, u32[]{:S(2)}) collective-permute-start(f32[6,1,256]{2,1,0:T(1,128)S(1)} %get-tuple-element.61), channel_id=1, source_target_pairs={{0,1},{1,2},{2,3},{3,4},{4,5},{5,6},{6,7},{7,8},{8,9},{9,10},{10,1... | collective-permute-start | bytes 18440 | tf_op jit(solution)/shard_map/ppermute | solution.py:19
  191.6 12.4 %collective-permute-start.30 = (f32[1,32,128]{2,0,1:T(1,128)S(1)}, f32[1,32,128]{2,0,1:T(1,128)S(1)}, u32[]{:S(2)}, u32[]{:S(2)}) collective-permute-start(f32[1,32,128]{2,0,1:T(1,128)S(1)} %get-tuple-element.58), channel_id=1, source_target_pairs={{16,0},{32,16},{48,32},{64,48},{80,64},{96,80},{112,96},{128,112},... | collective-permute-start | bytes 49160 | tf_op jit(solution)/shard_map/ppermute | solution.py:20
  200.7 4.0 %collective-permute-start.31 = (f32[1,32,128]{2,0,1:T(1,128)S(1)}, f32[1,32,128]{2,0,1:T(1,128)S(1)}, u32[]{:S(2)}, u32[]{:S(2)}) collective-permute-start(f32[1,32,128]{2,0,1:T(1,128)S(1)} %get-tuple-element.57), channel_id=1, source_target_pairs={{0,16},{16,32},{32,48},{48,64},{64,80},{80,96},{96,112},{112,128},... | collective-permute-start | bytes 49160 | tf_op jit(solution)/shard_map/ppermute | solution.py:19
  205.5 7.4 %collective-permute-start.32 = (f32[1,32,128]{2,0,1:T(1,128)S(1)}, f32[1,32,128]{2,0,1:T(1,128)S(1)}, u32[]{:S(2)}, u32[]{:S(2)}) collective-permute-start(f32[1,32,128]{2,0,1:T(1,128)S(1)} %get-tuple-element.54), channel_id=1, source_target_pairs={{16,0},{32,16},{48,32},{64,48},{80,64},{96,80},{112,96},{128,112},... | collective-permute-start | bytes 49160 | tf_op jit(solution)/shard_map/ppermute | solution.py:20
  207.4 5.5 %collective-permute-start.33 = (f32[1,32,128]{2,0,1:T(1,128)S(1)}, f32[1,32,128]{2,0,1:T(1,128)S(1)}, u32[]{:S(2)}, u32[]{:S(2)}) collective-permute-start(f32[1,32,128]{2,0,1:T(1,128)S(1)} %get-tuple-element.53), channel_id=1, source_target_pairs={{0,16},{16,32},{32,48},{48,64},{64,80},{80,96},{96,112},{112,128},... | collective-permute-start | bytes 49160 | tf_op jit(solution)/shard_map/ppermute | solution.py:19
  280.7 0.7 copy-start.3
where the time goes:
time: 288 us; the launch traced here: 286 us
  starting transfers between devices  116 us (40%)
  blocking collectives  97.6 us (34%)
  local copies, waits for them, and re-layouts  27.4 us (10%)
  other arithmetic  24.9 us (9%)
  between operations  16.2 us (6%)
  waiting for transfers between devices  3.99 us (1%)
    ppermute x17, starting transfers between devices, extended(): before = lax.ppermute(last, axis, up)  68.8 us
    ppermute x17, starting transfers between devices, extended(): after = lax.ppermute(leading, axis, down)  47.1 us
    all_gather x1, blocking collectives, shards(): collected = lax.all_gather(stacked, 'gx', axis=1, tiled=True)  44 us
    all_gather x1, blocking collectives, shards(): lax.all_gather(coef_low, 'gy', axis=1, tiled=True)  31.3 us
    all_gather x1, blocking collectives, shards(): lax.all_gather(source_low, 'gy', axis=1, tiled=True)  22.3 us
    reshape x3, local copies, waits for them, and re-layouts, restrict(): blocks = values.reshape(size_x // 2, 2, size_y // 2, 2, size_z // 2, 2)  21.2 us
    reduce_sum x8, other arithmetic, restrict(): return scale * jnp.mean(blocks, axis=(1, 3, 5))  9.64 us
    reduce_sum x6, other arithmetic, bottom_solve(): step_size = norm_now / jnp.sum(direction * image)  5.89 us
  transfers between devices with their start and end apart: 34, of which 6 were waited for; matrix products, arithmetic and copies ran while one was open for 7% of the time, Pallas kernels for 0%

commit v1 on v0

v1 whole, which is shorter than its diff:
```python
import jax
import jax.numpy as jnp
from jax import lax
from jax.experimental import pallas as pl
from jax.experimental.pallas import tpu as pltpu
from jax.sharding import PartitionSpec as P

BOTTOM = 6
RELAX_WEIGHT = 0.8
TINY = 1e-30
F32 = jnp.float32
VMEM = pl.BlockSpec(memory_space=pltpu.VMEM)
SMEM = pl.BlockSpec(memory_space=pltpu.SMEM)
PARAMS = pltpu.CompilerParams(vmem_limit_bytes=24 * 1024 * 1024)


def call(kernel, out_shapes, scratch=(), specs=None, n_in=0):
    return pl.pallas_call(
        kernel,
        out_shape=[jax.ShapeDtypeStruct(s, F32) for s in out_shapes],
        in_specs=specs if specs is not None else [VMEM] * n_in,
        out_specs=[VMEM] * len(out_shapes),
        scratch_shapes=[pltpu.VMEM(s, F32) for s in scratch],
        compiler_params=PARAMS,
    )


def harmonic(a, b):
    return 2.0 * a * b / jnp.maximum(a + b, TINY)


def along(v, axis, step):
    n = v.shape[axis]
    return pltpu.roll(v, (-step) % n, axis)


def positions(shape, axis):
    return lax.broadcasted_iota(jnp.int32, shape, axis)


def halving(rows, cols):
    return (positions((rows, cols), 0) // 2 == positions((rows, cols), 1)).astype(F32)


def doubling(rows, cols, factor):
    return (positions((rows, cols), 1) // factor == positions((rows, cols), 0)).astype(F32)


def matmul(a, b):
    return jnp.dot(a, b, precision=lax.Precision.HIGHEST, preferred_element_type=F32)


def weight(face, centre):
    return jnp.where(face > 0.0, face, centre)


def diagonal_of(c, xp, xm, hy, hz):
    return (weight(xp, c) + weight(xm, c) + weight(hy, c) + weight(along(hy, 0, -1), c)
            + weight(hz, c) + weight(along(hz, 1, -1), c))


def operate(d, v, xp, vp, xm, vm, hy, hz):
    out = d * v - xp * vp - xm * vm
    out = out - hy * along(v, 0, 1) - along(hy * v, 0, -1)
    return out - hz * along(v, 1, 1) - along(hz * v, 1, -1)


def z_face(c):
    nxt = jnp.where(positions(c.shape, 1) < c.shape[1] - 1, along(c, 1, 1), 0.0)
    return harmonic(c, nxt)


NP, NR, NC = 7, 6, 7
NROWS = NP + NR + NC


def pack_y(phi, rhs, coef, up, dn, stage):
    k = 0
    for a, (ref, n) in enumerate(((phi, NP), (rhs, NR), (coef, NC))):
        for q in range(4):
            lanes = slice(128 * q, 128 * q + 128)
            base = 64 * (4 * a + q)
            stage[base:base + 64, :] = ref[:, lanes]
            for j in range(n):
                rows = slice(8 * (k + j), 8 * (k + j) + 8)
                up[rows, lanes] = stage[pl.ds(base + 8 - n + j, 8, stride=8), :]
                dn[rows, lanes] = stage[pl.ds(base + j, 8, stride=8), :]
        k += n


def pack_x(phi, rhs, coef, lo, hi, pe, re, ce, up, dn, stage):
    zero = jnp.zeros((8, 128), F32)
    k = 0
    for a, (ref, ext, n) in enumerate(((phi, pe, NP), (rhs, re, NR), (coef, ce, NC))):
        for x in range(8):
            ext[24 * x:24 * x + 8, :] = ref[8 * x:8 * x + 8, :]
        for q in range(4):
            lanes = slice(128 * q, 128 * q + 128)
            base = 128 * (4 * a + q)
            for j in range(n):
                rows = slice(8 * (k + j), 8 * (k + j) + 8)
                stage[pl.ds(base + j, 8, stride=16), :] = hi[rows, lanes]
                stage[pl.ds(base + 16 - n + j, 8, stride=16), :] = lo[rows, lanes]
            for j in range(n, 16 - n):
                stage[pl.ds(base + j, 8, stride=16), :] = zero
            for x in range(8):
                ext[24 * x + 8:24 * x + 24, lanes] = stage[base + 16 * x:base + 16 * x + 16, :]
        k += n
    up[0:72, :] = pe[120:192, :]
    up[72:120, :] = re[144:192, :]
    up[120:192, :] = ce[120:192, :]
    dn[0:72, :] = pe[0:72, :]
    dn[72:120, :] = re[0:48, :]
    dn[120:192, :] = ce[0:72, :]


def fine(pe, re, ce, lo, hi, phi_out, smid, cmid, mup, mdn,
         p0, rs, c, hx, hy, hz, dg, rd, p1, p2, sums, packed):
    p0[0:3] = lo[0:3]
    p0[3:11] = pe[...]
    p0[11:14] = hi[0:3]
    rs[1:3] = lo[3:5]
    rs[3:11] = re[...]
    rs[11:13] = hi[3:5]
    c[0:3] = lo[5:8]
    c[3:11] = ce[...]
    c[11:14] = hi[5:8]
    hx[0] = harmonic(c[0], c[1])

    def first(i, carry):
        ci = c[i]
        xp, xm = harmonic(ci, c[i + 1]), hx[i - 1]
        hyi = harmonic(ci, along(ci, 0, 1))
        hzi = z_face(ci)
        d = diagonal_of(ci, xp, xm, hyi, hzi)
        r = RELAX_WEIGHT / jnp.maximum(d, TINY)
        hx[i], hy[i], hz[i], dg[i], rd[i] = xp, hyi, hzi, d, r
        v = p0[i]
        p1[i] = v + (rs[i] - operate(d, v, xp, p0[i + 1], xm, p0[i - 1], hyi, hzi)) * r
        return carry

    lax.fori_loop(1, 13, first, 0)

    def second(i, carry):
        v = p1[i]
        image = operate(dg[i], v, hx[i], p1[i + 1], hx[i - 1], p1[i - 1], hy[i], hz[i])
        p2[i] = v + (rs[i] - image) * rd[i]
        return carry

    lax.fori_loop(2, 12, second, 0)
    for x in range(8):
        phi_out[x] = p2[3 + x, 0:8, :]

    def residual(i):
        return rs[i] - operate(dg[i], p2[i], hx[i], p2[i + 1], hx[i - 1], p2[i - 1], hy[i], hz[i])

    def pairs(k, carry):
        i = 3 + 2 * k
        s = residual(i) + residual(i + 1)
        t = c[i] + c[i + 1]
        s = (s + along(s, 0, 1)) * 0.5
        t = (t + along(t, 0, 1)) * 0.125
        for q in range(4):
            sums[q, k] = s[:, 128 * q:128 * q + 128]
            sums[q, 4 + k] = t[:, 128 * q:128 * q + 128]
        return carry

    lax.fori_loop(0, 4, pairs, 0)
    for k in range(8):
        for q in range(4):
            lanes = slice(128 * q, 128 * q + 128)
            packed[16 * k:16 * k + 8, lanes] = sums[q, k, pl.ds(0, 8, stride=2), :]
            packed[16 * k + 8:16 * k + 12, lanes] = jnp.zeros((4, 128), F32)
            packed[16 * k + 12:16 * k + 16, lanes] = sums[q, k, pl.ds(16, 4, stride=2), :]
    mid = matmul(packed[...], halving(512, 256)).reshape(8, 16, 256)
    smid[...] = mid[0:4]
    cmid[...] = mid[4:8]
    mup[0:2] = mid[2:4]
    mup[2:6] = mid[4:8]
    mdn[0:2] = mid[0:2]
    mdn[2:6] = mid[4:8]


def middle(smid, cmid, lo, hi, emid, out, sums):
    s = [lo[0], lo[1]] + [smid[x] for x in range(4)] + [hi[0], hi[1]]
    c = [lo[2 + x] for x in range(4)] + [cmid[x] for x in range(4)] + [hi[2 + x] for x in range(4)]
    hx = [harmonic(c[j], c[j + 1]) for j in range(1, 10)]
    hy, hz, d, r, e1 = [], [], [], [], []
    for i in range(8):
        ci = c[i + 2]
        hy.append(harmonic(ci, along(ci, 0, 1)))
        hz.append(z_face(ci))
        d.append(diagonal_of(ci, hx[i + 1], hx[i], hy[i], hz[i]))
        r.append(RELAX_WEIGHT / jnp.maximum(d[i], TINY))
        e1.append(s[i] * r[i])

    def image(i, e):
        return operate(d[i], e[i], hx[i + 1], e[i + 1], hx[i], e[i - 1], hy[i], hz[i])

    e2 = [None] + [e1[i] + (s[i] - image(i, e1)) * r[i] for i in range(1, 7)] + [None]
    res = [s[i] - image(i, e2) for i in range(2, 6)]
    for x in range(4):
        emid[x] = e2[2 + x][0:4, :]
    groups = [(res[2 * x] + res[2 * x + 1]) * 0.5 for x in range(2)]
    groups += [(c[2 * x] + c[2 * x + 1]) * 0.125 for x in range(6)]
    for g in range(8):
        both = (groups[g] + along(groups[g], 0, 1))[0:8, :]
        sums[8 * g:8 * g + 8, :] = both[:, 0:128]
        sums[64 + 8 * g:72 + 8 * g, :] = both[:, 128:256]

    def rows(y):
        return jnp.concatenate([sums[pl.ds(64 * q + 2 * y, 8, stride=8), :] for q in range(2)], axis=1)

    low0 = matmul(rows(0), halving(256, 128))
    low1 = matmul(rows(1), halving(256, 128))
    for n in range(16):
        out[n, 0:8, :] = low0
        out[n, 8:16, :] = low1


def y_face(c):
    n = c.shape[0]
    return harmonic(c, jnp.where(positions(c.shape, 0) < n - 1, along(c, 0, 1), 0.0))


def columns(gathered, sd, ccol):
    for g in range(8):
        for y in range(2):
            rows = gathered[pl.ds(8 * y + g, 16, stride=16), :]
            if g < 2:
                sd[pl.ds(32 * g + y, 16, stride=2), :] = rows
            else:
                ccol[pl.ds(32 * (g - 2) + y, 16, stride=2), :] = rows
    c = [ccol[32 * j:32 * j + 32, :] for j in range(6)]
    hx = [harmonic(c[j], c[j + 1]) for j in range(1, 4)]
    for x in range(2):
        ci = c[2 + x]
        sd[64 + 32 * x:96 + 32 * x, :] = diagonal_of(ci, hx[x + 1], hx[x], y_face(ci), z_face(ci))


def low(sd, ccol, lo, hi, elow, out, sums):
    def part(ref, k):
        return ref[32 * k:32 * k + 32, :]

    s = [part(ref, k) for ref in (lo, sd, hi) for k in (0, 1)]
    d = [part(ref, k) for ref in (lo, sd, hi) for k in (2, 3)]
    c = [part(ccol, k) for k in range(6)]
    hx = [harmonic(c[j], c[j + 1]) for j in range(5)]
    hy = [y_face(ci) for ci in c]
    hz = [z_face(ci) for ci in c]
    r = [RELAX_WEIGHT / jnp.maximum(di, TINY) for di in d]
    e1 = [s[i] * r[i] for i in range(6)]

    def image(i, e):
        return operate(d[i], e[i], hx[i], e[i + 1], hx[i - 1], e[i - 1], hy[i], hz[i])

    e2 = [None] + [e1[i] + (s[i] - image(i, e1)) * r[i] for i in range(1, 5)] + [None]
    res = [s[i] - image(i, e2) for i in range(2, 4)]
    for x in range(2):
        elow[32 * x:32 * x + 32, :] = e2[2 + x]
    a = (res[0] + res[1]) * 0.5
    b = (c[2] + c[3]) * 0.125
    sums[0:32, :] = a + along(a, 0, 1)
    sums[32:64, :] = b + along(b, 0, 1)
    ra = sums[pl.ds(0, 16, stride=2), :]
    rb = sums[pl.ds(32, 16, stride=2), :]
    both = matmul(jnp.concatenate([ra, rb], axis=1), halving(256, 128))
    for n in range(32):
        out[n] = both


def bottom(place, gathered, elow, emid, out, hx, hy, hz, dg, sol, res, dire, img):
    half = positions((16, 128), 1) < 64
    last_z = positions((16, 128), 1) % 64 == 63
    last_y = positions((16, 128), 0) == 15
    c = []
    for x in range(16):
        a, b = gathered[x], gathered[x + 16]
        source = jnp.where(half, a, along(b, 1, 64))
        c.append(jnp.where(half, along(a, 1, 64), b))
        res[x] = source
        dire[x] = source
        sol[x] = jnp.zeros((16, 128), F32)
    for x in range(16):
        nxt = c[x + 1] if x < 15 else jnp.where(half, along(c[0], 1, 64), 0.0)
        hx[x + 1] = harmonic(c[x], nxt)
    hx[0] = along(hx[16], 1, 64)
    for x in range(16):
        hy[x] = harmonic(c[x], jnp.where(last_y, 0.0, along(c[x], 0, 1)))
        hz[x] = harmonic(c[x], jnp.where(last_z, 0.0, along(c[x], 1, 1)))
        dg[x] = diagonal_of(c[x], hx[x + 1], hx[x], hy[x], hz[x])

    def total(acc):
        return jnp.sum(acc, axis=(0, 1), keepdims=True)

    def dot_image():
        acc = jnp.zeros((16, 128), F32)
        for x in range(16):
            v = dire[x]
            vp = dire[x + 1] if x < 15 else along(dire[0], 1, 64)
            vm = dire[x - 1] if x > 0 else along(dire[15], 1, 64)
            image = operate(dg[x], v, hx[x + 1], vp, hx[x], vm, hy[x], hz[x])
            img[x] = image
            acc = acc + v * image
        return total(acc)

    def norm():
        acc = jnp.zeros((16, 128), F32)
        for x in range(16):
            acc = acc + res[x] * res[x]
        return total(acc)

    def step(_, rr):
        alpha = rr / dot_image()
        acc = jnp.zeros((16, 128), F32)
        for x in range(16):
            sol[x] = sol[x] + alpha * dire[x]
            rx = res[x] - alpha * img[x]
            res[x] = rx
            acc = acc + rx * rx
        new = total(acc)
        beta = new / rr
        for x in range(16):
            dire[x] = res[x] + beta * dire[x]
        return new

    rr = lax.fori_loop(0, BOTTOM - 1, step, norm())
    gx, gy = place[0], place[1]
    xi = lax.rem(gx, 16)
    alpha = rr / dot_image()
    mine = sol[xi] + alpha * dire[xi]
    mine = jnp.where(gx >= 16, along(mine, 1, 64), mine)
    row = positions((16, 128), 0)
    mine = jnp.sum(jnp.where(row == gy, mine, 0.0), axis=0, keepdims=True)
    row = positions((32, 128), 0)
    lows = []
    for x in range(2):
        e = elow[32 * x:32 * x + 32, :]
        for y in range(2):
            lows.append(jnp.sum(jnp.where(row == 2 * gy + y, e, 0.0), axis=0, keepdims=True))
    coarse = matmul(jnp.broadcast_to(mine, (8, 128)), doubling(128, 256, 4))
    finer = matmul(jnp.concatenate(lows + lows, axis=0), doubling(128, 256, 2))
    for x in range(4):
        k = 2 * (x // 2)
        for y in range(4):
            add = finer[k + y // 2:k + y // 2 + 1, :] + coarse[0:1, :]
            out[x, y:y + 1, :] = emid[x, y:y + 1, :] + add


def neighbours(up, dn, axis):
    n = lax.axis_size(axis)
    forth = [(i, i + 1) for i in range(n - 1)]
    back = [(i + 1, i) for i in range(n - 1)]
    return lax.ppermute(up, axis, forth), lax.ppermute(dn, axis, back)


def shards(phi_start, right_side, coefficient):
    own = [a.reshape(64, 512) for a in (phi_start, right_side, coefficient)]
    up, dn = call(pack_y, [(8 * NROWS, 512)] * 2, [(768, 128)], n_in=3)(*own)
    lo, hi = neighbours(up, dn, "gy")
    *ext, up, dn = call(pack_x, [(192, 512)] * 5, [(1536, 128)], n_in=5)(*own, lo, hi)
    lo, hi = neighbours(up, dn, "gx")
    box = (14, 24, 512)
    phi_fine, smid, cmid, up, dn = call(
        fine,
        [(8, 8, 512), (4, 16, 256), (4, 16, 256), (6, 16, 256), (6, 16, 256)],
        [box] * 10 + [(4, 8, 24, 128), (128, 512)],
        n_in=5,
    )(*[a.reshape(8, 24, 512) for a in (*ext, lo, hi)])
    lo, hi = neighbours(up, dn, "gx")
    emid, spread = call(middle, [(4, 4, 256), (16, 16, 128)], [(128, 128)], n_in=4)(smid, cmid, lo, hi)
    gathered = lax.all_to_all(spread, "gy", 0, 0, tiled=True)
    sd, ccol = call(columns, [(128, 128), (192, 128)], n_in=1)(gathered.reshape(256, 128))
    lo, hi = neighbours(sd, sd, "gx")
    elow, spread = call(low, [(64, 128), (32, 16, 128)], [(64, 128)], n_in=4)(sd, ccol, lo, hi)
    gathered = lax.all_to_all(spread, "gx", 0, 0, tiled=True)
    place = jnp.stack([lax.axis_index("gx"), lax.axis_index("gy")]).astype(jnp.int32)
    (correction,) = call(
        bottom,
        [(4, 4, 256)],
        [(17, 16, 128)] + [(16, 16, 128)] * 7,
        specs=[SMEM, VMEM, VMEM, VMEM],
    )(place, gathered, elow, emid)
    return phi_fine, correction


def solution(mesh):
    return jax.shard_map(
        shards,
        mesh=mesh,
        in_specs=(P("gx", "gy", None),) * 3,
        out_specs=(P("gx", "gy", None),) * 2,
        check_vma=False,
    )
```

time: 288 us -> 109 us (0.38)
  starting transfers between devices: 116 us -> 36.1 us
  blocking collectives: 97.6 us -> 27.7 us
  waiting for transfers between devices: 3.99 us -> 29.8 us
  other arithmetic: 24.9 us -> 0.08 us
  local copies, waits for them, and re-layouts: 27.4 us -> 2.7 us
  between operations: 16.2 us -> 0.76 us
  Pallas kernels: 0 us -> 11 us
    all_gather x3 -> x0, blocking collectives: 97.6 us -> none  [the longest x1 44 us: shards(): collected = lax.all_gather(stacked, 'gx', axis=1, tiled=True)]
    ppermute x34 -> x8, starting transfers between devices: 116 us -> 23.6 us  [neighbours(): return (lax.ppermute(up, axis, forth), lax.ppermute(dn, axis, back))]
    all_to_all x0 -> x1, blocking collectives: none -> 27.7 us  [shards(): gathered = lax.all_to_all(spread, 'gy', 0, 0, tiled=True)]
    reshape x5 -> x0, local copies, waits for them, and re-layouts: 21.6 us -> none  [the longest x3 21.2 us: restrict(): blocks = values.reshape(size_x // 2, 2, size_y // 2, 2, size_z // 2, 2)]
    reduce_sum x19 -> x0, other arithmetic: 19 us -> none  [the longest x8 9.64 us: restrict(): return scale * jnp.mean(blocks, axis=(1, 3, 5))]
    ppermute x34 -> x8, waiting for transfers between devices: 3.99 us -> 21 us  [neighbours(): return (lax.ppermute(up, axis, forth), lax.ppermute(dn, axis, back))]
    all_to_all x0 -> x1, starting transfers between devices: none -> 12.5 us  [shards(): gathered = lax.all_to_all(spread, 'gx', 0, 0, tiled=True)]
    pallas_call x0 -> x7, Pallas kernels: none -> 11 us  [the longest x1 4.54 us: shards(): call(fine, [(8, 8, 512), (4, 16, 256), (4, 16, 256), (6, 16, 256), (6, 16...]
  transfers between devices with their start and end apart: 34 -> 9, of which waited for: 6 -> 7; matrix products, arithmetic and copies ran while one was open for 7% -> 0% of each run, Pallas kernels for 0% -> 0%
where the time goes in v1:
time: 109 us; the launch traced here: 108 us
  starting transfers between devices  36.1 us (33%)
  waiting for transfers between devices  29.8 us (27%)
  blocking collectives  27.7 us (25%)
  Pallas kernels  11 us (10%)
  local copies, waits for them, and re-layouts  2.7 us (2%)
    all_to_all x1, blocking collectives, shards(): gathered = lax.all_to_all(spread, 'gy', 0, 0, tiled=True)  27.7 us
    ppermute x8, starting transfers between devices, neighbours(): return (lax.ppermute(up, axis, forth), lax.ppermute(dn, axis, back))  23.6 us
    ppermute x8, waiting for transfers between devices, neighbours(): return (lax.ppermute(up, axis, forth), lax.ppermute(dn, axis, back))  21 us
    all_to_all x1, starting transfers between devices, shards(): gathered = lax.all_to_all(spread, 'gx', 0, 0, tiled=True)  12.5 us
    all_to_all x1, waiting for transfers between devices, shards(): gathered = lax.all_to_all(spread, 'gx', 0, 0, tiled=True)  8.82 us
    pallas_call x1, Pallas kernels, shards(): call(fine, [(8, 8, 512), (4, 16, 256), (4, 16, 256), (6, 16, 256), (6, 16...  4.54 us
    pallas_call x1, Pallas kernels, shards(): call(bottom, [(4, 4, 256)], [(17, 16, 128)] + [(16, 16, 128)] * 7, specs=...  4.08 us
    unnamed x6, local copies, waits for them, and re-layouts  2.7 us
  transfers between devices with their start and end apart: 9, of which 7 were waited for; matrix products, arithmetic and copies ran while one was open for 0% of the time, Pallas kernels for 0%

profile of v1, /device:TPU:1, one launch (start us, length us, event | category | flops | bytes accessed | tf_op | source)
XLA Modules:
  0.0 108.2 jit_solution(5286208809733185523)
XLA Ops:
  0.6 0.0 copy-start
  0.6 0.9 copy-done
  1.5 0.0 copy-start.1
  1.5 0.9 copy-done.1
  2.4 0.0 copy-start.2
  2.4 0.9 copy-done.2
  3.3 0.1 shard_map.50
  3.5 4.4 %collective-permute-start = (f32[160,512]{1,0:T(8,128)S(1)}, f32[160,512]{1,0:T(8,128)S(1)}, u32[]{:S(2)}, u32[]{:S(2)}) collective-permute-start(f32[160,512]{1,0:T(8,128)S(1)} %get-tuple-element.20), channel_id=1, source_target_pairs={{0,1},{1,2},{2,3},{3,4},{4,5},{5,6},{6,7},{7,8},{8,9},{9,10},{10,1... | collective-permute-start | bytes 983048 | tf_op jit(solution)/shard_map/ppermute | solution.py:354
  7.9 1.3 %collective-permute-start.1 = (f32[160,512]{1,0:T(8,128)S(1)}, f32[160,512]{1,0:T(8,128)S(1)}, u32[]{:S(2)}, u32[]{:S(2)}) collective-permute-start(f32[160,512]{1,0:T(8,128)S(1)} %get-tuple-element.21), channel_id=1, source_target_pairs={{1,0},{2,1},{3,2},{4,3},{5,4},{6,5},{7,6},{8,7},{9,8},{10,9},{11,1... | collective-permute-start | bytes 983048 | tf_op jit(solution)/shard_map/ppermute | solution.py:354
  9.2 2.7 %collective-permute-done.lo = f32[160,512]{1,0:T(8,128)S(1)} collective-permute-done((f32[160,512]{1,0:T(8,128)S(1)}, f32[160,512]{1,0:T(8,128)S(1)}, u32[]{:S(2)}, u32[]{:S(2)}) %collective-permute-start) | collective-permute-done | bytes 327712 | tf_op jit(solution)/shard_map/ppermute | solution.py:354
  11.8 4.0 %collective-permute-done.1.hi = f32[160,512]{1,0:T(8,128)S(1)} collective-permute-done((f32[160,512]{1,0:T(8,128)S(1)}, f32[160,512]{1,0:T(8,128)S(1)}, u32[]{:S(2)}, u32[]{:S(2)}) %collective-permute-start.1) | collective-permute-done | bytes 327712 | tf_op jit(solution)/shard_map/ppermute | solution.py:354
  15.8 0.4 shard_map.51
  16.2 7.2 %collective-permute-start.2 = (f32[192,512]{1,0:T(8,128)S(1)}, f32[192,512]{1,0:T(8,128)S(1)}, u32[]{:S(2)}, u32[]{:S(2)}) collective-permute-start(f32[192,512]{1,0:T(8,128)S(1)} %get-tuple-element.25), channel_id=1, source_target_pairs={{0,16},{16,32},{32,48},{48,64},{64,80},{80,96},{96,112},{112,128},... | collective-permute-start | bytes 1179656 | tf_op jit(solution)/shard_map/ppermute | solution.py:354
  23.5 1.9 %collective-permute-start.3 = (f32[192,512]{1,0:T(8,128)S(1)}, f32[192,512]{1,0:T(8,128)S(1)}, u32[]{:S(2)}, u32[]{:S(2)}) collective-permute-start(f32[192,512]{1,0:T(8,128)S(1)} %get-tuple-element.26), channel_id=1, source_target_pairs={{16,0},{32,16},{48,32},{64,48},{80,64},{96,80},{112,96},{128,112},... | collective-permute-start | bytes 1179656 | tf_op jit(solution)/shard_map/ppermute | solution.py:354
  25.4 2.8 %collective-permute-done.2 = f32[192,512]{1,0:T(8,128)S(1)} collective-permute-done((f32[192,512]{1,0:T(8,128)S(1)}, f32[192,512]{1,0:T(8,128)S(1)}, u32[]{:S(2)}, u32[]{:S(2)}) %collective-permute-start.2) | collective-permute-done | bytes 393248 | tf_op jit(solution)/shard_map/ppermute | solution.py:354
  28.2 4.4 %collective-permute-done.3 = f32[192,512]{1,0:T(8,128)S(1)} collective-permute-done((f32[192,512]{1,0:T(8,128)S(1)}, f32[192,512]{1,0:T(8,128)S(1)}, u32[]{:S(2)}, u32[]{:S(2)}) %collective-permute-start.3) | collective-permute-done | bytes 393248 | tf_op jit(solution)/shard_map/ppermute | solution.py:354
  32.6 4.5 %shard_map.52 = (f32[8,8,512]{2,1,0:T(8,128)}, f32[4,16,256]{2,1,0:T(8,128)S(1)}, f32[4,16,256]{2,1,0:T(8,128)S(1)}, f32[6,16,256]{2,1,0:T(8,128)S(1)}, f32[6,16,256]{2,1,0:T(8,128)S(1)}) custom-call(f32[8,24,512]{2,1,0:T(8,128)S(1)} %bitcast.18, f32[8,24,512]{2,1,0:T(8,128)S(1)} %bitcast.19, f32[8,24,512]{2,1,0:T(8,128)S(1)} %bitcast.20, ...), custom_call_target="tpu_custom_call" | custom-call | tf_op jit(solution)/shard_map/pallas_call | solution.py:364
  37.1 1.9 %collective-permute-start.4 = (f32[6,16,256]{2,1,0:T(8,128)S(1)}, f32[6,16,256]{2,1,0:T(8,128)S(1)}, u32[]{:S(2)}, u32[]{:S(2)}) collective-permute-start(f32[6,16,256]{2,1,0:T(8,128)S(1)} %get-tuple-element.30), channel_id=1, source_target_pairs={{0,16},{16,32},{32,48},{48,64},{64,80},{80,96},{96,112},{112,128},... | collective-permute-start | bytes 294920 | tf_op jit(solution)/shard_map/ppermute | solution.py:354
  39.0 2.4 %collective-permute-start.5 = (f32[6,16,256]{2,1,0:T(8,128)S(1)}, f32[6,16,256]{2,1,0:T(8,128)S(1)}, u32[]{:S(2)}, u32[]{:S(2)}) collective-permute-start(f32[6,16,256]{2,1,0:T(8,128)S(1)} %get-tuple-element.31), channel_id=1, source_target_pairs={{16,0},{32,16},{48,32},{64,48},{80,64},{96,80},{112,96},{128,112},... | collective-permute-start | bytes 294920 | tf_op jit(solution)/shard_map/ppermute | solution.py:354
  41.4 0.0 collective-permute-done.4.lo
  41.4 3.5 %collective-permute-done.5.hi = f32[6,16,256]{2,1,0:T(8,128)S(1)} collective-permute-done((f32[6,16,256]{2,1,0:T(8,128)S(1)}, f32[6,16,256]{2,1,0:T(8,128)S(1)}, u32[]{:S(2)}, u32[]{:S(2)}) %collective-permute-start.5) | collective-permute-done | bytes 98336 | tf_op jit(solution)/shard_map/ppermute | solution.py:354
  44.9 0.6 shard_map.53
  45.6 27.7 %all_to_all.10 = f32[16,16,128]{2,1,0:T(8,128)S(1)} all-to-all(f32[16,16,128]{2,1,0:T(8,128)S(1)} %get-tuple-element.32), channel_id=1, replica_groups=mesh['gx'=32,'gy'=16] {'gy'}, dimensions={0} | all-to-all | bytes 262144 | tf_op jit(solution)/shard_map/all_to_all | solution.py:372
  73.3 0.2 shard_map.54
  73.4 2.6 %collective-permute-start.6 = (f32[128,128]{1,0:T(8,128)S(1)}, f32[128,128]{1,0:T(8,128)S(1)}, u32[]{:S(2)}, u32[]{:S(2)}) collective-permute-start(f32[128,128]{1,0:T(8,128)S(1)} %get-tuple-element.33.sd), channel_id=1, source_target_pairs={{0,16},{16,32},{32,48},{48,64},{64,80},{80,96},{96,112},{112,128},... | collective-permute-start | bytes 196616 | tf_op jit(solution)/shard_map/ppermute | solution.py:354
  76.0 1.9 %collective-permute-start.7 = (f32[128,128]{1,0:T(8,128)S(1)}, f32[128,128]{1,0:T(8,128)S(1)}, u32[]{:S(2)}, u32[]{:S(2)}) collective-permute-start(f32[128,128]{1,0:T(8,128)S(1)} %get-tuple-element.33.sd), channel_id=1, source_target_pairs={{16,0},{32,16},{48,32},{64,48},{80,64},{96,80},{112,96},{128,112},... | collective-permute-start | bytes 196616 | tf_op jit(solution)/shard_map/ppermute | solution.py:354
  78.0 0.0 collective-permute-done.6.lo
  78.0 3.6 %collective-permute-done.7.hi = f32[128,128]{1,0:T(8,128)S(1)} collective-permute-done((f32[128,128]{1,0:T(8,128)S(1)}, f32[128,128]{1,0:T(8,128)S(1)}, u32[]{:S(2)}, u32[]{:S(2)}) %collective-permute-start.7) | collective-permute-done | bytes 65568 | tf_op jit(solution)/shard_map/ppermute | solution.py:354
  81.6 1.1 %shard_map.55 = (f32[64,128]{1,0:T(8,128)S(1)}, f32[32,16,128]{2,1,0:T(8,128)}) custom-call(f32[128,128]{1,0:T(8,128)S(1)} %get-tuple-element.33.sd, f32[192,128]{1,0:T(8,128)S(1)} %get-tuple-element.34.ccol, f32[128,128]{1,0:T(8,128)S(1)} %collective-permute-done.6.lo, f32[128,128]{1,0:T(8,128)S(1)} %collective-permute-done.7.hi), custom_call_target="tpu_custom_call" | custom-call | tf_op jit(solution)/shard_map/pallas_call | solution.py:375
  82.7 12.5 %all-to-all-start.1 = ((f32[32,16,128]{2,1,0:T(8,128)}), f32[32,16,128]{2,1,0:T(8,128)S(1)}, u32[]{:S(2)}, u32[]{:S(2)}) async-start(f32[32,16,128]{2,1,0:T(8,128)} %get-tuple-element.35), calls=%async_computation.1 | async-start | bytes 524288 | tf_op jit(solution)/shard_map/all_to_all | solution.py:376
  95.2 0.1 pad_add_fusion.place
  95.3 8.8 %all-to-all-done.1.gathered = f32[32,16,128]{2,1,0:T(8,128)S(1)} async-done(((f32[32,16,128]{2,1,0:T(8,128)}), f32[32,16,128]{2,1,0:T(8,128)S(1)}, u32[]{:S(2)}, u32[]{:S(2)}) %all-to-all-start.1) | async-done | bytes 262176 | tf_op jit(solution)/shard_map/all_to_all | solution.py:376
  104.1 4.1 %shard_map.56 = f32[4,4,256]{2,1,0:T(4,128)} custom-call(s32[2]{0:T(128)S(1)} %pad_add_fusion.place, f32[32,16,128]{2,1,0:T(8,128)S(1)} %all-to-all-done.1.gathered, f32[64,128]{1,0:T(8,128)S(1)} %get-tuple-element.36.elow, f32[4,4,256]{2,1,0:T(4,128)S(1)} %get-tuple-element.37.emid), custom_call_target="tpu_custom_call" | custom-call | tf_op jit(solution)/shard_map/pallas_call | solution.py:378
Async XLA Ops:
  0.6 0.9 copy-start
  1.5 0.9 copy-start.1
  2.4 0.9 copy-start.2
  3.5 8.4 %collective-permute-start = (f32[160,512]{1,0:T(8,128)S(1)}, f32[160,512]{1,0:T(8,128)S(1)}, u32[]{:S(2)}, u32[]{:S(2)}) collective-permute-start(f32[160,512]{1,0:T(8,128)S(1)} %get-tuple-element.20), channel_id=1, source_target_pairs={{0,1},{1,2},{2,3},{3,4},{4,5},{5,6},{6,7},{7,8},{8,9},{9,10},{10,1... | collective-permute-start | bytes 983048 | tf_op jit(solution)/shard_map/ppermute | solution.py:354
  7.9 8.0 %collective-permute-start.1 = (f32[160,512]{1,0:T(8,128)S(1)}, f32[160,512]{1,0:T(8,128)S(1)}, u32[]{:S(2)}, u32[]{:S(2)}) collective-permute-start(f32[160,512]{1,0:T(8,128)S(1)} %get-tuple-element.21), channel_id=1, source_target_pairs={{1,0},{2,1},{3,2},{4,3},{5,4},{6,5},{7,6},{8,7},{9,8},{10,9},{11,1... | collective-permute-start | bytes 983048 | tf_op jit(solution)/shard_map/ppermute | solution.py:354
  16.2 11.9 %collective-permute-start.2 = (f32[192,512]{1,0:T(8,128)S(1)}, f32[192,512]{1,0:T(8,128)S(1)}, u32[]{:S(2)}, u32[]{:S(2)}) collective-permute-start(f32[192,512]{1,0:T(8,128)S(1)} %get-tuple-element.25), channel_id=1, source_target_pairs={{0,16},{16,32},{32,48},{48,64},{64,80},{80,96},{96,112},{112,128},... | collective-permute-start | bytes 1179656 | tf_op jit(solution)/shard_map/ppermute | solution.py:354
  23.5 9.1 %collective-permute-start.3 = (f32[192,512]{1,0:T(8,128)S(1)}, f32[192,512]{1,0:T(8,128)S(1)}, u32[]{:S(2)}, u32[]{:S(2)}) collective-permute-start(f32[192,512]{1,0:T(8,128)S(1)} %get-tuple-element.26), channel_id=1, source_target_pairs={{16,0},{32,16},{48,32},{64,48},{80,64},{96,80},{112,96},{128,112},... | collective-permute-start | bytes 1179656 | tf_op jit(solution)/shard_map/ppermute | solution.py:354
  37.1 4.3 %collective-permute-start.4 = (f32[6,16,256]{2,1,0:T(8,128)S(1)}, f32[6,16,256]{2,1,0:T(8,128)S(1)}, u32[]{:S(2)}, u32[]{:S(2)}) collective-permute-start(f32[6,16,256]{2,1,0:T(8,128)S(1)} %get-tuple-element.30), channel_id=1, source_target_pairs={{0,16},{16,32},{32,48},{48,64},{64,80},{80,96},{96,112},{112,128},... | collective-permute-start | bytes 294920 | tf_op jit(solution)/shard_map/ppermute | solution.py:354
  39.0 5.9 %collective-permute-start.5 = (f32[6,16,256]{2,1,0:T(8,128)S(1)}, f32[6,16,256]{2,1,0:T(8,128)S(1)}, u32[]{:S(2)}, u32[]{:S(2)}) collective-permute-start(f32[6,16,256]{2,1,0:T(8,128)S(1)} %get-tuple-element.31), channel_id=1, source_target_pairs={{16,0},{32,16},{48,32},{64,48},{80,64},{96,80},{112,96},{128,112},... | collective-permute-start | bytes 294920 | tf_op jit(solution)/shard_map/ppermute | solution.py:354
  73.4 4.5 %collective-permute-start.6 = (f32[128,128]{1,0:T(8,128)S(1)}, f32[128,128]{1,0:T(8,128)S(1)}, u32[]{:S(2)}, u32[]{:S(2)}) collective-permute-start(f32[128,128]{1,0:T(8,128)S(1)} %get-tuple-element.33.sd), channel_id=1, source_target_pairs={{0,16},{16,32},{32,48},{48,64},{64,80},{80,96},{96,112},{112,128},... | collective-permute-start | bytes 196616 | tf_op jit(solution)/shard_map/ppermute | solution.py:354
  76.0 5.6 %collective-permute-start.7 = (f32[128,128]{1,0:T(8,128)S(1)}, f32[128,128]{1,0:T(8,128)S(1)}, u32[]{:S(2)}, u32[]{:S(2)}) collective-permute-start(f32[128,128]{1,0:T(8,128)S(1)} %get-tuple-element.33.sd), channel_id=1, source_target_pairs={{16,0},{32,16},{48,32},{64,48},{80,64},{96,80},{112,96},{128,112},... | collective-permute-start | bytes 196616 | tf_op jit(solution)/shard_map/ppermute | solution.py:354
  82.7 21.4 %all-to-all-start.1 = ((f32[32,16,128]{2,1,0:T(8,128)}), f32[32,16,128]{2,1,0:T(8,128)S(1)}, u32[]{:S(2)}, u32[]{:S(2)}) async-start(f32[32,16,128]{2,1,0:T(8,128)} %get-tuple-element.35), calls=%async_computation.1 | async-start | bytes 524288 | tf_op jit(solution)/shard_map/all_to_all | solution.py:376

commit v2 on v1

--- a/solution.py
+++ b/solution.py
@@ -10,18 +10,18 @@
 TINY = 1e-30
 F32 = jnp.float32
 VMEM = pl.BlockSpec(memory_space=pltpu.VMEM)
-SMEM = pl.BlockSpec(memory_space=pltpu.SMEM)
-PARAMS = pltpu.CompilerParams(vmem_limit_bytes=24 * 1024 * 1024)
-
-
-def call(kernel, out_shapes, scratch=(), specs=None, n_in=0):
+HBM = pl.BlockSpec(memory_space=pltpu.HBM)
+
+
+def call(kernel, out_shapes, scratch=(), n_in=0, copies=0, in_hbm=0, out_hbm=0, limit=24 * 1024 * 1024):
+    semaphores = [pltpu.SemaphoreType.DMA((copies,))] if copies else []
     return pl.pallas_call(
         kernel,
         out_shape=[jax.ShapeDtypeStruct(s, F32) for s in out_shapes],
-        in_specs=specs if specs is not None else [VMEM] * n_in,
-        out_specs=[VMEM] * len(out_shapes),
-        scratch_shapes=[pltpu.VMEM(s, F32) for s in scratch],
-        compiler_params=PARAMS,
+        in_specs=[HBM] * in_hbm + [VMEM] * (n_in - in_hbm),
+        out_specs=[HBM] * out_hbm + [VMEM] * (len(out_shapes) - out_hbm),
+        scratch_shapes=[pltpu.VMEM(s, F32) for s in scratch] + semaphores,
+        compiler_params=pltpu.CompilerParams(vmem_limit_bytes=limit),
     )
 
 
@@ -74,9 +74,15 @@
 NROWS = NP + NR + NC
 
 
-def pack_y(phi, rhs, coef, up, dn, stage):
+def pack_y(phi_in, rhs_in, coef_in, up_out, dn_out, phi, rhs, coef, stage, up, dn, sem):
+    loads = [pltpu.make_async_copy(src, dst, sem.at[a])
+             for a, (src, dst) in enumerate(((phi_in, phi), (rhs_in, rhs), (coef_in, coef)))]
+    for load in loads:
+        load.start()
+    stores = []
     k = 0
     for a, (ref, n) in enumerate(((phi, NP), (rhs, NR), (coef, NC))):
+        loads[a].wait()
         for q in range(4):
             lanes = slice(128 * q, 128 * q + 128)
             base = 64 * (4 * a + q)
@@ -85,7 +91,13 @@
                 rows = slice(8 * (k + j), 8 * (k + j) + 8)
                 up[rows, lanes] = stage[pl.ds(base + 8 - n + j, 8, stride=8), :]
                 dn[rows, lanes] = stage[pl.ds(base + j, 8, stride=8), :]
+        for b, (src, dst) in enumerate(((up, up_out), (dn, dn_out))):
+            part = pl.ds(8 * k, 8 * n)
+            stores.append(pltpu.make_async_copy(src.at[part], dst.at[part], sem.at[3 + 2 * a + b]))
+            stores[-1].start()
         k += n
+    for store in stores:
+        store.wait()
 
 
 def pack_x(phi, rhs, coef, lo, hi, pe, re, ce, up, dn, stage):
@@ -115,7 +127,7 @@
 
 
 def fine(pe, re, ce, lo, hi, phi_out, smid, cmid, mup, mdn,
-         p0, rs, c, hx, hy, hz, dg, rd, p1, p2, sums, packed):
+         p0, rs, c, hx, hy, hz, dg, rd, p1, p2, sums, packed, own, left):
     p0[0:3] = lo[0:3]
     p0[3:11] = pe[...]
     p0[11:14] = hi[0:3]
@@ -149,7 +161,9 @@
 
     lax.fori_loop(2, 12, second, 0)
     for x in range(8):
-        phi_out[x] = p2[3 + x, 0:8, :]
+        own[x] = p2[3 + x, 0:8, :]
+    store = pltpu.make_async_copy(own, phi_out, left.at[0])
+    store.start()
 
     def residual(i):
         return rs[i] - operate(dg[i], p2[i], hx[i], p2[i + 1], hx[i - 1], p2[i - 1], hy[i], hz[i])
@@ -179,6 +193,7 @@
     mup[2:6] = mid[4:8]
     mdn[0:2] = mid[0:2]
     mdn[2:6] = mid[4:8]
+    store.wait()
 
 
 def middle(smid, cmid, lo, hi, emid, out, sums):
@@ -269,7 +284,7 @@
         out[n] = both
 
 
-def bottom(place, gathered, elow, emid, out, hx, hy, hz, dg, sol, res, dire, img):
+def bottom(gathered, elow, emid, out, hx, hy, hz, dg, sol, res, dire, img):
     half = positions((16, 128), 1) < 64
     last_z = positions((16, 128), 1) % 64 == 63
     last_y = positions((16, 128), 0) == 15
@@ -325,7 +340,7 @@
         return new
 
     rr = lax.fori_loop(0, BOTTOM - 1, step, norm())
-    gx, gy = place[0], place[1]
+    gx, gy = lax.axis_index("gx"), lax.axis_index("gy")
     xi = lax.rem(gx, 16)
     alpha = rr / dot_image()
     mine = sol[xi] + alpha * dire[xi]
@@ -356,7 +371,9 @@
 
 def shards(phi_start, right_side, coefficient):
     own = [a.reshape(64, 512) for a in (phi_start, right_side, coefficient)]
-    up, dn = call(pack_y, [(8 * NROWS, 512)] * 2, [(768, 128)], n_in=3)(*own)
+    up, dn = call(
+        pack_y, [(8 * NROWS, 512)] * 2, [(64, 512)] * 3 + [(768, 128)] + [(8 * NROWS, 512)] * 2,
+        n_in=3, copies=9, in_hbm=3, out_hbm=2, limit=64000000)(*own)
     lo, hi = neighbours(up, dn, "gy")
     *ext, up, dn = call(pack_x, [(192, 512)] * 5, [(1536, 128)], n_in=5)(*own, lo, hi)
     lo, hi = neighbours(up, dn, "gx")
@@ -364,8 +381,8 @@
     phi_fine, smid, cmid, up, dn = call(
         fine,
         [(8, 8, 512), (4, 16, 256), (4, 16, 256), (6, 16, 256), (6, 16, 256)],
-        [box] * 10 + [(4, 8, 24, 128), (128, 512)],
-        n_in=5,
+        [box] * 10 + [(4, 8, 24, 128), (128, 512), (8, 8, 512)],
+        n_in=5, copies=1, out_hbm=1,
     )(*[a.reshape(8, 24, 512) for a in (*ext, lo, hi)])
     lo, hi = neighbours(up, dn, "gx")
     emid, spread = call(middle, [(4, 4, 256), (16, 16, 128)], [(128, 128)], n_in=4)(smid, cmid, lo, hi)
@@ -374,13 +391,8 @@
     lo, hi = neighbours(sd, sd, "gx")
     elow, spread = call(low, [(64, 128), (32, 16, 128)], [(64, 128)], n_in=4)(sd, ccol, lo, hi)
     gathered = lax.all_to_all(spread, "gx", 0, 0, tiled=True)
-    place = jnp.stack([lax.axis_index("gx"), lax.axis_index("gy")]).astype(jnp.int32)
-    (correction,) = call(
-        bottom,
-        [(4, 4, 256)],
-        [(17, 16, 128)] + [(16, 16, 128)] * 7,
-        specs=[SMEM, VMEM, VMEM, VMEM],
-    )(place, gathered, elow, emid)
+    (correction,) = call(bottom, [(4, 4, 256)], [(17, 16, 128)] + [(16, 16, 128)] * 7, n_in=3)(
+        gathered, elow, emid)
     return phi_fine, correction
 
 

time: 109 us -> 106 us (0.972)
  blocking collectives: 27.7 us -> 50.1 us
  starting transfers between devices: 36.1 us -> 24.7 us
  waiting for transfers between devices: 29.8 us -> 18.9 us
  local copies, waits for them, and re-layouts: 2.7 us -> 0.01 us
    all_to_all x0 -> x1, blocking collectives: none -> 22.5 us  [shards(): gathered = lax.all_to_all(spread, 'gx', 0, 0, tiled=True)]
    all_to_all x1 -> x0, starting transfers between devices: 12.5 us -> none  [shards(): gathered = lax.all_to_all(spread, 'gx', 0, 0, tiled=True)]
    all_to_all x1 -> x0, waiting for transfers between devices: 8.82 us -> none  [shards(): gathered = lax.all_to_all(spread, 'gx', 0, 0, tiled=True)]
    unnamed x6, local copies, waits for them, and re-layouts: 2.7 us -> 0.01 us
    ppermute x8, waiting for transfers between devices: 21 us -> 18.9 us  [neighbours(): return (lax.ppermute(up, axis, forth), lax.ppermute(dn, axis, back))]
    pallas_call x2, Pallas kernels: 4.19 us -> 5.48 us  [the longest x1 3.54 us: shards(): call(bottom, [(4, 4, 256)], [(17, 16, 128)] + [(16, 16, 128)] * 7, n_in=3)]
  transfers between devices with their start and end apart: 9 -> 8, of which waited for: 7 -> 6; matrix products, arithmetic and copies ran while one was open for 0% -> 0% of each run, Pallas kernels for 0% -> 0%
where the time goes in v2:
time: 106 us
  blocking collectives  50.1 us (47%)
  starting transfers between devices  24.7 us (23%)
  waiting for transfers between devices  18.9 us (18%)
  Pallas kernels  11.5 us (11%)
    all_to_all x1, blocking collectives, shards(): gathered = lax.all_to_all(spread, 'gy', 0, 0, tiled=True)  27.7 us
    ppermute x8, starting transfers between devices, neighbours(): return (lax.ppermute(up, axis, forth), lax.ppermute(dn, axis, back))  24.7 us
    all_to_all x1, blocking collectives, shards(): gathered = lax.all_to_all(spread, 'gx', 0, 0, tiled=True)  22.5 us
    ppermute x8, waiting for transfers between devices, neighbours(): return (lax.ppermute(up, axis, forth), lax.ppermute(dn, axis, back))  18.9 us
    pallas_call x1, Pallas kernels, shards(): call(fine, [(8, 8, 512), (4, 16, 256), (4, 16, 256), (6, 16, 256), (6, 16...  4.42 us
    pallas_call x1, Pallas kernels, shards(): call(bottom, [(4, 4, 256)], [(17, 16, 128)] + [(16, 16, 128)] * 7, n_in=3)  3.54 us
  transfers between devices with their start and end apart: 8, of which 6 were waited for; matrix products, arithmetic and copies ran while one was open for 0% of the time, Pallas kernels for 0%

profile of v2, /device:TPU:1, one launch (start us, length us, event | category | flops | bytes accessed | tf_op | source)
XLA Modules:
  0.0 106.0 jit_solution(7106114489360086742)
XLA Ops:
  0.6 0.0 copy-start
  0.6 0.0 copy-start.1
  0.6 0.0 copy-start.2
  0.7 1.9 %shard_map.50 = (f32[160,512]{1,0:T(8,128)}, f32[160,512]{1,0:T(8,128)}) custom-call(f32[64,512]{1,0:T(8,128)} %bitcast.10, f32[64,512]{1,0:T(8,128)} %bitcast.12, f32[64,512]{1,0:T(8,128)} %bitcast.14), custom_call_target="tpu_custom_call" | custom-call | tf_op jit(solution)/shard_map/pallas_call | solution.py:374
  2.6 4.4 %collective-permute-start = (f32[160,512]{1,0:T(8,128)}, f32[160,512]{1,0:T(8,128)S(1)}, u32[]{:S(2)}, u32[]{:S(2)}) collective-permute-start(f32[160,512]{1,0:T(8,128)} %get-tuple-element.20), channel_id=1, source_target_pairs={{0,1},{1,2},{2,3},{3,4},{4,5},{5,6},{6,7},{7,8},{8,9},{9,10},{10,1... | collective-permute-start | bytes 983048 | tf_op jit(solution)/shard_map/ppermute | solution.py:369
  7.0 1.3 %collective-permute-start.1 = (f32[160,512]{1,0:T(8,128)}, f32[160,512]{1,0:T(8,128)S(1)}, u32[]{:S(2)}, u32[]{:S(2)}) collective-permute-start(f32[160,512]{1,0:T(8,128)} %get-tuple-element.21), channel_id=1, source_target_pairs={{1,0},{2,1},{3,2},{4,3},{5,4},{6,5},{7,6},{8,7},{9,8},{10,9},{11,1... | collective-permute-start | bytes 983048 | tf_op jit(solution)/shard_map/ppermute | solution.py:369
  8.3 3.0 %collective-permute-done.lo = f32[160,512]{1,0:T(8,128)S(1)} collective-permute-done((f32[160,512]{1,0:T(8,128)}, f32[160,512]{1,0:T(8,128)S(1)}, u32[]{:S(2)}, u32[]{:S(2)}) %collective-permute-start) | collective-permute-done | bytes 327712 | tf_op jit(solution)/shard_map/ppermute | solution.py:369
  11.3 3.9 %collective-permute-done.1.hi = f32[160,512]{1,0:T(8,128)S(1)} collective-permute-done((f32[160,512]{1,0:T(8,128)}, f32[160,512]{1,0:T(8,128)S(1)}, u32[]{:S(2)}, u32[]{:S(2)}) %collective-permute-start.1) | collective-permute-done | bytes 327712 | tf_op jit(solution)/shard_map/ppermute | solution.py:369
  15.2 0.0 copy-done
  15.2 0.0 copy-done.1
  15.2 0.0 copy-done.2
  15.2 0.4 shard_map.51
  15.6 7.2 %collective-permute-start.2 = (f32[192,512]{1,0:T(8,128)S(1)}, f32[192,512]{1,0:T(8,128)S(1)}, u32[]{:S(2)}, u32[]{:S(2)}) collective-permute-start(f32[192,512]{1,0:T(8,128)S(1)} %get-tuple-element.25), channel_id=1, source_target_pairs={{0,16},{16,32},{32,48},{48,64},{64,80},{80,96},{96,112},{112,128},... | collective-permute-start | bytes 1179656 | tf_op jit(solution)/shard_map/ppermute | solution.py:369
  22.8 1.9 %collective-permute-start.3 = (f32[192,512]{1,0:T(8,128)S(1)}, f32[192,512]{1,0:T(8,128)S(1)}, u32[]{:S(2)}, u32[]{:S(2)}) collective-permute-start(f32[192,512]{1,0:T(8,128)S(1)} %get-tuple-element.26), channel_id=1, source_target_pairs={{16,0},{32,16},{48,32},{64,48},{80,64},{96,80},{112,96},{128,112},... | collective-permute-start | bytes 1179656 | tf_op jit(solution)/shard_map/ppermute | solution.py:369
  24.8 2.8 %collective-permute-done.2 = f32[192,512]{1,0:T(8,128)S(1)} collective-permute-done((f32[192,512]{1,0:T(8,128)S(1)}, f32[192,512]{1,0:T(8,128)S(1)}, u32[]{:S(2)}, u32[]{:S(2)}) %collective-permute-start.2) | collective-permute-done | bytes 393248 | tf_op jit(solution)/shard_map/ppermute | solution.py:369
  27.5 4.4 %collective-permute-done.3 = f32[192,512]{1,0:T(8,128)S(1)} collective-permute-done((f32[192,512]{1,0:T(8,128)S(1)}, f32[192,512]{1,0:T(8,128)S(1)}, u32[]{:S(2)}, u32[]{:S(2)}) %collective-permute-start.3) | collective-permute-done | bytes 393248 | tf_op jit(solution)/shard_map/ppermute | solution.py:369
  31.9 4.4 %shard_map.52 = (f32[8,8,512]{2,1,0:T(8,128)}, f32[4,16,256]{2,1,0:T(8,128)S(1)}, f32[4,16,256]{2,1,0:T(8,128)S(1)}, f32[6,16,256]{2,1,0:T(8,128)S(1)}, f32[6,16,256]{2,1,0:T(8,128)S(1)}) custom-call(f32[8,24,512]{2,1,0:T(8,128)S(1)} %bitcast.16, f32[8,24,512]{2,1,0:T(8,128)S(1)} %bitcast.17, f32[8,24,512]{2,1,0:T(8,128)S(1)} %bitcast.18, ...), custom_call_target="tpu_custom_call" | custom-call | tf_op jit(solution)/shard_map/pallas_call | solution.py:381
  36.3 1.9 %collective-permute-start.4 = (f32[6,16,256]{2,1,0:T(8,128)S(1)}, f32[6,16,256]{2,1,0:T(8,128)S(1)}, u32[]{:S(2)}, u32[]{:S(2)}) collective-permute-start(f32[6,16,256]{2,1,0:T(8,128)S(1)} %get-tuple-element.30), channel_id=1, source_target_pairs={{0,16},{16,32},{32,48},{48,64},{64,80},{80,96},{96,112},{112,128},... | collective-permute-start | bytes 294920 | tf_op jit(solution)/shard_map/ppermute | solution.py:369
  38.3 2.4 %collective-permute-start.5 = (f32[6,16,256]{2,1,0:T(8,128)S(1)}, f32[6,16,256]{2,1,0:T(8,128)S(1)}, u32[]{:S(2)}, u32[]{:S(2)}) collective-permute-start(f32[6,16,256]{2,1,0:T(8,128)S(1)} %get-tuple-element.31), channel_id=1, source_target_pairs={{16,0},{32,16},{48,32},{64,48},{80,64},{96,80},{112,96},{128,112},... | collective-permute-start | bytes 294920 | tf_op jit(solution)/shard_map/ppermute | solution.py:369
  40.7 0.0 collective-permute-done.4.lo
  40.7 3.5 %collective-permute-done.5.hi = f32[6,16,256]{2,1,0:T(8,128)S(1)} collective-permute-done((f32[6,16,256]{2,1,0:T(8,128)S(1)}, f32[6,16,256]{2,1,0:T(8,128)S(1)}, u32[]{:S(2)}, u32[]{:S(2)}) %collective-permute-start.5) | collective-permute-done | bytes 98336 | tf_op jit(solution)/shard_map/ppermute | solution.py:369
  44.2 0.6 shard_map.53
  44.8 27.7 %all_to_all.10 = f32[16,16,128]{2,1,0:T(8,128)S(1)} all-to-all(f32[16,16,128]{2,1,0:T(8,128)S(1)} %get-tuple-element.32), channel_id=1, replica_groups=mesh['gx'=32,'gy'=16] {'gy'}, dimensions={0} | all-to-all | bytes 262144 | tf_op jit(solution)/shard_map/all_to_all | solution.py:389
  72.5 0.2 shard_map.54
  72.7 1.9 %collective-permute-start.7 = (f32[128,128]{1,0:T(8,128)S(1)}, f32[128,128]{1,0:T(8,128)S(1)}, u32[]{:S(2)}, u32[]{:S(2)}) collective-permute-start(f32[128,128]{1,0:T(8,128)S(1)} %get-tuple-element.33.sd), channel_id=1, source_target_pairs={{16,0},{32,16},{48,32},{64,48},{80,64},{96,80},{112,96},{128,112},... | collective-permute-start | bytes 196616 | tf_op jit(solution)/shard_map/ppermute | solution.py:369
  74.6 3.6 %collective-permute-start.6 = (f32[128,128]{1,0:T(8,128)S(1)}, f32[128,128]{1,0:T(8,128)S(1)}, u32[]{:S(2)}, u32[]{:S(2)}) collective-permute-start(f32[128,128]{1,0:T(8,128)S(1)} %get-tuple-element.33.sd), channel_id=1, source_target_pairs={{0,16},{16,32},{32,48},{48,64},{64,80},{80,96},{96,112},{112,128},... | collective-permute-start | bytes 196616 | tf_op jit(solution)/shard_map/ppermute | solution.py:369
  78.3 0.0 collective-permute-done.7.hi
  78.3 1.3 %collective-permute-done.6.lo = f32[128,128]{1,0:T(8,128)S(1)} collective-permute-done((f32[128,128]{1,0:T(8,128)S(1)}, f32[128,128]{1,0:T(8,128)S(1)}, u32[]{:S(2)}, u32[]{:S(2)}) %collective-permute-start.6) | collective-permute-done | bytes 65568 | tf_op jit(solution)/shard_map/ppermute | solution.py:369
  79.6 0.4 shard_map.55
  80.0 22.5 %all_to_all.11.gathered = f32[32,16,128]{2,1,0:T(8,128)S(1)} all-to-all(f32[32,16,128]{2,1,0:T(8,128)S(1)} %get-tuple-element.35), channel_id=1, replica_groups=mesh['gx'=32,'gy'=16] {'gx'}, dimensions={0} | all-to-all | bytes 524288 | tf_op jit(solution)/shard_map/all_to_all | solution.py:393
  102.5 3.5 %shard_map.56 = f32[4,4,256]{2,1,0:T(4,128)} custom-call(f32[32,16,128]{2,1,0:T(8,128)S(1)} %all_to_all.11.gathered, f32[64,128]{1,0:T(8,128)S(1)} %get-tuple-element.36.elow, f32[4,4,256]{2,1,0:T(4,128)S(1)} %get-tuple-element.37.emid), custom_call_target="tpu_custom_call" | custom-call | tf_op jit(solution)/shard_map/pallas_call | solution.py:394
Async XLA Ops:
  0.6 14.6 %copy-start = (f32[8,8,512]{2,1,0:T(8,128)S(1)}, f32[8,8,512]{2,1,0:T(8,128)}, u32[]{:S(2)}) copy-start(f32[8,8,512]{2,1,0:T(8,128)} %param.3) | copy-start | bytes 393220
  0.6 14.6 %copy-start.1 = (f32[8,8,512]{2,1,0:T(8,128)S(1)}, f32[8,8,512]{2,1,0:T(8,128)}, u32[]{:S(2)}) copy-start(f32[8,8,512]{2,1,0:T(8,128)} %param.4) | copy-start | bytes 393220
  0.6 14.6 %copy-start.2 = (f32[8,8,512]{2,1,0:T(8,128)S(1)}, f32[8,8,512]{2,1,0:T(8,128)}, u32[]{:S(2)}) copy-start(f32[8,8,512]{2,1,0:T(8,128)} %param.5) | copy-start | bytes 393220
  2.6 8.7 %collective-permute-start = (f32[160,512]{1,0:T(8,128)}, f32[160,512]{1,0:T(8,128)S(1)}, u32[]{:S(2)}, u32[]{:S(2)}) collective-permute-start(f32[160,512]{1,0:T(8,128)} %get-tuple-element.20), channel_id=1, source_target_pairs={{0,1},{1,2},{2,3},{3,4},{4,5},{5,6},{6,7},{7,8},{8,9},{9,10},{10,1... | collective-permute-start | bytes 983048 | tf_op jit(solution)/shard_map/ppermute | solution.py:369
  7.0 8.2 %collective-permute-start.1 = (f32[160,512]{1,0:T(8,128)}, f32[160,512]{1,0:T(8,128)S(1)}, u32[]{:S(2)}, u32[]{:S(2)}) collective-permute-start(f32[160,512]{1,0:T(8,128)} %get-tuple-element.21), channel_id=1, source_target_pairs={{1,0},{2,1},{3,2},{4,3},{5,4},{6,5},{7,6},{8,7},{9,8},{10,9},{11,1... | collective-permute-start | bytes 983048 | tf_op jit(solution)/shard_map/ppermute | solution.py:369
  15.6 11.9 %collective-permute-start.2 = (f32[192,512]{1,0:T(8,128)S(1)}, f32[192,512]{1,0:T(8,128)S(1)}, u32[]{:S(2)}, u32[]{:S(2)}) collective-permute-start(f32[192,512]{1,0:T(8,128)S(1)} %get-tuple-element.25), channel_id=1, source_target_pairs={{0,16},{16,32},{32,48},{48,64},{64,80},{80,96},{96,112},{112,128},... | collective-permute-start | bytes 1179656 | tf_op jit(solution)/shard_map/ppermute | solution.py:369
  22.8 9.1 %collective-permute-start.3 = (f32[192,512]{1,0:T(8,128)S(1)}, f32[192,512]{1,0:T(8,128)S(1)}, u32[]{:S(2)}, u32[]{:S(2)}) collective-permute-start(f32[192,512]{1,0:T(8,128)S(1)} %get-tuple-element.26), channel_id=1, source_target_pairs={{16,0},{32,16},{48,32},{64,48},{80,64},{96,80},{112,96},{128,112},... | collective-permute-start | bytes 1179656 | tf_op jit(solution)/shard_map/ppermute | solution.py:369
  36.3 4.3 %collective-permute-start.4 = (f32[6,16,256]{2,1,0:T(8,128)S(1)}, f32[6,16,256]{2,1,0:T(8,128)S(1)}, u32[]{:S(2)}, u32[]{:S(2)}) collective-permute-start(f32[6,16,256]{2,1,0:T(8,128)S(1)} %get-tuple-element.30), channel_id=1, source_target_pairs={{0,16},{16,32},{32,48},{48,64},{64,80},{80,96},{96,112},{112,128},... | collective-permute-start | bytes 294920 | tf_op jit(solution)/shard_map/ppermute | solution.py:369
  38.3 5.9 %collective-permute-start.5 = (f32[6,16,256]{2,1,0:T(8,128)S(1)}, f32[6,16,256]{2,1,0:T(8,128)S(1)}, u32[]{:S(2)}, u32[]{:S(2)}) collective-permute-start(f32[6,16,256]{2,1,0:T(8,128)S(1)} %get-tuple-element.31), channel_id=1, source_target_pairs={{16,0},{32,16},{48,32},{64,48},{80,64},{96,80},{112,96},{128,112},... | collective-permute-start | bytes 294920 | tf_op jit(solution)/shard_map/ppermute | solution.py:369
  72.7 5.6 %collective-permute-start.7 = (f32[128,128]{1,0:T(8,128)S(1)}, f32[128,128]{1,0:T(8,128)S(1)}, u32[]{:S(2)}, u32[]{:S(2)}) collective-permute-start(f32[128,128]{1,0:T(8,128)S(1)} %get-tuple-element.33.sd), channel_id=1, source_target_pairs={{16,0},{32,16},{48,32},{64,48},{80,64},{96,80},{112,96},{128,112},... | collective-permute-start | bytes 196616 | tf_op jit(solution)/shard_map/ppermute | solution.py:369
  74.6 5.0 %collective-permute-start.6 = (f32[128,128]{1,0:T(8,128)S(1)}, f32[128,128]{1,0:T(8,128)S(1)}, u32[]{:S(2)}, u32[]{:S(2)}) collective-permute-start(f32[128,128]{1,0:T(8,128)S(1)} %get-tuple-element.33.sd), channel_id=1, source_target_pairs={{0,16},{16,32},{32,48},{48,64},{64,80},{80,96},{96,112},{112,128},... | collective-permute-start | bytes 196616 | tf_op jit(solution)/shard_map/ppermute | solution.py:369

commit v3 on v2

--- a/solution.py
+++ b/solution.py
@@ -32,6 +32,10 @@
 def along(v, axis, step):
     n = v.shape[axis]
     return pltpu.roll(v, (-step) % n, axis)
+
+
+def is_first():
+    return lax.rem(lax.axis_index("gx"), 2) == 0
 
 
 def positions(shape, axis):
@@ -100,7 +104,7 @@
         store.wait()
 
 
-def pack_x(phi, rhs, coef, lo, hi, pe, re, ce, up, dn, stage):
+def pack_x(phi, rhs, coef, lo, hi, pe, re, ce, mate, other, stage):
     zero = jnp.zeros((8, 128), F32)
     k = 0
     for a, (ref, ext, n) in enumerate(((phi, pe, NP), (rhs, re, NR), (coef, ce, NC))):
@@ -118,28 +122,29 @@
             for x in range(8):
                 ext[24 * x + 8:24 * x + 24, lanes] = stage[base + 16 * x:base + 16 * x + 16, :]
         k += n
-    up[0:72, :] = pe[120:192, :]
-    up[72:120, :] = re[144:192, :]
-    up[120:192, :] = ce[120:192, :]
-    dn[0:72, :] = pe[0:72, :]
-    dn[72:120, :] = re[0:48, :]
-    dn[120:192, :] = ce[0:72, :]
-
-
-def fine(pe, re, ce, lo, hi, phi_out, smid, cmid, mup, mdn,
+    first = is_first()
+    for ref, end in ((mate, first), (other, jnp.logical_not(first))):
+        three = pl.multiple_of(jnp.where(end, 120, 0), 8)
+        two = pl.multiple_of(jnp.where(end, 144, 0), 8)
+        ref[0:72, :] = pe[pl.ds(three, 72), :]
+        ref[72:120, :] = re[pl.ds(two, 48), :]
+        ref[120:192, :] = ce[pl.ds(three, 72), :]
+
+
+def fine(pe, re, ce, other, mate, phi_out, smid, cmid, mmate, mother,
          p0, rs, c, hx, hy, hz, dg, rd, p1, p2, sums, packed, own, left):
-    p0[0:3] = lo[0:3]
+    first = is_first()
     p0[3:11] = pe[...]
-    p0[11:14] = hi[0:3]
-    rs[1:3] = lo[3:5]
     rs[3:11] = re[...]
-    rs[11:13] = hi[3:5]
-    c[0:3] = lo[5:8]
     c[3:11] = ce[...]
-    c[11:14] = hi[5:8]
+    for ref, end in ((mate, first), (other, jnp.logical_not(first))):
+        three = jnp.where(end, 11, 0)
+        p0[pl.ds(three, 3)] = ref[0:3]
+        rs[pl.ds(jnp.where(end, 11, 1), 2)] = ref[3:5]
+        c[pl.ds(three, 3)] = ref[5:8]
     hx[0] = harmonic(c[0], c[1])
 
-    def first(i, carry):
+    def start(i, carry):
         ci = c[i]
         xp, xm = harmonic(ci, c[i + 1]), hx[i - 1]
         hyi = harmonic(ci, along(ci, 0, 1))
@@ -151,7 +156,7 @@
         p1[i] = v + (rs[i] - operate(d, v, xp, p0[i + 1], xm, p0[i - 1], hyi, hzi)) * r
         return carry
 
-    lax.fori_loop(1, 13, first, 0)
+    lax.fori_loop(1, 13, start, 0)
 
     def second(i, carry):
         v = p1[i]
@@ -189,14 +194,17 @@
     mid = matmul(packed[...], halving(512, 256)).reshape(8, 16, 256)
     smid[...] = mid[0:4]
     cmid[...] = mid[4:8]
-    mup[0:2] = mid[2:4]
-    mup[2:6] = mid[4:8]
-    mdn[0:2] = mid[0:2]
-    mdn[2:6] = mid[4:8]
+    mmate[0:2] = jnp.where(first, mid[2:4], mid[0:2])
+    mmate[2:6] = mid[4:8]
+    mother[0:2] = jnp.where(first, mid[0:2], mid[2:4])
+    mother[2:6] = mid[4:8]
     store.wait()
 
 
-def middle(smid, cmid, lo, hi, emid, out, sums):
+def middle(smid, cmid, other, mate, emid, out, sums):
+    first = is_first()
+    hi = [jnp.where(first, mate[j], other[j]) for j in range(6)]
+    lo = [jnp.where(first, other[j], mate[j]) for j in range(6)]
     s = [lo[0], lo[1]] + [smid[x] for x in range(4)] + [hi[0], hi[1]]
     c = [lo[2 + x] for x in range(4)] + [cmid[x] for x in range(4)] + [hi[2 + x] for x in range(4)]
     hx = [harmonic(c[j], c[j + 1]) for j in range(1, 10)]
@@ -253,7 +261,11 @@
         sd[64 + 32 * x:96 + 32 * x, :] = diagonal_of(ci, hx[x + 1], hx[x], y_face(ci), z_face(ci))
 
 
-def low(sd, ccol, lo, hi, elow, out, sums):
+def low(sd, ccol, mate, other, elow, out, sums):
+    first = is_first()
+    hi = jnp.where(first, mate[...], other[...])
+    lo = jnp.where(first, other[...], mate[...])
+
     def part(ref, k):
         return ref[32 * k:32 * k + 32, :]
 
@@ -369,27 +381,34 @@
     return lax.ppermute(up, axis, forth), lax.ppermute(dn, axis, back)
 
 
+def neighbours_x(mate, other):
+    n = lax.axis_size("gx")
+    far = [(i, i + 1) for i in range(1, n - 1, 2)] + [(i + 1, i) for i in range(1, n - 1, 2)]
+    other = lax.ppermute(other, "gx", far)
+    return lax.ppermute(mate, "gx", [(i, i ^ 1) for i in range(n)]), other
+
+
 def shards(phi_start, right_side, coefficient):
     own = [a.reshape(64, 512) for a in (phi_start, right_side, coefficient)]
     up, dn = call(
         pack_y, [(8 * NROWS, 512)] * 2, [(64, 512)] * 3 + [(768, 128)] + [(8 * NROWS, 512)] * 2,
         n_in=3, copies=9, in_hbm=3, out_hbm=2, limit=64000000)(*own)
     lo, hi = neighbours(up, dn, "gy")
-    *ext, up, dn = call(pack_x, [(192, 512)] * 5, [(1536, 128)], n_in=5)(*own, lo, hi)
-    lo, hi = neighbours(up, dn, "gx")
+    *ext, mate, other = call(pack_x, [(192, 512)] * 5, [(1536, 128)], n_in=5)(*own, lo, hi)
+    mate, other = neighbours_x(mate, other)
     box = (14, 24, 512)
-    phi_fine, smid, cmid, up, dn = call(
+    phi_fine, smid, cmid, mate, other = call(
         fine,
         [(8, 8, 512), (4, 16, 256), (4, 16, 256), (6, 16, 256), (6, 16, 256)],
         [box] * 10 + [(4, 8, 24, 128), (128, 512), (8, 8, 512)],
         n_in=5, copies=1, out_hbm=1,
-    )(*[a.reshape(8, 24, 512) for a in (*ext, lo, hi)])
-    lo, hi = neighbours(up, dn, "gx")
-    emid, spread = call(middle, [(4, 4, 256), (16, 16, 128)], [(128, 128)], n_in=4)(smid, cmid, lo, hi)
+    )(*[a.reshape(8, 24, 512) for a in (*ext, other, mate)])
+    mate, other = neighbours_x(mate, other)
+    emid, spread = call(middle, [(4, 4, 256), (16, 16, 128)], [(128, 128)], n_in=4)(smid, cmid, other, mate)
     gathered = lax.all_to_all(spread, "gy", 0, 0, tiled=True)
     sd, ccol = call(columns, [(128, 128), (192, 128)], n_in=1)(gathered.reshape(256, 128))
-    lo, hi = neighbours(sd, sd, "gx")
-    elow, spread = call(low, [(64, 128), (32, 16, 128)], [(64, 128)], n_in=4)(sd, ccol, lo, hi)
+    mate, other = neighbours_x(sd, sd)
+    elow, spread = call(low, [(64, 128), (32, 16, 128)], [(64, 128)], n_in=4)(sd, ccol, mate, other)
     gathered = lax.all_to_all(spread, "gx", 0, 0, tiled=True)
     (correction,) = call(bottom, [(4, 4, 256)], [(17, 16, 128)] + [(16, 16, 128)] * 7, n_in=3)(
         gathered, elow, emid)

time: 106 us -> 98.3 us (0.927)
  waiting for transfers between devices: 18.9 us -> 12.9 us
  blocking collectives: 50.1 us -> 44.8 us
  starting transfers between devices: 24.7 us -> 28 us
    ppermute x0 -> x6, starting transfers between devices: none -> 22.3 us  [the longest x3 16.5 us: neighbours_x(): other = lax.ppermute(other, 'gx', far)]
    ppermute x8 -> x2, starting transfers between devices: 24.7 us -> 5.68 us  [neighbours(): return (lax.ppermute(up, axis, forth), lax.ppermute(dn, axis, back))]
    ppermute x8 -> x2, waiting for transfers between devices: 18.9 us -> 6.9 us  [neighbours(): return (lax.ppermute(up, axis, forth), lax.ppermute(dn, axis, back))]
    ppermute x0 -> x6, waiting for transfers between devices: none -> 6 us  [the longest x3 3.88 us: neighbours_x(): other = lax.ppermute(other, 'gx', far)]
    all_to_all x1, blocking collectives: 22.5 us -> 18.2 us  [shards(): gathered = lax.all_to_all(spread, 'gx', 0, 0, tiled=True)]
    all_to_all x1, blocking collectives: 27.7 us -> 26.5 us  [shards(): gathered = lax.all_to_all(spread, 'gy', 0, 0, tiled=True)]
where the time goes in v3:
time: 98.3 us; the launch traced here: 97.9 us
  blocking collectives  44.8 us (46%)
  starting transfers between devices  28 us (28%)
  waiting for transfers between devices  12.9 us (13%)
  Pallas kernels  11.5 us (12%)
    all_to_all x1, blocking collectives, shards(): gathered = lax.all_to_all(spread, 'gy', 0, 0, tiled=True)  26.5 us
    all_to_all x1, blocking collectives, shards(): gathered = lax.all_to_all(spread, 'gx', 0, 0, tiled=True)  18.2 us
    ppermute x3, starting transfers between devices, neighbours_x(): other = lax.ppermute(other, 'gx', far)  16.5 us
    ppermute x2, waiting for transfers between devices, neighbours(): return (lax.ppermute(up, axis, forth), lax.ppermute(dn, axis, back))  6.9 us
    ppermute x3, starting transfers between devices, neighbours_x(): return (lax.ppermute(mate, 'gx', [(i, i ^ 1) for i in range(n)]), other)  5.76 us
    ppermute x2, starting transfers between devices, neighbours(): return (lax.ppermute(up, axis, forth), lax.ppermute(dn, axis, back))  5.68 us
    pallas_call x1, Pallas kernels, shards(): call(fine, [(8, 8, 512), (4, 16, 256), (4, 16, 256), (6, 16, 256), (6, 16...  4.41 us
    ppermute x3, waiting for transfers between devices, neighbours_x(): other = lax.ppermute(other, 'gx', far)  3.88 us
  transfers between devices with their start and end apart: 8, of which 6 were waited for; matrix products, arithmetic and copies ran while one was open for 0% of the time, Pallas kernels for 0%

profile of v3, /device:TPU:1, one launch (start us, length us, event | category | flops | bytes accessed | tf_op | source)
XLA Modules:
  0.0 97.9 jit_solution(8809623450189076103)
XLA Ops:
  0.6 0.0 copy-start
  0.6 0.0 copy-start.1
  0.6 0.0 copy-start.2
  0.7 1.9 %shard_map.50 = (f32[160,512]{1,0:T(8,128)}, f32[160,512]{1,0:T(8,128)}) custom-call(f32[64,512]{1,0:T(8,128)} %bitcast.10, f32[64,512]{1,0:T(8,128)} %bitcast.12, f32[64,512]{1,0:T(8,128)} %bitcast.14), custom_call_target="tpu_custom_call" | custom-call | tf_op jit(solution)/shard_map/pallas_call | solution.py:393
  2.6 4.4 %collective-permute-start = (f32[160,512]{1,0:T(8,128)}, f32[160,512]{1,0:T(8,128)S(1)}, u32[]{:S(2)}, u32[]{:S(2)}) collective-permute-start(f32[160,512]{1,0:T(8,128)} %get-tuple-element.20), channel_id=1, source_target_pairs={{0,1},{1,2},{2,3},{3,4},{4,5},{5,6},{6,7},{7,8},{8,9},{9,10},{10,1... | collective-permute-start | bytes 983048 | tf_op jit(solution)/shard_map/ppermute | solution.py:381
  7.0 1.3 %collective-permute-start.1 = (f32[160,512]{1,0:T(8,128)}, f32[160,512]{1,0:T(8,128)S(1)}, u32[]{:S(2)}, u32[]{:S(2)}) collective-permute-start(f32[160,512]{1,0:T(8,128)} %get-tuple-element.21), channel_id=1, source_target_pairs={{1,0},{2,1},{3,2},{4,3},{5,4},{6,5},{7,6},{8,7},{9,8},{10,9},{11,1... | collective-permute-start | bytes 983048 | tf_op jit(solution)/shard_map/ppermute | solution.py:381
  8.3 3.0 %collective-permute-done.lo = f32[160,512]{1,0:T(8,128)S(1)} collective-permute-done((f32[160,512]{1,0:T(8,128)}, f32[160,512]{1,0:T(8,128)S(1)}, u32[]{:S(2)}, u32[]{:S(2)}) %collective-permute-start) | collective-permute-done | bytes 327712 | tf_op jit(solution)/shard_map/ppermute | solution.py:381
  11.3 3.9 %collective-permute-done.1.hi = f32[160,512]{1,0:T(8,128)S(1)} collective-permute-done((f32[160,512]{1,0:T(8,128)}, f32[160,512]{1,0:T(8,128)S(1)}, u32[]{:S(2)}, u32[]{:S(2)}) %collective-permute-start.1) | collective-permute-done | bytes 327712 | tf_op jit(solution)/shard_map/ppermute | solution.py:381
  15.2 0.0 copy-done
  15.2 0.0 copy-done.1
  15.2 0.0 copy-done.2
  15.2 0.4 shard_map.51
  15.6 7.2 %collective-permute-start.2 = (f32[192,512]{1,0:T(8,128)S(1)}, f32[192,512]{1,0:T(8,128)S(1)}, u32[]{:S(2)}, u32[]{:S(2)}) collective-permute-start(f32[192,512]{1,0:T(8,128)S(1)} %get-tuple-element.25), channel_id=1, source_target_pairs={{16,32},{48,64},{80,96},{112,128},{144,160},{176,192},{208,224},{2... | collective-permute-start | bytes 1179656 | tf_op jit(solution)/shard_map/ppermute | solution.py:387
  22.8 1.9 %collective-permute-start.3 = (f32[192,512]{1,0:T(8,128)S(1)}, f32[192,512]{1,0:T(8,128)S(1)}, u32[]{:S(2)}, u32[]{:S(2)}) collective-permute-start(f32[192,512]{1,0:T(8,128)S(1)} %get-tuple-element.26), channel_id=1, source_target_pairs={{0,16},{16,0},{32,48},{48,32},{64,80},{80,64},{96,112},{112,96},{1... | collective-permute-start | bytes 1179656 | tf_op jit(solution)/shard_map/ppermute | solution.py:388
  24.8 3.5 %collective-permute-done.2 = f32[192,512]{1,0:T(8,128)S(1)} collective-permute-done((f32[192,512]{1,0:T(8,128)S(1)}, f32[192,512]{1,0:T(8,128)S(1)}, u32[]{:S(2)}, u32[]{:S(2)}) %collective-permute-start.2) | collective-permute-done | bytes 393248 | tf_op jit(solution)/shard_map/ppermute | solution.py:387
  28.3 0.0 collective-permute-done.3
  28.3 4.4 %shard_map.52 = (f32[8,8,512]{2,1,0:T(8,128)}, f32[4,16,256]{2,1,0:T(8,128)S(1)}, f32[4,16,256]{2,1,0:T(8,128)S(1)}, f32[6,16,256]{2,1,0:T(8,128)S(1)}, f32[6,16,256]{2,1,0:T(8,128)S(1)}) custom-call(f32[8,24,512]{2,1,0:T(8,128)S(1)} %bitcast.16, f32[8,24,512]{2,1,0:T(8,128)S(1)} %bitcast.17, f32[8,24,512]{2,1,0:T(8,128)S(1)} %bitcast.18, ...), custom_call_target="tpu_custom_call" | custom-call | tf_op jit(solution)/shard_map/pallas_call | solution.py:400
  32.7 3.6 %collective-permute-start.4 = (f32[6,16,256]{2,1,0:T(8,128)S(1)}, f32[6,16,256]{2,1,0:T(8,128)S(1)}, u32[]{:S(2)}, u32[]{:S(2)}) collective-permute-start(f32[6,16,256]{2,1,0:T(8,128)S(1)} %get-tuple-element.30), channel_id=1, source_target_pairs={{16,32},{48,64},{80,96},{112,128},{144,160},{176,192},{208,224},{2... | collective-permute-start | bytes 294920 | tf_op jit(solution)/shard_map/ppermute | solution.py:387
  36.3 1.9 %collective-permute-start.5 = (f32[6,16,256]{2,1,0:T(8,128)S(1)}, f32[6,16,256]{2,1,0:T(8,128)S(1)}, u32[]{:S(2)}, u32[]{:S(2)}) collective-permute-start(f32[6,16,256]{2,1,0:T(8,128)S(1)} %get-tuple-element.31), channel_id=1, source_target_pairs={{0,16},{16,0},{32,48},{48,32},{64,80},{80,64},{96,112},{112,96},{1... | collective-permute-start | bytes 294920 | tf_op jit(solution)/shard_map/ppermute | solution.py:388
  38.3 0.4 collective-permute-done.4.other
  38.6 0.9 collective-permute-done.5.mate
  39.5 0.6 shard_map.53
  40.1 26.5 %all_to_all.10 = f32[16,16,128]{2,1,0:T(8,128)S(1)} all-to-all(f32[16,16,128]{2,1,0:T(8,128)S(1)} %get-tuple-element.32), channel_id=1, replica_groups=mesh['gx'=32,'gy'=16] {'gy'}, dimensions={0} | all-to-all | bytes 262144 | tf_op jit(solution)/shard_map/all_to_all | solution.py:408
  66.7 0.2 shard_map.54
  66.9 5.7 %collective-permute-start.7 = (f32[128,128]{1,0:T(8,128)S(1)}, f32[128,128]{1,0:T(8,128)S(1)}, u32[]{:S(2)}, u32[]{:S(2)}) collective-permute-start(f32[128,128]{1,0:T(8,128)S(1)} %get-tuple-element.33.sd), channel_id=1, source_target_pairs={{16,32},{48,64},{80,96},{112,128},{144,160},{176,192},{208,224},{2... | collective-permute-start | bytes 196616 | tf_op jit(solution)/shard_map/ppermute | solution.py:387
  72.6 1.9 %collective-permute-start.6 = (f32[128,128]{1,0:T(8,128)S(1)}, f32[128,128]{1,0:T(8,128)S(1)}, u32[]{:S(2)}, u32[]{:S(2)}) collective-permute-start(f32[128,128]{1,0:T(8,128)S(1)} %get-tuple-element.33.sd), channel_id=1, source_target_pairs={{0,16},{16,0},{32,48},{48,32},{64,80},{80,64},{96,112},{112,96},{1... | collective-permute-start | bytes 196616 | tf_op jit(solution)/shard_map/ppermute | solution.py:388
  74.5 0.0 collective-permute-done.7.other
  74.5 1.2 %collective-permute-done.6.mate = f32[128,128]{1,0:T(8,128)S(1)} collective-permute-done((f32[128,128]{1,0:T(8,128)S(1)}, f32[128,128]{1,0:T(8,128)S(1)}, u32[]{:S(2)}, u32[]{:S(2)}) %collective-permute-start.6) | collective-permute-done | bytes 65568 | tf_op jit(solution)/shard_map/ppermute | solution.py:388
  75.7 0.4 shard_map.55
  76.1 18.2 %all_to_all.11.gathered = f32[32,16,128]{2,1,0:T(8,128)S(1)} all-to-all(f32[32,16,128]{2,1,0:T(8,128)S(1)} %get-tuple-element.35), channel_id=1, replica_groups=mesh['gx'=32,'gy'=16] {'gx'}, dimensions={0} | all-to-all | bytes 524288 | tf_op jit(solution)/shard_map/all_to_all | solution.py:412
  94.4 3.5 %shard_map.56 = f32[4,4,256]{2,1,0:T(4,128)} custom-call(f32[32,16,128]{2,1,0:T(8,128)S(1)} %all_to_all.11.gathered, f32[64,128]{1,0:T(8,128)S(1)} %get-tuple-element.36.elow, f32[4,4,256]{2,1,0:T(4,128)S(1)} %get-tuple-element.37.emid), custom_call_target="tpu_custom_call" | custom-call | tf_op jit(solution)/shard_map/pallas_call | solution.py:413
Async XLA Ops:
  0.6 14.6 %copy-start = (f32[8,8,512]{2,1,0:T(8,128)S(1)}, f32[8,8,512]{2,1,0:T(8,128)}, u32[]{:S(2)}) copy-start(f32[8,8,512]{2,1,0:T(8,128)} %param.3) | copy-start | bytes 393220
  0.6 14.6 %copy-start.1 = (f32[8,8,512]{2,1,0:T(8,128)S(1)}, f32[8,8,512]{2,1,0:T(8,128)}, u32[]{:S(2)}) copy-start(f32[8,8,512]{2,1,0:T(8,128)} %param.4) | copy-start | bytes 393220
  0.6 14.6 %copy-start.2 = (f32[8,8,512]{2,1,0:T(8,128)S(1)}, f32[8,8,512]{2,1,0:T(8,128)}, u32[]{:S(2)}) copy-start(f32[8,8,512]{2,1,0:T(8,128)} %param.5) | copy-start | bytes 393220
  2.6 8.7 %collective-permute-start = (f32[160,512]{1,0:T(8,128)}, f32[160,512]{1,0:T(8,128)S(1)}, u32[]{:S(2)}, u32[]{:S(2)}) collective-permute-start(f32[160,512]{1,0:T(8,128)} %get-tuple-element.20), channel_id=1, source_target_pairs={{0,1},{1,2},{2,3},{3,4},{4,5},{5,6},{6,7},{7,8},{8,9},{9,10},{10,1... | collective-permute-start | bytes 983048 | tf_op jit(solution)/shard_map/ppermute | solution.py:381
  7.0 8.2 %collective-permute-start.1 = (f32[160,512]{1,0:T(8,128)}, f32[160,512]{1,0:T(8,128)S(1)}, u32[]{:S(2)}, u32[]{:S(2)}) collective-permute-start(f32[160,512]{1,0:T(8,128)} %get-tuple-element.21), channel_id=1, source_target_pairs={{1,0},{2,1},{3,2},{4,3},{5,4},{6,5},{7,6},{8,7},{9,8},{10,9},{11,1... | collective-permute-start | bytes 983048 | tf_op jit(solution)/shard_map/ppermute | solution.py:381
  15.6 12.7 %collective-permute-start.2 = (f32[192,512]{1,0:T(8,128)S(1)}, f32[192,512]{1,0:T(8,128)S(1)}, u32[]{:S(2)}, u32[]{:S(2)}) collective-permute-start(f32[192,512]{1,0:T(8,128)S(1)} %get-tuple-element.25), channel_id=1, source_target_pairs={{16,32},{48,64},{80,96},{112,128},{144,160},{176,192},{208,224},{2... | collective-permute-start | bytes 1179656 | tf_op jit(solution)/shard_map/ppermute | solution.py:387
  22.8 5.4 %collective-permute-start.3 = (f32[192,512]{1,0:T(8,128)S(1)}, f32[192,512]{1,0:T(8,128)S(1)}, u32[]{:S(2)}, u32[]{:S(2)}) collective-permute-start(f32[192,512]{1,0:T(8,128)S(1)} %get-tuple-element.26), channel_id=1, source_target_pairs={{0,16},{16,0},{32,48},{48,32},{64,80},{80,64},{96,112},{112,96},{1... | collective-permute-start | bytes 1179656 | tf_op jit(solution)/shard_map/ppermute | solution.py:388
  32.7 5.9 %collective-permute-start.4 = (f32[6,16,256]{2,1,0:T(8,128)S(1)}, f32[6,16,256]{2,1,0:T(8,128)S(1)}, u32[]{:S(2)}, u32[]{:S(2)}) collective-permute-start(f32[6,16,256]{2,1,0:T(8,128)S(1)} %get-tuple-element.30), channel_id=1, source_target_pairs={{16,32},{48,64},{80,96},{112,128},{144,160},{176,192},{208,224},{2... | collective-permute-start | bytes 294920 | tf_op jit(solution)/shard_map/ppermute | solution.py:387
  36.3 3.2 %collective-permute-start.5 = (f32[6,16,256]{2,1,0:T(8,128)S(1)}, f32[6,16,256]{2,1,0:T(8,128)S(1)}, u32[]{:S(2)}, u32[]{:S(2)}) collective-permute-start(f32[6,16,256]{2,1,0:T(8,128)S(1)} %get-tuple-element.31), channel_id=1, source_target_pairs={{0,16},{16,0},{32,48},{48,32},{64,80},{80,64},{96,112},{112,96},{1... | collective-permute-start | bytes 294920 | tf_op jit(solution)/shard_map/ppermute | solution.py:388
  66.9 7.6 %collective-permute-start.7 = (f32[128,128]{1,0:T(8,128)S(1)}, f32[128,128]{1,0:T(8,128)S(1)}, u32[]{:S(2)}, u32[]{:S(2)}) collective-permute-start(f32[128,128]{1,0:T(8,128)S(1)} %get-tuple-element.33.sd), channel_id=1, source_target_pairs={{16,32},{48,64},{80,96},{112,128},{144,160},{176,192},{208,224},{2... | collective-permute-start | bytes 196616 | tf_op jit(solution)/shard_map/ppermute | solution.py:387
  72.6 3.1 %collective-permute-start.6 = (f32[128,128]{1,0:T(8,128)S(1)}, f32[128,128]{1,0:T(8,128)S(1)}, u32[]{:S(2)}, u32[]{:S(2)}) collective-permute-start(f32[128,128]{1,0:T(8,128)S(1)} %get-tuple-element.33.sd), channel_id=1, source_target_pairs={{0,16},{16,0},{32,48},{48,32},{64,80},{80,64},{96,112},{112,96},{1... | collective-permute-start | bytes 196616 | tf_op jit(solution)/shard_map/ppermute | solution.py:388

commit v4 on v3

v4 whole, which is shorter than its diff:
```python
import jax
import jax.numpy as jnp
from jax import lax
from jax.experimental import pallas as pl
from jax.experimental.pallas import tpu as pltpu
from jax.sharding import PartitionSpec as P

BOTTOM = 6
RELAX_WEIGHT = 0.8
FLOOR = 1e-3
F32 = jnp.float32
VMEM = pl.BlockSpec(memory_space=pltpu.VMEM)
HBM = pl.BlockSpec(memory_space=pltpu.HBM)


def call(kernel, out_shapes, scratch=(), n_in=0, copies=0, in_hbm=0, out_hbm=0, limit=24 * 1024 * 1024, cost=None):
    semaphores = [pltpu.SemaphoreType.DMA((copies,))] if copies else []
    return pl.pallas_call(
        kernel,
        out_shape=[jax.ShapeDtypeStruct(s, F32) for s in out_shapes],
        in_specs=[HBM] * in_hbm + [VMEM] * (n_in - in_hbm),
        out_specs=[HBM] * out_hbm + [VMEM] * (len(out_shapes) - out_hbm),
        scratch_shapes=[pltpu.VMEM(s, F32) for s in scratch] + semaphores,
        compiler_params=pltpu.CompilerParams(vmem_limit_bytes=limit),
        cost_estimate=cost,
    )


def harmonic(a, b):
    return 2.0 * a * b / jnp.maximum(a + b, FLOOR)


def along(v, axis, step):
    n = v.shape[axis]
    return pltpu.roll(v, (-step) % n, axis)


def is_first():
    return lax.rem(lax.axis_index("gx"), 2) == 0


def positions(shape, axis):
    return lax.broadcasted_iota(jnp.int32, shape, axis)


def halving(rows, cols):
    return (positions((rows, cols), 0) // 2 == positions((rows, cols), 1)).astype(F32)


def doubling(rows, cols, factor):
    return (positions((rows, cols), 1) // factor == positions((rows, cols), 0)).astype(F32)


def matmul(a, b):
    return jnp.dot(a, b, precision=lax.Precision.HIGHEST, preferred_element_type=F32)


def weight(face, centre):
    return jnp.where(face > 0.0, face, centre)


def diagonal_of(c, xp, xm, hy, hz):
    return (weight(xp, c) + weight(xm, c) + weight(hy, c) + weight(along(hy, 0, -1), c)
            + weight(hz, c) + weight(along(hz, 1, -1), c))


def operate(d, v, xp, vp, xm, vm, hy, hz):
    out = d * v - xp * vp - xm * vm
    out = out - hy * along(v, 0, 1) - along(hy * v, 0, -1)
    return out - hz * along(v, 1, 1) - along(hz * v, 1, -1)


def z_face(c):
    nxt = jnp.where(positions(c.shape, 1) < c.shape[1] - 1, along(c, 1, 1), 0.0)
    return harmonic(c, nxt)


NP, NR, NC = 7, 6, 7
NROWS = NP + NR + NC
PHI_TILES = (3, 3, 2, 2, 2, 2, 1)
RHS_TILES = (3, 2, 2, 2, 2, 1)
END_ROWS = 8 * (2 * sum(PHI_TILES) + sum(RHS_TILES))


def pack_y(phi_in, rhs_in, coef_in, near, far, phi, rhs, coef, stage, ends, sem):
    loads = [pltpu.make_async_copy(src, dst, sem.at[a])
             for a, (src, dst) in enumerate(((phi_in, phi), (rhs_in, rhs), (coef_in, coef)))]
    for load in loads:
        load.start()
    stores = []
    k = 0
    for a, (ref, n) in enumerate(((phi, NP), (rhs, NR), (coef, NC))):
        loads[a].wait()
        for q in range(4):
            lanes = slice(128 * q, 128 * q + 128)
            base = 64 * (4 * a + q)
            stage[base:base + 64, :] = ref[:, lanes]
            for j in range(n):
                rows = slice(8 * (k + j), 8 * (k + j) + 8)
                ends[0, rows, lanes] = stage[pl.ds(base + 8 - n + j, 8, stride=8), :]
                ends[1, rows, lanes] = stage[pl.ds(base + j, 8, stride=8), :]
        for b, dst in enumerate((near, far)):
            part = pl.ds(8 * k, 8 * n)
            src = ends.at[lax.rem(lax.axis_index("gy") + b, 2), part]
            stores.append(pltpu.make_async_copy(src, dst.at[part], sem.at[3 + 2 * a + b]))
            stores[-1].start()
        k += n
    for store in stores:
        store.wait()


def pack_x(phi, rhs, coef, far, near, pe, re, ce, mate, other, stage):
    zero = jnp.zeros((8, 128), F32)
    odd = lax.rem(lax.axis_index("gy"), 2)
    k = 0
    for a, (ref, ext, n) in enumerate(((phi, pe, NP), (rhs, re, NR), (coef, ce, NC))):
        for x in range(8):
            ext[24 * x:24 * x + 8, :] = ref[8 * x:8 * x + 8, :]
        for q in range(4):
            lanes = slice(128 * q, 128 * q + 128)
            base = 128 * (4 * a + q)
            for j in range(n):
                rows = slice(8 * (k + j), 8 * (k + j) + 8)
                stage[pl.ds(base + j + odd * (16 - n), 8, stride=16), :] = near[rows, lanes]
                stage[pl.ds(base + j + (1 - odd) * (16 - n), 8, stride=16), :] = far[rows, lanes]
            for j in range(n, 16 - n):
                stage[pl.ds(base + j, 8, stride=16), :] = zero
            for x in range(8):
                ext[24 * x + 8:24 * x + 24, lanes] = stage[base + 16 * x:base + 16 * x + 16, :]
        k += n
    first = is_first()
    top = positions((8, 512), 0) < 4
    for ref, end in ((mate, first), (other, jnp.logical_not(first))):
        row = 0
        for ext, tiles in ((pe, PHI_TILES), (re, RHS_TILES), (ce, PHI_TILES)):
            for k, n in enumerate(tiles):
                at = 24 * jnp.where(end, 7 - k, k)
                parts = [ext[pl.ds(pl.multiple_of(at + 8 * t, 8), 8), :] for t in range(min(n + n // 2, 3))]
                if n == 2:
                    parts = [parts[0], jnp.where(top, parts[1], parts[2])]
                for part in parts:
                    ref[row:row + 8, :] = part
                    row += 8


def slab_x(side, t):
    return jnp.where(side == 0, 3 - t, 4 + t)


def first_weights(c, xp, xm):
    hy = harmonic(c, along(c, 0, 1))
    hz = z_face(c)
    d = weight(xm, c) + weight(hy, c) + weight(along(hy, 0, -1), c) + weight(hz, c) + weight(along(hz, 1, -1), c)
    return hy, hz, d if xp is None else d + weight(xp, c)


def inverse(d):
    return RELAX_WEIGHT / jnp.maximum(d, FLOOR)


def pair_sums(sums, place, a, b, scale):
    t = a + b
    t = (t + along(t, 0, 1)) * scale
    for q in range(4):
        sums[q, place] = t[:, 128 * q:128 * q + 128]


def halve_fine(sums, packed, n):
    for k in range(n):
        for q in range(4):
            lanes = slice(128 * q, 128 * q + 128)
            packed[16 * k:16 * k + 8, lanes] = sums[q, k, pl.ds(0, 8, stride=2), :]
            packed[16 * k + 8:16 * k + 12, lanes] = jnp.zeros((4, 128), F32)
            packed[16 * k + 12:16 * k + 16, lanes] = sums[q, k, pl.ds(16, 4, stride=2), :]
    return matmul(packed[...], halving(512, 256)).reshape(n, 16, 256)


def inner(pe, re, ce, hx, hc, hy, hz, dg, rd, p1, p2, res, cmid, sums, packed):
    hc[0] = harmonic(ce[3], ce[4])

    def start(side, carry):
        for t in range(4):
            x = slab_x(side, t)
            c = ce[x]
            xm = hc[0] if t == 0 else hx[side, t - 1]
            xp = None
            if t < 3:
                xp = harmonic(c, ce[slab_x(side, t + 1)])
                hx[side, t] = xp
            hyt, hzt, d = first_weights(c, xp, xm)
            hy[side, t], hz[side, t], dg[side, t] = hyt, hzt, d
            if t < 3:
                r = inverse(d)
                rd[side, t] = r
                v = pe[x]
                image = operate(d, v, xp, pe[slab_x(side, t + 1)], xm, pe[slab_x(side, t - 1)], hyt, hzt)
                p1[side, t] = v + (re[x] - image) * r
        for q in range(2):
            pair_sums(sums, jnp.where(side == 0, 1 - q, 2 + q),
                      ce[slab_x(side, 2 * q)], ce[slab_x(side, 2 * q + 1)], 0.125)
        return carry

    lax.fori_loop(0, 2, start, 0)

    def image(side, t, p):
        xm, pm = (hc[0], p[1 - side, 0]) if t == 0 else (hx[side, t - 1], p[side, t - 1])
        return operate(dg[side, t], p[side, t], hx[side, t], p[side, t + 1], xm, pm, hy[side, t], hz[side, t])

    def second(side, carry):
        for t in range(2):
            p2[side, t] = p1[side, t] + (re[slab_x(side, t)] - image(side, t, p1)) * rd[side, t]
        return carry

    lax.fori_loop(0, 2, second, 0)

    def third(side, carry):
        res[side] = re[slab_x(side, 0)] - image(side, 0, p2)
        return carry

    lax.fori_loop(0, 2, third, 0)
    cmid[...] = halve_fine(sums, packed, 4)


def unpack(ref, p0, rs, c, side):
    row = 0
    for dst, tiles in ((p0, PHI_TILES), (rs, RHS_TILES), (c, PHI_TILES)):
        for k, n in enumerate(tiles):
            parts = [ref[row + 8 * t:row + 8 * t + 8, :] for t in range(n)]
            row += 8 * n
            if n == 1:
                parts += [jnp.zeros((8, 512), F32)] * 2
            if n == 2:
                parts += [parts[1]]
            for t in range(3):
                dst[side, k + 1, 8 * t:8 * t + 8, :] = parts[t]


def outer(pe, re, ce, hx, hc, hy, hz, dg, rd, p1, p2, res, other, mate, phi_out, smid, chalo,
          p0h, rsh, ch, hxh, hyh, hzh, dgh, rdh, p1h, p2h, resh, own, sums, packed, left):
    first = is_first()
    near = jnp.where(first, 1, 0)
    unpack(mate, p0h, rsh, ch, near)
    unpack(other, p0h, rsh, ch, 1 - near)

    def sweeps(side, carry):
        x0 = slab_x(side, 3)
        p0h[side, 0], rsh[side, 0], ch[side, 0] = pe[x0], re[x0], ce[x0]
        c = ch[side, 0]
        xp = harmonic(c, ch[side, 1])
        d = dg[side, 3] + weight(xp, c)
        r = inverse(d)
        hxh[side, 0], hyh[side, 0], hzh[side, 0], dgh[side, 0], rdh[side, 0] = xp, hy[side, 3], hz[side, 3], d, r
        v = p0h[side, 0]
        image = operate(d, v, xp, p0h[side, 1], hx[side, 2], pe[slab_x(side, 2)], hy[side, 3], hz[side, 3])
        p1h[side, 0] = v + (rsh[side, 0] - image) * r

        def start(j, carry):
            c = ch[side, j]
            xp, xm = harmonic(c, ch[side, j + 1]), hxh[side, j - 1]
            hyj, hzj, d = first_weights(c, xp, xm)
            r = inverse(d)
            hxh[side, j], hyh[side, j], hzh[side, j], dgh[side, j], rdh[side, j] = xp, hyj, hzj, d, r
            v = p0h[side, j]
            image = operate(d, v, xp, p0h[side, j + 1], xm, p0h[side, j - 1], hyj, hzj)
            p1h[side, j] = v + (rsh[side, j] - image) * r
            return carry

        lax.fori_loop(1, 7, start, 0)

        image = operate(dg[side, 2], p1[side, 2], hx[side, 2], p1h[side, 0], hx[side, 1], p1[side, 1],
                        hy[side, 2], hz[side, 2])
        p2h[side, 1] = p1[side, 2] + (re[slab_x(side, 2)] - image) * rd[side, 2]
        p2h[side, 0] = p2[side, 1]
        image = operate(dgh[side, 0], p1h[side, 0], hxh[side, 0], p1h[side, 1], hx[side, 2], p1[side, 2],
                        hyh[side, 0], hzh[side, 0])
        p2h[side, 2] = p1h[side, 0] + (rsh[side, 0] - image) * rdh[side, 0]

        def second(j, carry):
            v = p1h[side, j]
            image = operate(dgh[side, j], v, hxh[side, j], p1h[side, j + 1], hxh[side, j - 1], p1h[side, j - 1],
                            hyh[side, j], hzh[side, j])
            p2h[side, j + 2] = v + (rsh[side, j] - image) * rdh[side, j]
            return carry

        lax.fori_loop(1, 6, second, 0)
        for t in range(4):
            own[slab_x(side, t)] = (p2[side, t] if t < 2 else p2h[side, t - 1])[0:8, :]

        for t in (1, 2):
            image = operate(dg[side, t], p2h[side, t - 1], hx[side, t], p2h[side, t], hx[side, t - 1],
                            p2[side, 0] if t == 1 else p2h[side, 0], hy[side, t], hz[side, t])
            resh[side, t - 1] = re[slab_x(side, t)] - image
        image = operate(dgh[side, 0], p2h[side, 2], hxh[side, 0], p2h[side, 3], hx[side, 2], p2h[side, 1],
                        hyh[side, 0], hzh[side, 0])
        resh[side, 2] = rsh[side, 0] - image

        def third(j, carry):
            image = operate(dgh[side, j], p2h[side, j + 2], hxh[side, j], p2h[side, j + 3], hxh[side, j - 1],
                            p2h[side, j + 1], hyh[side, j], hzh[side, j])
            resh[side, j + 2] = rsh[side, j] - image
            return carry

        lax.fori_loop(1, 5, third, 0)
        for q in range(4):
            a = res[side] if q == 0 else resh[side, 2 * q - 1]
            pair_sums(sums, jnp.where(side == 0, 3 - q, 4 + q), a, resh[side, 2 * q], 0.5)
        for q in range(3):
            pair_sums(sums, 8 + jnp.where(side == 0, 2 - q, 3 + q), ch[side, 2 * q + 1], ch[side, 2 * q + 2], 0.125)
        return carry

    lax.fori_loop(0, 2, sweeps, 0)
    store = pltpu.make_async_copy(own, phi_out, left.at[0])
    store.start()
    mid = halve_fine(sums, packed, 14)
    smid[...] = mid[0:8]
    chalo[...] = mid[8:14]
    store.wait()


def middle(smid, cmid, chalo, emid, out, sums):
    s = [smid[j] for j in range(8)]
    c = [chalo[j] for j in range(3)] + [cmid[j] for j in range(4)] + [chalo[j] for j in range(3, 6)]
    hx = [harmonic(c[j], c[j + 1]) for j in range(9)]
    hy, hz, d, r, e1 = [], [], [], [], []
    for i in range(8):
        ci = c[i + 1]
        hy.append(harmonic(ci, along(ci, 0, 1)))
        hz.append(z_face(ci))
        d.append(diagonal_of(ci, hx[i + 1], hx[i], hy[i], hz[i]))
        r.append(RELAX_WEIGHT / jnp.maximum(d[i], FLOOR))
        e1.append(s[i] * r[i])

    def image(i, e):
        return operate(d[i], e[i], hx[i + 1], e[i + 1], hx[i], e[i - 1], hy[i], hz[i])

    e2 = [None] + [e1[i] + (s[i] - image(i, e1)) * r[i] for i in range(1, 7)] + [None]
    res = [s[i] - image(i, e2) for i in range(2, 6)]
    for x in range(4):
        emid[x] = e2[2 + x][0:4, :]
    groups = [(res[2 * x] + res[2 * x + 1]) * 0.5 for x in range(2)]
    groups += [(c[2 * x + 1] + c[2 * x + 2]) * 0.125 for x in range(4)]
    groups += groups[0:2]
    for g in range(8):
        both = (groups[g] + along(groups[g], 0, 1))[0:8, :]
        sums[8 * g:8 * g + 8, :] = both[:, 0:128]
        sums[64 + 8 * g:72 + 8 * g, :] = both[:, 128:256]

    def rows(y):
        return jnp.concatenate([sums[pl.ds(64 * q + 2 * y, 8, stride=8), :] for q in range(2)], axis=1)

    low0 = matmul(rows(0), halving(256, 128))
    low1 = matmul(rows(1), halving(256, 128))
    for n in range(16):
        out[n, 0:8, :] = low0
        out[n, 8:16, :] = low1


def y_face(c):
    n = c.shape[0]
    return harmonic(c, jnp.where(positions(c.shape, 0) < n - 1, along(c, 0, 1), 0.0))


def columns(gathered, sdc, ccol):
    for g in range(6):
        for y in range(2):
            rows = gathered[pl.ds(8 * y + g, 16, stride=16), :]
            ref, k = (sdc, g) if g < 2 else (ccol, g - 2)
            ref[pl.ds(32 * k + y, 16, stride=2), :] = rows
    c = [ccol[32 * j:32 * j + 32, :] for j in range(4)]
    hx = [harmonic(c[j], c[j + 1]) for j in range(3)]
    for x in range(2):
        ci = c[1 + x]
        sdc[64 + 32 * x:96 + 32 * x, :] = diagonal_of(ci, hx[x + 1], hx[x], y_face(ci), z_face(ci))
        sdc[128 + 32 * x:160 + 32 * x, :] = ci


def low(sdc, mate, other, elow, out, sums):
    first = is_first()
    hi = jnp.where(first, mate[...], other[...])
    lo = jnp.where(first, other[...], mate[...])

    def part(ref, k):
        return ref[32 * k:32 * k + 32, :]

    s, d, c = ([part(ref, k + j) for ref in (lo, sdc, hi) for j in (0, 1)] for k in (0, 2, 4))
    hx = [harmonic(c[j], c[j + 1]) for j in range(5)]
    hy = [y_face(ci) for ci in c]
    hz = [z_face(ci) for ci in c]
    r = [RELAX_WEIGHT / jnp.maximum(di, FLOOR) for di in d]
    e1 = [s[i] * r[i] for i in range(6)]

    def image(i, e):
        return operate(d[i], e[i], hx[i], e[i + 1], hx[i - 1], e[i - 1], hy[i], hz[i])

    e2 = [None] + [e1[i] + (s[i] - image(i, e1)) * r[i] for i in range(1, 5)] + [None]
    res = [s[i] - image(i, e2) for i in range(2, 4)]
    for x in range(2):
        elow[32 * x:32 * x + 32, :] = e2[2 + x]
    a = (res[0] + res[1]) * 0.5
    b = (c[2] + c[3]) * 0.125
    sums[0:32, :] = a + along(a, 0, 1)
    sums[32:64, :] = b + along(b, 0, 1)
    ra = sums[pl.ds(0, 16, stride=2), :]
    rb = sums[pl.ds(32, 16, stride=2), :]
    both = matmul(jnp.concatenate([ra, rb], axis=1), halving(256, 128))
    for n in range(32):
        out[n] = both


def bottom(gathered, elow, emid, out, hx, hy, hz, dg, sol, res, dire, img):
    half = positions((16, 128), 1) < 64
    last_z = positions((16, 128), 1) % 64 == 63
    last_y = positions((16, 128), 0) == 15
    c = []
    for x in range(16):
        a, b = gathered[x], gathered[x + 16]
        source = jnp.where(half, a, along(b, 1, 64))
        c.append(jnp.where(half, along(a, 1, 64), b))
        res[x] = source
        dire[x] = source
        sol[x] = jnp.zeros((16, 128), F32)
    for x in range(16):
        nxt = c[x + 1] if x < 15 else jnp.where(half, along(c[0], 1, 64), 0.0)
        hx[x + 1] = harmonic(c[x], nxt)
    hx[0] = along(hx[16], 1, 64)
    for x in range(16):
        hy[x] = harmonic(c[x], jnp.where(last_y, 0.0, along(c[x], 0, 1)))
        hz[x] = harmonic(c[x], jnp.where(last_z, 0.0, along(c[x], 1, 1)))
        dg[x] = diagonal_of(c[x], hx[x + 1], hx[x], hy[x], hz[x])

    def total(acc):
        return jnp.sum(acc, axis=(0, 1), keepdims=True)

    def dot_image():
        acc = jnp.zeros((16, 128), F32)
        for x in range(16):
            v = dire[x]
            vp = dire[x + 1] if x < 15 else along(dire[0], 1, 64)
            vm = dire[x - 1] if x > 0 else along(dire[15], 1, 64)
            image = operate(dg[x], v, hx[x + 1], vp, hx[x], vm, hy[x], hz[x])
            img[x] = image
            acc = acc + v * image
        return total(acc)

    def norm():
        acc = jnp.zeros((16, 128), F32)
        for x in range(16):
            acc = acc + res[x] * res[x]
        return total(acc)

    def step(_, rr):
        alpha = rr / dot_image()
        acc = jnp.zeros((16, 128), F32)
        for x in range(16):
            sol[x] = sol[x] + alpha * dire[x]
            rx = res[x] - alpha * img[x]
            res[x] = rx
            acc = acc + rx * rx
        new = total(acc)
        beta = new / rr
        for x in range(16):
            dire[x] = res[x] + beta * dire[x]
        return new

    rr = lax.fori_loop(0, BOTTOM - 1, step, norm())
    gx, gy = lax.axis_index("gx"), lax.axis_index("gy")
    xi = lax.rem(gx, 16)
    alpha = rr / dot_image()
    mine = sol[xi] + alpha * dire[xi]
    mine = jnp.where(gx >= 16, along(mine, 1, 64), mine)
    row = positions((16, 128), 0)
    mine = jnp.sum(jnp.where(row == gy, mine, 0.0), axis=0, keepdims=True)
    row = positions((32, 128), 0)
    lows = []
    for x in range(2):
        e = elow[32 * x:32 * x + 32, :]
        for y in range(2):
            lows.append(jnp.sum(jnp.where(row == 2 * gy + y, e, 0.0), axis=0, keepdims=True))
    coarse = matmul(jnp.broadcast_to(mine, (8, 128)), doubling(128, 256, 4))
    finer = matmul(jnp.concatenate(lows + lows, axis=0), doubling(128, 256, 2))
    for x in range(4):
        k = 2 * (x // 2)
        for y in range(4):
            add = finer[k + y // 2:k + y // 2 + 1, :] + coarse[0:1, :]
            out[x, y:y + 1, :] = emid[x, y:y + 1, :] + add


def swaps(near, far, axis):
    n = lax.axis_size(axis)
    pairs = [(i, i + 1) for i in range(1, n - 1, 2)] + [(i + 1, i) for i in range(1, n - 1, 2)]
    far = lax.ppermute(far, axis, pairs)
    return lax.ppermute(near, axis, [(i, i ^ 1) for i in range(n)]), far


def shards(phi_start, right_side, coefficient):
    own = [a.reshape(64, 512) for a in (phi_start, right_side, coefficient)]
    near, far = call(
        pack_y, [(8 * NROWS, 512)] * 2, [(64, 512)] * 3 + [(768, 128), (2, 8 * NROWS, 512)],
        n_in=3, copies=9, in_hbm=3, out_hbm=2, limit=64000000)(*own)
    near, far = swaps(near, far, "gy")
    *ext, mate, other = call(pack_x, [(192, 512)] * 3 + [(END_ROWS, 512)] * 2, [(1536, 128)], n_in=5)(*own, far, near)
    mate, other = swaps(mate, other, "gx")
    ext = [a.reshape(8, 24, 512) for a in ext]

    def slabs(*n):
        return (*n, 24, 512)

    *inside, cmid = call(
        inner,
        [slabs(2, 3), slabs(1)] + [slabs(2, 4)] * 3 + [slabs(2, 3)] * 2 + [slabs(2, 2), slabs(2), (4, 16, 256)],
        [(4, 4, 24, 128), (64, 512)], n_in=3,
        cost=pl.CostEstimate(flops=16_000_000, bytes_accessed=4_000_000, transcendentals=0),
    )(*ext)
    phi_fine, smid, chalo = call(
        outer,
        [(8, 8, 512), (8, 16, 256), (6, 16, 256)],
        [slabs(2, 8)] * 11 + [(8, 8, 512), (4, 14, 24, 128), (224, 512)],
        n_in=14, copies=1, out_hbm=1,
    )(*ext, *inside, other, mate)
    emid, spread = call(middle, [(4, 4, 256), (16, 16, 128)], [(128, 128)], n_in=3)(smid, cmid, chalo)
    gathered = lax.all_to_all(spread, "gy", 0, 0, tiled=True)
    (sdc,) = call(columns, [(192, 128)], [(128, 128)], n_in=1)(gathered.reshape(256, 128))
    mate, other = swaps(sdc, sdc, "gx")
    elow, spread = call(low, [(64, 128), (32, 16, 128)], [(64, 128)], n_in=3)(sdc, mate, other)
    gathered = lax.all_to_all(spread, "gx", 0, 0, tiled=True)
    (correction,) = call(bottom, [(4, 4, 256)], [(17, 16, 128)] + [(16, 16, 128)] * 7, n_in=3)(
        gathered, elow, emid)
    return phi_fine, correction


def solution(mesh):
    return jax.shard_map(
        shards,
        mesh=mesh,
        in_specs=(P("gx", "gy", None),) * 3,
        out_specs=(P("gx", "gy", None),) * 2,
        check_vma=False,
    )
```

time: 98.3 us -> 93.5 us (0.951)
  starting transfers between devices: 28 us -> 24.1 us
  blocking collectives: 44.8 us -> 41.5 us
  Pallas kernels: 11.5 us -> 14.5 us
    ppermute x8 -> x6, starting transfers between devices: 28 us -> 24.1 us  [the longest x3 13 us: swaps(): far = lax.ppermute(far, axis, pairs)]
    pallas_call x6 -> x7, Pallas kernels: 7.94 us -> 11 us  [the longest x1 5.69 us: shards(): call(outer, [(8, 8, 512), (8, 16, 256), (6, 16, 256)], [slabs(2, 8)] * 11...]
    all_to_all x1, blocking collectives: 18.2 us -> 16.2 us  [shards(): gathered = lax.all_to_all(spread, 'gx', 0, 0, tiled=True)]
    all_to_all x1, blocking collectives: 26.5 us -> 25.4 us  [shards(): gathered = lax.all_to_all(spread, 'gy', 0, 0, tiled=True)]
    ppermute x8 -> x6, waiting for transfers between devices: 12.9 us -> 12.2 us  [the longest x3 6.91 us: swaps(): return (lax.ppermute(near, axis, [(i, i ^ 1) for i in range(n)]), far)]
  transfers between devices with their start and end apart: 8 -> 6, of which waited for: 6 -> 4; matrix products, arithmetic and copies ran while one was open for 0% -> 0% of each run, Pallas kernels for 0% -> 2%
where the time goes in v4:
time: 93.5 us; the launch traced here: 93.2 us
  blocking collectives  41.5 us (44%)
  starting transfers between devices  24.1 us (26%)
  Pallas kernels  14.5 us (16%)
  waiting for transfers between devices  12.2 us (13%)
    all_to_all x1, blocking collectives, shards(): gathered = lax.all_to_all(spread, 'gy', 0, 0, tiled=True)  25.4 us
    all_to_all x1, blocking collectives, shards(): gathered = lax.all_to_all(spread, 'gx', 0, 0, tiled=True)  16.2 us
    ppermute x3, starting transfers between devices, swaps(): far = lax.ppermute(far, axis, pairs)  13 us
    ppermute x3, starting transfers between devices, swaps(): return (lax.ppermute(near, axis, [(i, i ^ 1) for i in range(n)]), far)  11.1 us
    ppermute x3, waiting for transfers between devices, swaps(): return (lax.ppermute(near, axis, [(i, i ^ 1) for i in range(n)]), far)  6.91 us
    pallas_call x1, Pallas kernels, shards(): call(outer, [(8, 8, 512), (8, 16, 256), (6, 16, 256)], [slabs(2, 8)] * 11...  5.69 us
    ppermute x3, waiting for transfers between devices, swaps(): far = lax.ppermute(far, axis, pairs)  5.34 us
    pallas_call x1, Pallas kernels, shards(): call(bottom, [(4, 4, 256)], [(17, 16, 128)] + [(16, 16, 128)] * 7, n_in=3)  3.54 us
  transfers between devices with their start and end apart: 6, of which 4 were waited for; matrix products, arithmetic and copies ran while one was open for 0% of the time, Pallas kernels for 2%

profile of v4, /device:TPU:1, one launch (start us, length us, event | category | flops | bytes accessed | tf_op | source)
XLA Modules:
  0.0 93.2 jit_solution(1339866258609850548)
XLA Ops:
  0.6 0.0 copy-start
  0.6 0.0 copy-start.1
  0.6 0.0 copy-start.2
  0.7 1.9 %shard_map.50 = (f32[160,512]{1,0:T(8,128)}, f32[160,512]{1,0:T(8,128)}) custom-call(f32[64,512]{1,0:T(8,128)} %bitcast.14, f32[64,512]{1,0:T(8,128)} %bitcast.16, f32[64,512]{1,0:T(8,128)} %bitcast.18), custom_call_target="tpu_custom_call" | custom-call | tf_op jit(solution)/shard_map/pallas_call | solution.py:497
  2.6 0.7 collective-permute-start
  3.3 7.2 %collective-permute-start.1 = (f32[160,512]{1,0:T(8,128)}, f32[160,512]{1,0:T(8,128)S(1)}, u32[]{:S(2)}, u32[]{:S(2)}) collective-permute-start(f32[160,512]{1,0:T(8,128)} %get-tuple-element.27), channel_id=1, source_target_pairs={{0,1},{1,0},{2,3},{3,2},{4,5},{5,4},{6,7},{7,6},{8,9},{9,8},{10,11... | collective-permute-start | bytes 983048 | tf_op jit(solution)/shard_map/ppermute | solution.py:492
  10.5 0.0 collective-permute-done.far
  10.5 6.0 %collective-permute-done.1.near = f32[160,512]{1,0:T(8,128)S(1)} collective-permute-done((f32[160,512]{1,0:T(8,128)}, f32[160,512]{1,0:T(8,128)S(1)}, u32[]{:S(2)}, u32[]{:S(2)}) %collective-permute-start.1) | collective-permute-done | bytes 327712 | tf_op jit(solution)/shard_map/ppermute | solution.py:492
  16.5 0.0 copy-done
  16.5 0.0 copy-done.1
  16.5 0.0 copy-done.2
  16.5 0.5 shard_map.51
  17.0 5.9 %collective-permute-start.2 = (f32[336,512]{1,0:T(8,128)S(1)}, f32[336,512]{1,0:T(8,128)S(1)}, u32[]{:S(2)}, u32[]{:S(2)}) collective-permute-start(f32[336,512]{1,0:T(8,128)S(1)} %get-tuple-element.40), channel_id=1, source_target_pairs={{16,32},{48,64},{80,96},{112,128},{144,160},{176,192},{208,224},{2... | collective-permute-start | bytes 2064392 | tf_op jit(solution)/shard_map/ppermute | solution.py:491
  22.9 1.9 %collective-permute-start.3 = (f32[336,512]{1,0:T(8,128)S(1)}, f32[336,512]{1,0:T(8,128)S(1)}, u32[]{:S(2)}, u32[]{:S(2)}) collective-permute-start(f32[336,512]{1,0:T(8,128)S(1)} %get-tuple-element.41), channel_id=1, source_target_pairs={{0,16},{16,0},{32,48},{48,32},{64,80},{80,64},{96,112},{112,96},{1... | collective-permute-start | bytes 2064392 | tf_op jit(solution)/shard_map/ppermute | solution.py:492
  24.8 1.7 %shard_map.52 = (f32[2,3,24,512]{3,2,1,0:T(8,128)S(1)}, f32[1,24,512]{2,1,0:T(8,128)S(1)}, f32[2,4,24,512]{3,2,1,0:T(8,128)S(1)}, f32[2,4,24,512]{3,2,1,0:T(8,12...) custom-call(f32[8,24,512]{2,1,0:T(8,128)S(1)} %bitcast.7, ...), custom_call_target="tpu_custom_call" | custom-call | flops 16000000 | bytes 4000000 | tf_op jit(solution)/shard_map/pallas_call | solution.py:508
  26.5 5.0 %collective-permute-done.2.other = f32[336,512]{1,0:T(8,128)S(1)} collective-permute-done((f32[336,512]{1,0:T(8,128)S(1)}, f32[336,512]{1,0:T(8,128)S(1)}, u32[]{:S(2)}, u32[]{:S(2)}) %collective-permute-start.2) | collective-permute-done | bytes 688160 | tf_op jit(solution)/shard_map/ppermute | solution.py:491
  31.5 0.0 collective-permute-done.3.mate
  31.5 5.7 %shard_map.53 = (f32[8,8,512]{2,1,0:T(8,128)}, f32[8,16,256]{2,1,0:T(8,128)S(1)}, f32[6,16,256]{2,1,0:T(8,128)S(1)}) custom-call(f32[8,24,512]{2,1,0:T(8,128)S(1)} %bitcast.8, f32[8,24,512]{2,1,0:T(8,128)S(1)} %bitcast.10, f32[8,24,512]{2,1,0:T(8,128)S(1)} %bitcast.12, f32[2,3,24,512]{3,2,1,0:T(8,128)S(1)} %get-tuple-element.31.hx, ...), custom_call_target="tpu_custom_call" | custom-call | tf_op jit(solution)/shard_map/pallas_call | solution.py:514
  37.2 0.6 shard_map.54
  37.8 25.4 %all_to_all.10 = f32[16,16,128]{2,1,0:T(8,128)S(1)} all-to-all(f32[16,16,128]{2,1,0:T(8,128)S(1)} %get-tuple-element.46), channel_id=1, replica_groups=mesh['gx'=32,'gy'=16] {'gy'}, dimensions={0} | all-to-all | bytes 262144 | tf_op jit(solution)/shard_map/all_to_all | solution.py:521
  63.2 0.2 shard_map.55.sdc
  63.4 6.5 %collective-permute-start.5 = (f32[192,128]{1,0:T(8,128)S(1)}, f32[192,128]{1,0:T(8,128)S(1)}, u32[]{:S(2)}, u32[]{:S(2)}) collective-permute-start(f32[192,128]{1,0:T(8,128)S(1)} %shard_map.55.sdc), channel_id=1, source_target_pairs={{16,32},{48,64},{80,96},{112,128},{144,160},{176,192},{208,224},{2... | collective-permute-start | bytes 294920 | tf_op jit(solution)/shard_map/ppermute | solution.py:491
  69.8 1.9 %collective-permute-start.4 = (f32[192,128]{1,0:T(8,128)S(1)}, f32[192,128]{1,0:T(8,128)S(1)}, u32[]{:S(2)}, u32[]{:S(2)}) collective-permute-start(f32[192,128]{1,0:T(8,128)S(1)} %shard_map.55.sdc), channel_id=1, source_target_pairs={{0,16},{16,0},{32,48},{48,32},{64,80},{80,64},{96,112},{112,96},{1... | collective-permute-start | bytes 294920 | tf_op jit(solution)/shard_map/ppermute | solution.py:492
  71.7 0.4 collective-permute-done.5.other
  72.1 0.9 collective-permute-done.4.mate
  73.0 0.4 shard_map.56
  73.4 16.2 %all_to_all.11.gathered = f32[32,16,128]{2,1,0:T(8,128)S(1)} all-to-all(f32[32,16,128]{2,1,0:T(8,128)S(1)} %get-tuple-element.47), channel_id=1, replica_groups=mesh['gx'=32,'gy'=16] {'gx'}, dimensions={0} | all-to-all | bytes 524288 | tf_op jit(solution)/shard_map/all_to_all | solution.py:525
  89.6 3.5 %shard_map.57 = f32[4,4,256]{2,1,0:T(4,128)} custom-call(f32[32,16,128]{2,1,0:T(8,128)S(1)} %all_to_all.11.gathered, f32[64,128]{1,0:T(8,128)S(1)} %get-tuple-element.48.elow, f32[4,4,256]{2,1,0:T(4,128)S(1)} %get-tuple-element.49.emid), custom_call_target="tpu_custom_call" | custom-call | tf_op jit(solution)/shard_map/pallas_call | solution.py:526
Async XLA Ops:
  0.6 15.9 %copy-start = (f32[8,8,512]{2,1,0:T(8,128)S(1)}, f32[8,8,512]{2,1,0:T(8,128)}, u32[]{:S(2)}) copy-start(f32[8,8,512]{2,1,0:T(8,128)} %param.3) | copy-start | bytes 393220
  0.6 15.9 %copy-start.1 = (f32[8,8,512]{2,1,0:T(8,128)S(1)}, f32[8,8,512]{2,1,0:T(8,128)}, u32[]{:S(2)}) copy-start(f32[8,8,512]{2,1,0:T(8,128)} %param.4) | copy-start | bytes 393220
  0.6 15.9 %copy-start.2 = (f32[8,8,512]{2,1,0:T(8,128)S(1)}, f32[8,8,512]{2,1,0:T(8,128)}, u32[]{:S(2)}) copy-start(f32[8,8,512]{2,1,0:T(8,128)} %param.5) | copy-start | bytes 393220
  2.6 7.9 %collective-permute-start = (f32[160,512]{1,0:T(8,128)}, f32[160,512]{1,0:T(8,128)S(1)}, u32[]{:S(2)}, u32[]{:S(2)}) collective-permute-start(f32[160,512]{1,0:T(8,128)} %get-tuple-element.26), channel_id=1, source_target_pairs={{1,2},{3,4},{5,6},{7,8},{9,10},{11,12},{13,14},{2,1},{4,3},{6,5},{... | collective-permute-start | bytes 983048 | tf_op jit(solution)/shard_map/ppermute | solution.py:491
  3.3 13.3 %collective-permute-start.1 = (f32[160,512]{1,0:T(8,128)}, f32[160,512]{1,0:T(8,128)S(1)}, u32[]{:S(2)}, u32[]{:S(2)}) collective-permute-start(f32[160,512]{1,0:T(8,128)} %get-tuple-element.27), channel_id=1, source_target_pairs={{0,1},{1,0},{2,3},{3,2},{4,5},{5,4},{6,7},{7,6},{8,9},{9,8},{10,11... | collective-permute-start | bytes 983048 | tf_op jit(solution)/shard_map/ppermute | solution.py:492
  17.0 14.5 %collective-permute-start.2 = (f32[336,512]{1,0:T(8,128)S(1)}, f32[336,512]{1,0:T(8,128)S(1)}, u32[]{:S(2)}, u32[]{:S(2)}) collective-permute-start(f32[336,512]{1,0:T(8,128)S(1)} %get-tuple-element.40), channel_id=1, source_target_pairs={{16,32},{48,64},{80,96},{112,128},{144,160},{176,192},{208,224},{2... | collective-permute-start | bytes 2064392 | tf_op jit(solution)/shard_map/ppermute | solution.py:491
  22.9 8.6 %collective-permute-start.3 = (f32[336,512]{1,0:T(8,128)S(1)}, f32[336,512]{1,0:T(8,128)S(1)}, u32[]{:S(2)}, u32[]{:S(2)}) collective-permute-start(f32[336,512]{1,0:T(8,128)S(1)} %get-tuple-element.41), channel_id=1, source_target_pairs={{0,16},{16,0},{32,48},{48,32},{64,80},{80,64},{96,112},{112,96},{1... | collective-permute-start | bytes 2064392 | tf_op jit(solution)/shard_map/ppermute | solution.py:492
  63.4 8.7 %collective-permute-start.5 = (f32[192,128]{1,0:T(8,128)S(1)}, f32[192,128]{1,0:T(8,128)S(1)}, u32[]{:S(2)}, u32[]{:S(2)}) collective-permute-start(f32[192,128]{1,0:T(8,128)S(1)} %shard_map.55.sdc), channel_id=1, source_target_pairs={{16,32},{48,64},{80,96},{112,128},{144,160},{176,192},{208,224},{2... | collective-permute-start | bytes 294920 | tf_op jit(solution)/shard_map/ppermute | solution.py:491
  69.8 3.2 %collective-permute-start.4 = (f32[192,128]{1,0:T(8,128)S(1)}, f32[192,128]{1,0:T(8,128)S(1)}, u32[]{:S(2)}, u32[]{:S(2)}) collective-permute-start(f32[192,128]{1,0:T(8,128)S(1)} %shard_map.55.sdc), channel_id=1, source_target_pairs={{0,16},{16,0},{32,48},{48,32},{64,80},{80,64},{96,112},{112,96},{1... | collective-permute-start | bytes 294920 | tf_op jit(solution)/shard_map/ppermute | solution.py:492

commit v5 on v4

--- a/solution.py
+++ b/solution.py
@@ -26,8 +26,13 @@
     )
 
 
+def reciprocal(x):
+    r = pl.reciprocal(x, approx=True)
+    return r * (2.0 - x * r)
+
+
 def harmonic(a, b):
-    return 2.0 * a * b / jnp.maximum(a + b, FLOOR)
+    return 2.0 * a * b * reciprocal(jnp.maximum(a + b, FLOOR))
 
 
 def along(v, axis, step):
@@ -53,6 +58,15 @@
 
 def matmul(a, b):
     return jnp.dot(a, b, precision=lax.Precision.HIGHEST, preferred_element_type=F32)
+
+
+def exact_matmul(a, ones):
+    parts = []
+    for _ in range(3):
+        parts.append(a.astype(jnp.bfloat16))
+        a = a - parts[-1].astype(F32)
+    ones = ones.astype(jnp.bfloat16)
+    return sum(jnp.dot(p, ones, preferred_element_type=F32) for p in reversed(parts))
 
 
 def weight(face, centre):
@@ -155,7 +169,7 @@
 
 
 def inverse(d):
-    return RELAX_WEIGHT / jnp.maximum(d, FLOOR)
+    return RELAX_WEIGHT * reciprocal(jnp.maximum(d, FLOOR))
 
 
 def pair_sums(sums, place, a, b, scale):
@@ -172,7 +186,7 @@
             packed[16 * k:16 * k + 8, lanes] = sums[q, k, pl.ds(0, 8, stride=2), :]
             packed[16 * k + 8:16 * k + 12, lanes] = jnp.zeros((4, 128), F32)
             packed[16 * k + 12:16 * k + 16, lanes] = sums[q, k, pl.ds(16, 4, stride=2), :]
-    return matmul(packed[...], halving(512, 256)).reshape(n, 16, 256)
+    return exact_matmul(packed[...], halving(512, 256)).reshape(n, 16, 256)
 
 
 def inner(pe, re, ce, hx, hc, hy, hz, dg, rd, p1, p2, res, cmid, sums, packed):
@@ -265,7 +279,7 @@
             p1h[side, j] = v + (rsh[side, j] - image) * r
             return carry
 
-        lax.fori_loop(1, 7, start, 0)
+        lax.fori_loop(1, 7, start, 0, unroll=True)
 
         image = operate(dg[side, 2], p1[side, 2], hx[side, 2], p1h[side, 0], hx[side, 1], p1[side, 1],
                         hy[side, 2], hz[side, 2])
@@ -282,7 +296,7 @@
             p2h[side, j + 2] = v + (rsh[side, j] - image) * rdh[side, j]
             return carry
 
-        lax.fori_loop(1, 6, second, 0)
+        lax.fori_loop(1, 6, second, 0, unroll=True)
         for t in range(4):
             own[slab_x(side, t)] = (p2[side, t] if t < 2 else p2h[side, t - 1])[0:8, :]
 
@@ -300,7 +314,7 @@
             resh[side, j + 2] = rsh[side, j] - image
             return carry
 
-        lax.fori_loop(1, 5, third, 0)
+        lax.fori_loop(1, 5, third, 0, unroll=True)
         for q in range(4):
             a = res[side] if q == 0 else resh[side, 2 * q - 1]
             pair_sums(sums, jnp.where(side == 0, 3 - q, 4 + q), a, resh[side, 2 * q], 0.5)
@@ -327,7 +341,7 @@
         hy.append(harmonic(ci, along(ci, 0, 1)))
         hz.append(z_face(ci))
         d.append(diagonal_of(ci, hx[i + 1], hx[i], hy[i], hz[i]))
-        r.append(RELAX_WEIGHT / jnp.maximum(d[i], FLOOR))
+        r.append(inverse(d[i]))
         e1.append(s[i] * r[i])
 
     def image(i, e):
@@ -386,7 +400,7 @@
     hx = [harmonic(c[j], c[j + 1]) for j in range(5)]
     hy = [y_face(ci) for ci in c]
     hz = [z_face(ci) for ci in c]
-    r = [RELAX_WEIGHT / jnp.maximum(di, FLOOR) for di in d]
+    r = [inverse(di) for di in d]
     e1 = [s[i] * r[i] for i in range(6)]
 
     def image(i, e):
@@ -429,7 +443,7 @@
         dg[x] = diagonal_of(c[x], hx[x + 1], hx[x], hy[x], hz[x])
 
     def total(acc):
-        return jnp.sum(acc, axis=(0, 1), keepdims=True)
+        return jnp.sum(jnp.sum(acc, axis=0, keepdims=True), axis=1, keepdims=True)
 
     def dot_image():
         acc = jnp.zeros((16, 128), F32)

time: 93.5 us -> 91.3 us (0.976)
  Pallas kernels: 14.5 us -> 12.3 us
    pallas_call x1, Pallas kernels: 5.69 us -> 3.71 us  [shards(): call(outer, [(8, 8, 512), (8, 16, 256), (6, 16, 256)], [slabs(2, 8)] * 11...]
where the time goes in v5:
time: 91.3 us; the launch traced here: 90.9 us
  blocking collectives  41.5 us (45%)
  starting transfers between devices  24.1 us (26%)
  Pallas kernels  12.3 us (13%)
  waiting for transfers between devices  12.3 us (13%)
    all_to_all x1, blocking collectives, shards(): gathered = lax.all_to_all(spread, 'gy', 0, 0, tiled=True)  25.4 us
    all_to_all x1, blocking collectives, shards(): gathered = lax.all_to_all(spread, 'gx', 0, 0, tiled=True)  16.2 us
    ppermute x3, starting transfers between devices, swaps(): far = lax.ppermute(far, axis, pairs)  13 us
    ppermute x3, starting transfers between devices, swaps(): return (lax.ppermute(near, axis, [(i, i ^ 1) for i in range(n)]), far)  11.1 us
    ppermute x3, waiting for transfers between devices, swaps(): return (lax.ppermute(near, axis, [(i, i ^ 1) for i in range(n)]), far)  6.91 us
    ppermute x3, waiting for transfers between devices, swaps(): far = lax.ppermute(far, axis, pairs)  5.34 us
    pallas_call x1, Pallas kernels, shards(): call(outer, [(8, 8, 512), (8, 16, 256), (6, 16, 256)], [slabs(2, 8)] * 11...  3.71 us
    pallas_call x1, Pallas kernels, shards(): call(bottom, [(4, 4, 256)], [(17, 16, 128)] + [(16, 16, 128)] * 7, n_in=3)  3.23 us
  transfers between devices with their start and end apart: 6, of which 4 were waited for; matrix products, arithmetic and copies ran while one was open for 0% of the time, Pallas kernels for 2%

profile of v5, /device:TPU:1, one launch (start us, length us, event | category | flops | bytes accessed | tf_op | source)
XLA Modules:
  0.0 90.9 jit_solution(6011656615530866567)
XLA Ops:
  0.6 0.0 copy-start
  0.6 0.0 copy-start.1
  0.6 0.0 copy-start.2
  0.7 1.9 %shard_map.50 = (f32[160,512]{1,0:T(8,128)}, f32[160,512]{1,0:T(8,128)}) custom-call(f32[64,512]{1,0:T(8,128)} %bitcast.14, f32[64,512]{1,0:T(8,128)} %bitcast.16, f32[64,512]{1,0:T(8,128)} %bitcast.18), custom_call_target="tpu_custom_call" | custom-call | tf_op jit(solution)/shard_map/pallas_call | solution.py:511
  2.6 0.7 collective-permute-start
  3.3 7.2 %collective-permute-start.1 = (f32[160,512]{1,0:T(8,128)}, f32[160,512]{1,0:T(8,128)S(1)}, u32[]{:S(2)}, u32[]{:S(2)}) collective-permute-start(f32[160,512]{1,0:T(8,128)} %get-tuple-element.27), channel_id=1, source_target_pairs={{0,1},{1,0},{2,3},{3,2},{4,5},{5,4},{6,7},{7,6},{8,9},{9,8},{10,11... | collective-permute-start | bytes 983048 | tf_op jit(solution)/shard_map/ppermute | solution.py:506
  10.5 0.0 collective-permute-done.far
  10.5 6.0 %collective-permute-done.1.near = f32[160,512]{1,0:T(8,128)S(1)} collective-permute-done((f32[160,512]{1,0:T(8,128)}, f32[160,512]{1,0:T(8,128)S(1)}, u32[]{:S(2)}, u32[]{:S(2)}) %collective-permute-start.1) | collective-permute-done | bytes 327712 | tf_op jit(solution)/shard_map/ppermute | solution.py:506
  16.5 0.0 copy-done
  16.5 0.0 copy-done.1
  16.5 0.0 copy-done.2
  16.5 0.5 shard_map.51
  17.0 5.9 %collective-permute-start.2 = (f32[336,512]{1,0:T(8,128)S(1)}, f32[336,512]{1,0:T(8,128)S(1)}, u32[]{:S(2)}, u32[]{:S(2)}) collective-permute-start(f32[336,512]{1,0:T(8,128)S(1)} %get-tuple-element.40), channel_id=1, source_target_pairs={{16,32},{48,64},{80,96},{112,128},{144,160},{176,192},{208,224},{2... | collective-permute-start | bytes 2064392 | tf_op jit(solution)/shard_map/ppermute | solution.py:505
  22.9 1.9 %collective-permute-start.3 = (f32[336,512]{1,0:T(8,128)S(1)}, f32[336,512]{1,0:T(8,128)S(1)}, u32[]{:S(2)}, u32[]{:S(2)}) collective-permute-start(f32[336,512]{1,0:T(8,128)S(1)} %get-tuple-element.41), channel_id=1, source_target_pairs={{0,16},{16,0},{32,48},{48,32},{64,80},{80,64},{96,112},{112,96},{1... | collective-permute-start | bytes 2064392 | tf_op jit(solution)/shard_map/ppermute | solution.py:506
  24.8 1.7 %shard_map.52 = (f32[2,3,24,512]{3,2,1,0:T(8,128)S(1)}, f32[1,24,512]{2,1,0:T(8,128)S(1)}, f32[2,4,24,512]{3,2,1,0:T(8,128)S(1)}, f32[2,4,24,512]{3,2,1,0:T(8,12...) custom-call(f32[8,24,512]{2,1,0:T(8,128)S(1)} %bitcast.7, ...), custom_call_target="tpu_custom_call" | custom-call | flops 16000000 | bytes 4000000 | tf_op jit(solution)/shard_map/pallas_call | solution.py:522
  26.5 5.0 %collective-permute-done.2.other = f32[336,512]{1,0:T(8,128)S(1)} collective-permute-done((f32[336,512]{1,0:T(8,128)S(1)}, f32[336,512]{1,0:T(8,128)S(1)}, u32[]{:S(2)}, u32[]{:S(2)}) %collective-permute-start.2) | collective-permute-done | bytes 688160 | tf_op jit(solution)/shard_map/ppermute | solution.py:505
  31.5 0.0 collective-permute-done.3.mate
  31.5 3.7 %shard_map.53 = (f32[8,8,512]{2,1,0:T(8,128)}, f32[8,16,256]{2,1,0:T(8,128)S(1)}, f32[6,16,256]{2,1,0:T(8,128)S(1)}) custom-call(f32[8,24,512]{2,1,0:T(8,128)S(1)} %bitcast.8, f32[8,24,512]{2,1,0:T(8,128)S(1)} %bitcast.10, f32[8,24,512]{2,1,0:T(8,128)S(1)} %bitcast.12, f32[2,3,24,512]{3,2,1,0:T(8,128)S(1)} %get-tuple-element.31.hx, ...), custom_call_target="tpu_custom_call" | custom-call | tf_op jit(solution)/shard_map/pallas_call | solution.py:528
  35.2 0.7 shard_map.54
  35.9 25.4 %all_to_all.10 = f32[16,16,128]{2,1,0:T(8,128)S(1)} all-to-all(f32[16,16,128]{2,1,0:T(8,128)S(1)} %get-tuple-element.46), channel_id=1, replica_groups=mesh['gx'=32,'gy'=16] {'gy'}, dimensions={0} | all-to-all | bytes 262144 | tf_op jit(solution)/shard_map/all_to_all | solution.py:535
  61.2 0.2 shard_map.55.sdc
  61.4 6.4 %collective-permute-start.5 = (f32[192,128]{1,0:T(8,128)S(1)}, f32[192,128]{1,0:T(8,128)S(1)}, u32[]{:S(2)}, u32[]{:S(2)}) collective-permute-start(f32[192,128]{1,0:T(8,128)S(1)} %shard_map.55.sdc), channel_id=1, source_target_pairs={{16,32},{48,64},{80,96},{112,128},{144,160},{176,192},{208,224},{2... | collective-permute-start | bytes 294920 | tf_op jit(solution)/shard_map/ppermute | solution.py:505
  67.9 1.9 %collective-permute-start.4 = (f32[192,128]{1,0:T(8,128)S(1)}, f32[192,128]{1,0:T(8,128)S(1)}, u32[]{:S(2)}, u32[]{:S(2)}) collective-permute-start(f32[192,128]{1,0:T(8,128)S(1)} %shard_map.55.sdc), channel_id=1, source_target_pairs={{0,16},{16,0},{32,48},{48,32},{64,80},{80,64},{96,112},{112,96},{1... | collective-permute-start | bytes 294920 | tf_op jit(solution)/shard_map/ppermute | solution.py:506
  69.8 0.4 collective-permute-done.5.other
  70.2 0.9 collective-permute-done.4.mate
  71.1 0.4 shard_map.56
  71.5 16.2 %all_to_all.11.gathered = f32[32,16,128]{2,1,0:T(8,128)S(1)} all-to-all(f32[32,16,128]{2,1,0:T(8,128)S(1)} %get-tuple-element.47), channel_id=1, replica_groups=mesh['gx'=32,'gy'=16] {'gx'}, dimensions={0} | all-to-all | bytes 524288 | tf_op jit(solution)/shard_map/all_to_all | solution.py:539
  87.7 3.2 %shard_map.57 = f32[4,4,256]{2,1,0:T(4,128)} custom-call(f32[32,16,128]{2,1,0:T(8,128)S(1)} %all_to_all.11.gathered, f32[64,128]{1,0:T(8,128)S(1)} %get-tuple-element.48.elow, f32[4,4,256]{2,1,0:T(4,128)S(1)} %get-tuple-element.49.emid), custom_call_target="tpu_custom_call" | custom-call | tf_op jit(solution)/shard_map/pallas_call | solution.py:540
Async XLA Ops:
  0.6 15.9 %copy-start = (f32[8,8,512]{2,1,0:T(8,128)S(1)}, f32[8,8,512]{2,1,0:T(8,128)}, u32[]{:S(2)}) copy-start(f32[8,8,512]{2,1,0:T(8,128)} %param.3) | copy-start | bytes 393220
  0.6 15.9 %copy-start.1 = (f32[8,8,512]{2,1,0:T(8,128)S(1)}, f32[8,8,512]{2,1,0:T(8,128)}, u32[]{:S(2)}) copy-start(f32[8,8,512]{2,1,0:T(8,128)} %param.4) | copy-start | bytes 393220
  0.6 15.9 %copy-start.2 = (f32[8,8,512]{2,1,0:T(8,128)S(1)}, f32[8,8,512]{2,1,0:T(8,128)}, u32[]{:S(2)}) copy-start(f32[8,8,512]{2,1,0:T(8,128)} %param.5) | copy-start | bytes 393220
  2.6 7.9 %collective-permute-start = (f32[160,512]{1,0:T(8,128)}, f32[160,512]{1,0:T(8,128)S(1)}, u32[]{:S(2)}, u32[]{:S(2)}) collective-permute-start(f32[160,512]{1,0:T(8,128)} %get-tuple-element.26), channel_id=1, source_target_pairs={{1,2},{3,4},{5,6},{7,8},{9,10},{11,12},{13,14},{2,1},{4,3},{6,5},{... | collective-permute-start | bytes 983048 | tf_op jit(solution)/shard_map/ppermute | solution.py:505
  3.3 13.3 %collective-permute-start.1 = (f32[160,512]{1,0:T(8,128)}, f32[160,512]{1,0:T(8,128)S(1)}, u32[]{:S(2)}, u32[]{:S(2)}) collective-permute-start(f32[160,512]{1,0:T(8,128)} %get-tuple-element.27), channel_id=1, source_target_pairs={{0,1},{1,0},{2,3},{3,2},{4,5},{5,4},{6,7},{7,6},{8,9},{9,8},{10,11... | collective-permute-start | bytes 983048 | tf_op jit(solution)/shard_map/ppermute | solution.py:506
  17.0 14.5 %collective-permute-start.2 = (f32[336,512]{1,0:T(8,128)S(1)}, f32[336,512]{1,0:T(8,128)S(1)}, u32[]{:S(2)}, u32[]{:S(2)}) collective-permute-start(f32[336,512]{1,0:T(8,128)S(1)} %get-tuple-element.40), channel_id=1, source_target_pairs={{16,32},{48,64},{80,96},{112,128},{144,160},{176,192},{208,224},{2... | collective-permute-start | bytes 2064392 | tf_op jit(solution)/shard_map/ppermute | solution.py:505
  22.9 8.6 %collective-permute-start.3 = (f32[336,512]{1,0:T(8,128)S(1)}, f32[336,512]{1,0:T(8,128)S(1)}, u32[]{:S(2)}, u32[]{:S(2)}) collective-permute-start(f32[336,512]{1,0:T(8,128)S(1)} %get-tuple-element.41), channel_id=1, source_target_pairs={{0,16},{16,0},{32,48},{48,32},{64,80},{80,64},{96,112},{112,96},{1... | collective-permute-start | bytes 2064392 | tf_op jit(solution)/shard_map/ppermute | solution.py:506
  61.4 8.7 %collective-permute-start.5 = (f32[192,128]{1,0:T(8,128)S(1)}, f32[192,128]{1,0:T(8,128)S(1)}, u32[]{:S(2)}, u32[]{:S(2)}) collective-permute-start(f32[192,128]{1,0:T(8,128)S(1)} %shard_map.55.sdc), channel_id=1, source_target_pairs={{16,32},{48,64},{80,96},{112,128},{144,160},{176,192},{208,224},{2... | collective-permute-start | bytes 294920 | tf_op jit(solution)/shard_map/ppermute | solution.py:505
  67.9 3.2 %collective-permute-start.4 = (f32[192,128]{1,0:T(8,128)S(1)}, f32[192,128]{1,0:T(8,128)S(1)}, u32[]{:S(2)}, u32[]{:S(2)}) collective-permute-start(f32[192,128]{1,0:T(8,128)S(1)} %shard_map.55.sdc), channel_id=1, source_target_pairs={{0,16},{16,0},{32,48},{48,32},{64,80},{80,64},{96,112},{112,96},{1... | collective-permute-start | bytes 294920 | tf_op jit(solution)/shard_map/ppermute | solution.py:506

commit v6 on v5

--- a/solution.py
+++ b/solution.py
@@ -93,7 +93,8 @@
 NROWS = NP + NR + NC
 PHI_TILES = (3, 3, 2, 2, 2, 2, 1)
 RHS_TILES = (3, 2, 2, 2, 2, 1)
-END_ROWS = 8 * (2 * sum(PHI_TILES) + sum(RHS_TILES))
+COEF_TILES = (3, 3, 2, 2, 2, 2, 1, 1)
+END_ROWS = 8 * (sum(PHI_TILES) + sum(RHS_TILES) + sum(COEF_TILES))
 
 
 def pack_y(phi_in, rhs_in, coef_in, near, far, phi, rhs, coef, stage, ends, sem):
@@ -146,7 +147,7 @@
     top = positions((8, 512), 0) < 4
     for ref, end in ((mate, first), (other, jnp.logical_not(first))):
         row = 0
-        for ext, tiles in ((pe, PHI_TILES), (re, RHS_TILES), (ce, PHI_TILES)):
+        for ext, tiles in ((pe, PHI_TILES), (re, RHS_TILES), (ce, COEF_TILES)):
             for k, n in enumerate(tiles):
                 at = 24 * jnp.where(end, 7 - k, k)
                 parts = [ext[pl.ds(pl.multiple_of(at + 8 * t, 8), 8), :] for t in range(min(n + n // 2, 3))]
@@ -237,7 +238,7 @@
 
 def unpack(ref, p0, rs, c, side):
     row = 0
-    for dst, tiles in ((p0, PHI_TILES), (rs, RHS_TILES), (c, PHI_TILES)):
+    for dst, tiles in ((p0, PHI_TILES), (rs, RHS_TILES), (c, COEF_TILES)):
         for k, n in enumerate(tiles):
             parts = [ref[row + 8 * t:row + 8 * t + 8, :] for t in range(n)]
             row += 8 * n
@@ -318,26 +319,26 @@
         for q in range(4):
             a = res[side] if q == 0 else resh[side, 2 * q - 1]
             pair_sums(sums, jnp.where(side == 0, 3 - q, 4 + q), a, resh[side, 2 * q], 0.5)
-        for q in range(3):
-            pair_sums(sums, 8 + jnp.where(side == 0, 2 - q, 3 + q), ch[side, 2 * q + 1], ch[side, 2 * q + 2], 0.125)
+        for q in range(4):
+            pair_sums(sums, 8 + jnp.where(side == 0, 3 - q, 4 + q), ch[side, 2 * q + 1], ch[side, 2 * q + 2], 0.125)
         return carry
 
     lax.fori_loop(0, 2, sweeps, 0)
     store = pltpu.make_async_copy(own, phi_out, left.at[0])
     store.start()
-    mid = halve_fine(sums, packed, 14)
+    mid = halve_fine(sums, packed, 16)
     smid[...] = mid[0:8]
-    chalo[...] = mid[8:14]
+    chalo[...] = mid[8:16]
     store.wait()
 
 
 def middle(smid, cmid, chalo, emid, out, sums):
     s = [smid[j] for j in range(8)]
-    c = [chalo[j] for j in range(3)] + [cmid[j] for j in range(4)] + [chalo[j] for j in range(3, 6)]
-    hx = [harmonic(c[j], c[j + 1]) for j in range(9)]
+    c = [chalo[j] for j in range(4)] + [cmid[j] for j in range(4)] + [chalo[j] for j in range(4, 8)]
+    hx = [harmonic(c[j], c[j + 1]) for j in range(1, 10)]
     hy, hz, d, r, e1 = [], [], [], [], []
     for i in range(8):
-        ci = c[i + 1]
+        ci = c[i + 2]
         hy.append(harmonic(ci, along(ci, 0, 1)))
         hz.append(z_face(ci))
         d.append(diagonal_of(ci, hx[i + 1], hx[i], hy[i], hz[i]))
@@ -352,8 +353,7 @@
     for x in range(4):
         emid[x] = e2[2 + x][0:4, :]
     groups = [(res[2 * x] + res[2 * x + 1]) * 0.5 for x in range(2)]
-    groups += [(c[2 * x + 1] + c[2 * x + 2]) * 0.125 for x in range(4)]
-    groups += groups[0:2]
+    groups += [(c[2 * x] + c[2 * x + 1]) * 0.125 for x in range(6)]
     for g in range(8):
         both = (groups[g] + along(groups[g], 0, 1))[0:8, :]
         sums[8 * g:8 * g + 8, :] = both[:, 0:128]
@@ -374,51 +374,44 @@
     return harmonic(c, jnp.where(positions(c.shape, 0) < n - 1, along(c, 0, 1), 0.0))
 
 
-def columns(gathered, sdc, ccol):
-    for g in range(6):
+def low(gathered, elow, out, scol, ccol, sums):
+    for g in range(8):
         for y in range(2):
-            rows = gathered[pl.ds(8 * y + g, 16, stride=16), :]
-            ref, k = (sdc, g) if g < 2 else (ccol, g - 2)
-            ref[pl.ds(32 * k + y, 16, stride=2), :] = rows
-    c = [ccol[32 * j:32 * j + 32, :] for j in range(4)]
-    hx = [harmonic(c[j], c[j + 1]) for j in range(3)]
-    for x in range(2):
-        ci = c[1 + x]
-        sdc[64 + 32 * x:96 + 32 * x, :] = diagonal_of(ci, hx[x + 1], hx[x], y_face(ci), z_face(ci))
-        sdc[128 + 32 * x:160 + 32 * x, :] = ci
-
-
-def low(sdc, mate, other, elow, out, sums):
-    first = is_first()
-    hi = jnp.where(first, mate[...], other[...])
-    lo = jnp.where(first, other[...], mate[...])
-
-    def part(ref, k):
-        return ref[32 * k:32 * k + 32, :]
-
-    s, d, c = ([part(ref, k + j) for ref in (lo, sdc, hi) for j in (0, 1)] for k in (0, 2, 4))
+            ref, k = (scol, g) if g < 2 else (ccol, g - 2)
+            ref[pl.ds(32 * k + y, 16, stride=2), :] = gathered[pl.ds(8 * y + g, 16, stride=16), :]
+    c = [ccol[32 * j:32 * j + 32, :] for j in range(6)]
+    zero = jnp.zeros((32, 128), F32)
+    s = [zero, zero, scol[0:32, :], scol[32:64, :], zero, zero]
     hx = [harmonic(c[j], c[j + 1]) for j in range(5)]
-    hy = [y_face(ci) for ci in c]
-    hz = [z_face(ci) for ci in c]
-    r = [inverse(di) for di in d]
-    e1 = [s[i] * r[i] for i in range(6)]
-
-    def image(i, e):
-        return operate(d[i], e[i], hx[i], e[i + 1], hx[i - 1], e[i - 1], hy[i], hz[i])
-
-    e2 = [None] + [e1[i] + (s[i] - image(i, e1)) * r[i] for i in range(1, 5)] + [None]
-    res = [s[i] - image(i, e2) for i in range(2, 4)]
-    for x in range(2):
-        elow[32 * x:32 * x + 32, :] = e2[2 + x]
-    a = (res[0] + res[1]) * 0.5
-    b = (c[2] + c[3]) * 0.125
-    sums[0:32, :] = a + along(a, 0, 1)
-    sums[32:64, :] = b + along(b, 0, 1)
-    ra = sums[pl.ds(0, 16, stride=2), :]
-    rb = sums[pl.ds(32, 16, stride=2), :]
-    both = matmul(jnp.concatenate([ra, rb], axis=1), halving(256, 128))
+    hy, hz, d, r = [None], [None], [None], [None]
+    for j in range(1, 5):
+        hy.append(y_face(c[j]))
+        hz.append(z_face(c[j]))
+        d.append(diagonal_of(c[j], hx[j], hx[j - 1], hy[j], hz[j]))
+        r.append(inverse(d[j]))
+    e1 = [zero, zero, s[2] * r[2], s[3] * r[3], zero, zero]
+
+    def image(j, e):
+        return operate(d[j], e[j], hx[j], e[j + 1], hx[j - 1], e[j - 1], hy[j], hz[j])
+
+    e2 = [zero, hx[1] * e1[2] * r[1]]
+    e2 += [e1[j] + (s[j] - image(j, e1)) * r[j] for j in (2, 3)]
+    e2 += [hx[3] * e1[3] * r[4], zero]
+    res = [hx[0] * e2[1]] + [s[j] - image(j, e2) for j in range(1, 5)] + [hx[4] * e2[4]]
+
+    quads = [(res[2] + res[3]) * 0.5, (c[2] + c[3]) * 0.125, (res[0] + res[1]) * 0.5, (res[4] + res[5]) * 0.5]
+    for k in range(4):
+        sums[32 * k:32 * k + 32, :] = quads[k] + along(quads[k], 0, 1)
+    rows = [sums[pl.ds(32 * k, 16, stride=2), :] for k in range(4)]
+    both = matmul(jnp.concatenate([jnp.concatenate(rows[0:2], axis=1), jnp.concatenate(rows[2:4], axis=1)], axis=0),
+                  halving(256, 128))
+    row = positions((32, 128), 0) - 2 * lax.axis_index("gy")
+    errors = [jnp.sum(jnp.where(row == y, e2[j], 0.0), axis=0, keepdims=True) for j in (2, 3, 1, 4) for y in range(2)]
+    errors = jnp.concatenate(errors, axis=0)
+    elow[...] = errors
     for n in range(32):
-        out[n] = both
+        out[n, 0:32, :] = both
+        out[n, 32:40, :] = errors
 
 
 def bottom(gathered, elow, emid, out, hx, hy, hz, dg, sol, res, dire, img):
@@ -427,9 +420,13 @@
     last_y = positions((16, 128), 0) == 15
     c = []
     for x in range(16):
-        a, b = gathered[x], gathered[x + 16]
+        a, b = gathered[x, 0:16, :], gathered[x + 16, 0:16, :]
         source = jnp.where(half, a, along(b, 1, 64))
         c.append(jnp.where(half, along(a, 1, 64), b))
+        b = along(gathered[x + 17, 16:32, :], 1, 64) if x < 15 else 0.0
+        source = source + jnp.where(half, gathered[x + 1, 16:32, :], b)
+        a = along(gathered[x - 1, 16:32, :], 1, 64) if x > 0 else 0.0
+        source = source + jnp.where(half, a, gathered[x + 15, 16:32, :])
         res[x] = source
         dire[x] = source
         sol[x] = jnp.zeros((16, 128), F32)
@@ -484,14 +481,11 @@
     mine = jnp.where(gx >= 16, along(mine, 1, 64), mine)
     row = positions((16, 128), 0)
     mine = jnp.sum(jnp.where(row == gy, mine, 0.0), axis=0, keepdims=True)
-    row = positions((32, 128), 0)
-    lows = []
-    for x in range(2):
-        e = elow[32 * x:32 * x + 32, :]
-        for y in range(2):
-            lows.append(jnp.sum(jnp.where(row == 2 * gy + y, e, 0.0), axis=0, keepdims=True))
+    after = jnp.where(gx < 31, gathered[jnp.minimum(gx + 1, 31), 32:40, :], 0.0)
+    before = jnp.where(gx > 0, gathered[jnp.maximum(gx - 1, 0), 32:40, :], 0.0)
+    lows = elow[0:4, :] + jnp.concatenate([before[6:8, :], after[4:6, :]], axis=0)
     coarse = matmul(jnp.broadcast_to(mine, (8, 128)), doubling(128, 256, 4))
-    finer = matmul(jnp.concatenate(lows + lows, axis=0), doubling(128, 256, 2))
+    finer = matmul(jnp.concatenate([lows, lows], axis=0), doubling(128, 256, 2))
     for x in range(4):
         k = 2 * (x // 2)
         for y in range(4):
@@ -527,15 +521,14 @@
     )(*ext)
     phi_fine, smid, chalo = call(
         outer,
-        [(8, 8, 512), (8, 16, 256), (6, 16, 256)],
-        [slabs(2, 8)] * 11 + [(8, 8, 512), (4, 14, 24, 128), (224, 512)],
+        [(8, 8, 512), (8, 16, 256), (8, 16, 256)],
+        [slabs(2, 9)] * 11 + [(8, 8, 512), (4, 16, 24, 128), (256, 512)],
         n_in=14, copies=1, out_hbm=1,
     )(*ext, *inside, other, mate)
     emid, spread = call(middle, [(4, 4, 256), (16, 16, 128)], [(128, 128)], n_in=3)(smid, cmid, chalo)
     gathered = lax.all_to_all(spread, "gy", 0, 0, tiled=True)
-    (sdc,) = call(columns, [(192, 128)], [(128, 128)], n_in=1)(gathered.reshape(256, 128))
-    mate, other = swaps(sdc, sdc, "gx")
-    elow, spread = call(low, [(64, 128), (32, 16, 128)], [(64, 128)], n_in=3)(sdc, mate, other)
+    elow, spread = call(low, [(8, 128), (32, 40, 128)], [(64, 128), (192, 128), (128, 128)], n_in=1)(
+        gathered.reshape(256, 128))
     gathered = lax.all_to_all(spread, "gx", 0, 0, tiled=True)
     (correction,) = call(bottom, [(4, 4, 256)], [(17, 16, 128)] + [(16, 16, 128)] * 7, n_in=3)(
         gathered, elow, emid)

time: 91.3 us -> 88.9 us (0.974)
  starting transfers between devices: 24.1 us -> 15.7 us
  blocking collectives: 41.5 us -> 48.7 us
  waiting for transfers between devices: 12.3 us -> 11.2 us
    all_to_all x1, blocking collectives: 16.2 us -> 23.4 us  [shards(): gathered = lax.all_to_all(spread, 'gx', 0, 0, tiled=True)]
    ppermute x3 -> x2, starting transfers between devices: 13 us -> 6.54 us  [swaps(): far = lax.ppermute(far, axis, pairs)]
    ppermute x3 -> x2, starting transfers between devices: 11.1 us -> 9.16 us  [swaps(): return (lax.ppermute(near, axis, [(i, i ^ 1) for i in range(n)]), far)]
    ppermute x3 -> x2, waiting for transfers between devices: 6.91 us -> 6.01 us  [swaps(): return (lax.ppermute(near, axis, [(i, i ^ 1) for i in range(n)]), far)]
    ppermute x3 -> x2, waiting for transfers between devices: 5.34 us -> 5.16 us  [swaps(): far = lax.ppermute(far, axis, pairs)]
    pallas_call x3 -> x2, Pallas kernels: 4.32 us -> 4.39 us  [the longest x1 3.81 us: shards(): call(outer, [(8, 8, 512), (8, 16, 256), (8, 16, 256)], [slabs(2, 9)] * 11...]
  transfers between devices with their start and end apart: 6 -> 4, of which waited for: 4 -> 2; matrix products, arithmetic and copies ran while one was open for 0% -> 0% of each run, Pallas kernels for 2% -> 2%
where the time goes in v6:
time: 88.9 us; the launch traced here: 88.7 us
  blocking collectives  48.7 us (55%)
  starting transfers between devices  15.7 us (18%)
  Pallas kernels  12.4 us (14%)
  waiting for transfers between devices  11.2 us (13%)
    all_to_all x1, blocking collectives, shards(): gathered = lax.all_to_all(spread, 'gy', 0, 0, tiled=True)  25.3 us
    all_to_all x1, blocking collectives, shards(): gathered = lax.all_to_all(spread, 'gx', 0, 0, tiled=True)  23.4 us
    ppermute x2, starting transfers between devices, swaps(): return (lax.ppermute(near, axis, [(i, i ^ 1) for i in range(n)]), far)  9.16 us
    ppermute x2, starting transfers between devices, swaps(): far = lax.ppermute(far, axis, pairs)  6.54 us
    ppermute x2, waiting for transfers between devices, swaps(): return (lax.ppermute(near, axis, [(i, i ^ 1) for i in range(n)]), far)  6.01 us
    ppermute x2, waiting for transfers between devices, swaps(): far = lax.ppermute(far, axis, pairs)  5.16 us
    pallas_call x1, Pallas kernels, shards(): call(outer, [(8, 8, 512), (8, 16, 256), (8, 16, 256)], [slabs(2, 9)] * 11...  3.81 us
    pallas_call x1, Pallas kernels, shards(): call(bottom, [(4, 4, 256)], [(17, 16, 128)] + [(16, 16, 128)] * 7, n_in=3)  3.25 us
  transfers between devices with their start and end apart: 4, of which 2 were waited for; matrix products, arithmetic and copies ran while one was open for 0% of the time, Pallas kernels for 2%

profile of v6, /device:TPU:1, one launch (start us, length us, event | category | flops | bytes accessed | tf_op | source)
XLA Modules:
  0.0 88.7 jit_solution(2927005887549313823)
XLA Ops:
  0.6 0.0 copy-start
  0.6 0.0 copy-start.1
  0.6 0.0 copy-start.2
  0.7 1.9 %shard_map.50 = (f32[160,512]{1,0:T(8,128)}, f32[160,512]{1,0:T(8,128)}) custom-call(f32[64,512]{1,0:T(8,128)} %bitcast.14, f32[64,512]{1,0:T(8,128)} %bitcast.16, f32[64,512]{1,0:T(8,128)} %bitcast.18), custom_call_target="tpu_custom_call" | custom-call | tf_op jit(solution)/shard_map/pallas_call | solution.py:505
  2.6 0.7 collective-permute-start
  3.3 7.2 %collective-permute-start.1 = (f32[160,512]{1,0:T(8,128)}, f32[160,512]{1,0:T(8,128)S(1)}, u32[]{:S(2)}, u32[]{:S(2)}) collective-permute-start(f32[160,512]{1,0:T(8,128)} %get-tuple-element.27), channel_id=1, source_target_pairs={{0,1},{1,0},{2,3},{3,2},{4,5},{5,4},{6,7},{7,6},{8,9},{9,8},{10,11... | collective-permute-start | bytes 983048 | tf_op jit(solution)/shard_map/ppermute | solution.py:500
  10.5 0.0 collective-permute-done.far
  10.5 6.0 %collective-permute-done.1.near = f32[160,512]{1,0:T(8,128)S(1)} collective-permute-done((f32[160,512]{1,0:T(8,128)}, f32[160,512]{1,0:T(8,128)S(1)}, u32[]{:S(2)}, u32[]{:S(2)}) %collective-permute-start.1) | collective-permute-done | bytes 327712 | tf_op jit(solution)/shard_map/ppermute | solution.py:500
  16.5 0.0 copy-done
  16.5 0.0 copy-done.1
  16.5 0.0 copy-done.2
  16.5 0.5 shard_map.51
  17.0 5.9 %collective-permute-start.2 = (f32[344,512]{1,0:T(8,128)S(1)}, f32[344,512]{1,0:T(8,128)S(1)}, u32[]{:S(2)}, u32[]{:S(2)}) collective-permute-start(f32[344,512]{1,0:T(8,128)S(1)} %get-tuple-element.40), channel_id=1, source_target_pairs={{16,32},{48,64},{80,96},{112,128},{144,160},{176,192},{208,224},{2... | collective-permute-start | bytes 2113544 | tf_op jit(solution)/shard_map/ppermute | solution.py:499
  22.9 1.9 %collective-permute-start.3 = (f32[344,512]{1,0:T(8,128)S(1)}, f32[344,512]{1,0:T(8,128)S(1)}, u32[]{:S(2)}, u32[]{:S(2)}) collective-permute-start(f32[344,512]{1,0:T(8,128)S(1)} %get-tuple-element.41), channel_id=1, source_target_pairs={{0,16},{16,0},{32,48},{48,32},{64,80},{80,64},{96,112},{112,96},{1... | collective-permute-start | bytes 2113544 | tf_op jit(solution)/shard_map/ppermute | solution.py:500
  24.8 1.7 %shard_map.52 = (f32[2,3,24,512]{3,2,1,0:T(8,128)S(1)}, f32[1,24,512]{2,1,0:T(8,128)S(1)}, f32[2,4,24,512]{3,2,1,0:T(8,128)S(1)}, f32[2,4,24,512]{3,2,1,0:T(8,12...) custom-call(f32[8,24,512]{2,1,0:T(8,128)S(1)} %bitcast.7, ...), custom_call_target="tpu_custom_call" | custom-call | flops 16000000 | bytes 4000000 | tf_op jit(solution)/shard_map/pallas_call | solution.py:516
  26.5 5.2 %collective-permute-done.2.other = f32[344,512]{1,0:T(8,128)S(1)} collective-permute-done((f32[344,512]{1,0:T(8,128)S(1)}, f32[344,512]{1,0:T(8,128)S(1)}, u32[]{:S(2)}, u32[]{:S(2)}) %collective-permute-start.2) | collective-permute-done | bytes 704544 | tf_op jit(solution)/shard_map/ppermute | solution.py:499
  31.6 0.0 collective-permute-done.3.mate
  31.6 3.8 %shard_map.53 = (f32[8,8,512]{2,1,0:T(8,128)}, f32[8,16,256]{2,1,0:T(8,128)S(1)}, f32[8,16,256]{2,1,0:T(8,128)S(1)}) custom-call(f32[8,24,512]{2,1,0:T(8,128)S(1)} %bitcast.8, f32[8,24,512]{2,1,0:T(8,128)S(1)} %bitcast.10, f32[8,24,512]{2,1,0:T(8,128)S(1)} %bitcast.12, f32[2,3,24,512]{3,2,1,0:T(8,128)S(1)} %get-tuple-element.31.hx, ...), custom_call_target="tpu_custom_call" | custom-call | tf_op jit(solution)/shard_map/pallas_call | solution.py:522
  35.5 0.7 shard_map.54
  36.1 25.3 %all_to_all.10 = f32[16,16,128]{2,1,0:T(8,128)S(1)} all-to-all(f32[16,16,128]{2,1,0:T(8,128)S(1)} %get-tuple-element.46), channel_id=1, replica_groups=mesh['gx'=32,'gy'=16] {'gy'}, dimensions={0} | all-to-all | bytes 262144 | tf_op jit(solution)/shard_map/all_to_all | solution.py:529
  61.4 0.6 shard_map.55
  62.0 23.4 %all_to_all.11.gathered = f32[32,40,128]{2,1,0:T(8,128)S(1)} all-to-all(f32[32,40,128]{2,1,0:T(8,128)S(1)} %get-tuple-element.47), channel_id=1, replica_groups=mesh['gx'=32,'gy'=16] {'gx'}, dimensions={0} | all-to-all | bytes 1310720 | tf_op jit(solution)/shard_map/all_to_all | solution.py:532
  85.4 3.3 %shard_map.56 = f32[4,4,256]{2,1,0:T(4,128)} custom-call(f32[32,40,128]{2,1,0:T(8,128)S(1)} %all_to_all.11.gathered, f32[8,128]{1,0:T(8,128)S(1)} %get-tuple-element.48.elow, f32[4,4,256]{2,1,0:T(4,128)S(1)} %get-tuple-element.49.emid), custom_call_target="tpu_custom_call" | custom-call | tf_op jit(solution)/shard_map/pallas_call | solution.py:533
Async XLA Ops:
  0.6 15.9 %copy-start = (f32[8,8,512]{2,1,0:T(8,128)S(1)}, f32[8,8,512]{2,1,0:T(8,128)}, u32[]{:S(2)}) copy-start(f32[8,8,512]{2,1,0:T(8,128)} %param.3) | copy-start | bytes 393220
  0.6 15.9 %copy-start.1 = (f32[8,8,512]{2,1,0:T(8,128)S(1)}, f32[8,8,512]{2,1,0:T(8,128)}, u32[]{:S(2)}) copy-start(f32[8,8,512]{2,1,0:T(8,128)} %param.4) | copy-start | bytes 393220
  0.6 15.9 %copy-start.2 = (f32[8,8,512]{2,1,0:T(8,128)S(1)}, f32[8,8,512]{2,1,0:T(8,128)}, u32[]{:S(2)}) copy-start(f32[8,8,512]{2,1,0:T(8,128)} %param.5) | copy-start | bytes 393220
  2.6 7.9 %collective-permute-start = (f32[160,512]{1,0:T(8,128)}, f32[160,512]{1,0:T(8,128)S(1)}, u32[]{:S(2)}, u32[]{:S(2)}) collective-permute-start(f32[160,512]{1,0:T(8,128)} %get-tuple-element.26), channel_id=1, source_target_pairs={{1,2},{3,4},{5,6},{7,8},{9,10},{11,12},{13,14},{2,1},{4,3},{6,5},{... | collective-permute-start | bytes 983048 | tf_op jit(solution)/shard_map/ppermute | solution.py:499
  3.3 13.3 %collective-permute-start.1 = (f32[160,512]{1,0:T(8,128)}, f32[160,512]{1,0:T(8,128)S(1)}, u32[]{:S(2)}, u32[]{:S(2)}) collective-permute-start(f32[160,512]{1,0:T(8,128)} %get-tuple-element.27), channel_id=1, source_target_pairs={{0,1},{1,0},{2,3},{3,2},{4,5},{5,4},{6,7},{7,6},{8,9},{9,8},{10,11... | collective-permute-start | bytes 983048 | tf_op jit(solution)/shard_map/ppermute | solution.py:500
  17.0 14.6 %collective-permute-start.2 = (f32[344,512]{1,0:T(8,128)S(1)}, f32[344,512]{1,0:T(8,128)S(1)}, u32[]{:S(2)}, u32[]{:S(2)}) collective-permute-start(f32[344,512]{1,0:T(8,128)S(1)} %get-tuple-element.40), channel_id=1, source_target_pairs={{16,32},{48,64},{80,96},{112,128},{144,160},{176,192},{208,224},{2... | collective-permute-start | bytes 2113544 | tf_op jit(solution)/shard_map/ppermute | solution.py:499
  22.9 8.8 %collective-permute-start.3 = (f32[344,512]{1,0:T(8,128)S(1)}, f32[344,512]{1,0:T(8,128)S(1)}, u32[]{:S(2)}, u32[]{:S(2)}) collective-permute-start(f32[344,512]{1,0:T(8,128)S(1)} %get-tuple-element.41), channel_id=1, source_target_pairs={{0,16},{16,0},{32,48},{48,32},{64,80},{80,64},{96,112},{112,96},{1... | collective-permute-start | bytes 2113544 | tf_op jit(solution)/shard_map/ppermute | solution.py:500

commit v7 on v6

--- a/solution.py
+++ b/solution.py
@@ -57,7 +57,7 @@
 
 
 def matmul(a, b):
-    return jnp.dot(a, b, precision=lax.Precision.HIGHEST, preferred_element_type=F32)
+    return exact_matmul(a, b)
 
 
 def exact_matmul(a, ones):
@@ -124,7 +124,12 @@
         store.wait()
 
 
-def pack_x(phi, rhs, coef, far, near, pe, re, ce, mate, other, stage):
+def hold(*refs):
+    for src, dst in zip(refs[:3], refs[3:]):
+        dst[...] = src[...]
+
+
+def pack_x(phi, rhs, coef, far, near, pe, re, ce, other, stage):
     zero = jnp.zeros((8, 128), F32)
     odd = lax.rem(lax.axis_index("gy"), 2)
     k = 0
@@ -144,18 +149,21 @@
                 ext[24 * x + 8:24 * x + 24, lanes] = stage[base + 16 * x:base + 16 * x + 16, :]
         k += n
     first = is_first()
+    pack_end(other, lambda ext, x, t: ext[pl.ds(pl.multiple_of(24 * x + 8 * t, 8), 8), :], pe, re, ce, first)
+
+
+def pack_end(out, tile, pe, re, ce, is_low):
     top = positions((8, 512), 0) < 4
-    for ref, end in ((mate, first), (other, jnp.logical_not(first))):
-        row = 0
-        for ext, tiles in ((pe, PHI_TILES), (re, RHS_TILES), (ce, COEF_TILES)):
-            for k, n in enumerate(tiles):
-                at = 24 * jnp.where(end, 7 - k, k)
-                parts = [ext[pl.ds(pl.multiple_of(at + 8 * t, 8), 8), :] for t in range(min(n + n // 2, 3))]
-                if n == 2:
-                    parts = [parts[0], jnp.where(top, parts[1], parts[2])]
-                for part in parts:
-                    ref[row:row + 8, :] = part
-                    row += 8
+    row = 0
+    for ext, tiles in ((pe, PHI_TILES), (re, RHS_TILES), (ce, COEF_TILES)):
+        for k, n in enumerate(tiles):
+            x = jnp.where(is_low, k, 7 - k)
+            parts = [tile(ext, x, t) for t in range(min(n + n // 2, 3))]
+            if n == 2:
+                parts = [parts[0], jnp.where(top, parts[1], parts[2])]
+            for part in parts:
+                out[row:row + 8, :] = part
+                row += 8
 
 
 def slab_x(side, t):
@@ -190,7 +198,10 @@
     return exact_matmul(packed[...], halving(512, 256)).reshape(n, 16, 256)
 
 
-def inner(pe, re, ce, hx, hc, hy, hz, dg, rd, p1, p2, res, cmid, sums, packed):
+def inner(pe, re, ce, hx, hc, hy, hz, dg, rd, p1, p2, res, cmid, mate, sums, packed):
+    first = is_first()
+    block = mate.at[jnp.where(first, 1, 0)]
+    pack_end(block, lambda ext, x, t: ext[x, 8 * t:8 * t + 8, :], pe, re, ce, jnp.logical_not(first))
     hc[0] = harmonic(ce[3], ce[4])
 
     def start(side, carry):
@@ -236,7 +247,7 @@
     cmid[...] = halve_fine(sums, packed, 4)
 
 
-def unpack(ref, p0, rs, c, side):
+def unpack(ref, p0, rs, c):
     row = 0
     for dst, tiles in ((p0, PHI_TILES), (rs, RHS_TILES), (c, COEF_TILES)):
         for k, n in enumerate(tiles):
@@ -247,94 +258,103 @@
             if n == 2:
                 parts += [parts[1]]
             for t in range(3):
-                dst[side, k + 1, 8 * t:8 * t + 8, :] = parts[t]
-
-
-def outer(pe, re, ce, hx, hc, hy, hz, dg, rd, p1, p2, res, other, mate, phi_out, smid, chalo,
-          p0h, rsh, ch, hxh, hyh, hzh, dgh, rdh, p1h, p2h, resh, own, sums, packed, left):
+                dst[k + 1, 8 * t:8 * t + 8, :] = parts[t]
+
+
+def one_side(side, received, done, pe, re, ce, hx, hc, hy, hz, dg, rd, p1, p2, res, phi, half,
+             p0h, rsh, ch, hxh, hyh, hzh, dgh, rdh, p1h, p2h, resh, sums, packed):
+    unpack(received, p0h, rsh, ch)
+    x0 = slab_x(side, 3)
+    p0h[0], rsh[0], ch[0] = pe[x0], re[x0], ce[x0]
+    c = ch[0]
+    xp = harmonic(c, ch[1])
+    d = dg[side, 3] + weight(xp, c)
+    r = inverse(d)
+    hxh[0], hyh[0], hzh[0], dgh[0], rdh[0] = xp, hy[side, 3], hz[side, 3], d, r
+    v = p0h[0]
+    image = operate(d, v, xp, p0h[1], hx[side, 2], pe[slab_x(side, 2)], hy[side, 3], hz[side, 3])
+    p1h[0] = v + (rsh[0] - image) * r
+
+    def start(j, carry):
+        c = ch[j]
+        xp, xm = harmonic(c, ch[j + 1]), hxh[j - 1]
+        hyj, hzj, d = first_weights(c, xp, xm)
+        r = inverse(d)
+        hxh[j], hyh[j], hzh[j], dgh[j], rdh[j] = xp, hyj, hzj, d, r
+        v = p0h[j]
+        image = operate(d, v, xp, p0h[j + 1], xm, p0h[j - 1], hyj, hzj)
+        p1h[j] = v + (rsh[j] - image) * r
+        return carry
+
+    lax.fori_loop(1, 7, start, 0, unroll=True)
+
+    image = operate(dg[side, 2], p1[side, 2], hx[side, 2], p1h[0], hx[side, 1], p1[side, 1],
+                    hy[side, 2], hz[side, 2])
+    p2h[1] = p1[side, 2] + (re[slab_x(side, 2)] - image) * rd[side, 2]
+    p2h[0] = p2[side, 1]
+    image = operate(dgh[0], p1h[0], hxh[0], p1h[1], hx[side, 2], p1[side, 2],
+                    hyh[0], hzh[0])
+    p2h[2] = p1h[0] + (rsh[0] - image) * rdh[0]
+
+    def second(j, carry):
+        v = p1h[j]
+        image = operate(dgh[j], v, hxh[j], p1h[j + 1], hxh[j - 1], p1h[j - 1],
+                        hyh[j], hzh[j])
+        p2h[j + 2] = v + (rsh[j] - image) * rdh[j]
+        return carry
+
+    lax.fori_loop(1, 6, second, 0, unroll=True)
+    for t in range(4):
+        phi[jnp.where(side == 0, 3 - t, t)] = (p2[side, t] if t < 2 else p2h[t - 1])[0:8, :]
+
+    for t in (1, 2):
+        image = operate(dg[side, t], p2h[t - 1], hx[side, t], p2h[t], hx[side, t - 1],
+                        p2[side, 0] if t == 1 else p2h[0], hy[side, t], hz[side, t])
+        resh[t - 1] = re[slab_x(side, t)] - image
+    image = operate(dgh[0], p2h[2], hxh[0], p2h[3], hx[side, 2], p2h[1],
+                    hyh[0], hzh[0])
+    resh[2] = rsh[0] - image
+
+    def third(j, carry):
+        image = operate(dgh[j], p2h[j + 2], hxh[j], p2h[j + 3], hxh[j - 1],
+                        p2h[j + 1], hyh[j], hzh[j])
+        resh[j + 2] = rsh[j] - image
+        return carry
+
+    lax.fori_loop(1, 5, third, 0, unroll=True)
+    if done is not None:
+        done()
+    for q in range(4):
+        a = res[side] if q == 0 else resh[2 * q - 1]
+        pair_sums(sums, q, a, resh[2 * q], 0.5)
+        pair_sums(sums, 4 + q, ch[2 * q + 1], ch[2 * q + 2], 0.125)
+    half[...] = halve_fine(sums, packed, 8)
+
+
+def mate_side(*refs):
+    inputs, received, rest = refs[:12], refs[12], refs[13:]
+    side = jnp.where(is_first(), 1, 0)
+    one_side(side, received.at[side], None, *inputs, *rest)
+
+
+def other_side(*refs):
+    inputs, (received, phi_mate, phi_out, half), scratch = refs[:12], refs[12:16], refs[16:-2]
+    phi, left = refs[-2:]
+    side = jnp.where(is_first(), 0, 1)
+    stores = [pltpu.make_async_copy(src, phi_out.at[pl.ds(4 * at, 4)], left.at[k])
+              for k, (src, at) in enumerate(((phi_mate, 1 - side), (phi, side)))]
+    stores[0].start()
+    one_side(side, received, stores[1].start, *inputs, phi, half, *scratch)
+    for store in stores:
+        store.wait()
+
+
+def middle(mate, other, cmid, emid, out, sums):
     first = is_first()
-    near = jnp.where(first, 1, 0)
-    unpack(mate, p0h, rsh, ch, near)
-    unpack(other, p0h, rsh, ch, 1 - near)
-
-    def sweeps(side, carry):
-        x0 = slab_x(side, 3)
-        p0h[side, 0], rsh[side, 0], ch[side, 0] = pe[x0], re[x0], ce[x0]
-        c = ch[side, 0]
-        xp = harmonic(c, ch[side, 1])
-        d = dg[side, 3] + weight(xp, c)
-        r = inverse(d)
-        hxh[side, 0], hyh[side, 0], hzh[side, 0], dgh[side, 0], rdh[side, 0] = xp, hy[side, 3], hz[side, 3], d, r
-        v = p0h[side, 0]
-        image = operate(d, v, xp, p0h[side, 1], hx[side, 2], pe[slab_x(side, 2)], hy[side, 3], hz[side, 3])
-        p1h[side, 0] = v + (rsh[side, 0] - image) * r
-
-        def start(j, carry):
-            c = ch[side, j]
-            xp, xm = harmonic(c, ch[side, j + 1]), hxh[side, j - 1]
-            hyj, hzj, d = first_weights(c, xp, xm)
-            r = inverse(d)
-            hxh[side, j], hyh[side, j], hzh[side, j], dgh[side, j], rdh[side, j] = xp, hyj, hzj, d, r
-            v = p0h[side, j]
-            image = operate(d, v, xp, p0h[side, j + 1], xm, p0h[side, j - 1], hyj, hzj)
-            p1h[side, j] = v + (rsh[side, j] - image) * r
-            return carry
-
-        lax.fori_loop(1, 7, start, 0, unroll=True)
-
-        image = operate(dg[side, 2], p1[side, 2], hx[side, 2], p1h[side, 0], hx[side, 1], p1[side, 1],
-                        hy[side, 2], hz[side, 2])
-        p2h[side, 1] = p1[side, 2] + (re[slab_x(side, 2)] - image) * rd[side, 2]
-        p2h[side, 0] = p2[side, 1]
-        image = operate(dgh[side, 0], p1h[side, 0], hxh[side, 0], p1h[side, 1], hx[side, 2], p1[side, 2],
-                        hyh[side, 0], hzh[side, 0])
-        p2h[side, 2] = p1h[side, 0] + (rsh[side, 0] - image) * rdh[side, 0]
-
-        def second(j, carry):
-            v = p1h[side, j]
-            image = operate(dgh[side, j], v, hxh[side, j], p1h[side, j + 1], hxh[side, j - 1], p1h[side, j - 1],
-                            hyh[side, j], hzh[side, j])
-            p2h[side, j + 2] = v + (rsh[side, j] - image) * rdh[side, j]
-            return carry
-
-        lax.fori_loop(1, 6, second, 0, unroll=True)
-        for t in range(4):
-            own[slab_x(side, t)] = (p2[side, t] if t < 2 else p2h[side, t - 1])[0:8, :]
-
-        for t in (1, 2):
-            image = operate(dg[side, t], p2h[side, t - 1], hx[side, t], p2h[side, t], hx[side, t - 1],
-                            p2[side, 0] if t == 1 else p2h[side, 0], hy[side, t], hz[side, t])
-            resh[side, t - 1] = re[slab_x(side, t)] - image
-        image = operate(dgh[side, 0], p2h[side, 2], hxh[side, 0], p2h[side, 3], hx[side, 2], p2h[side, 1],
-                        hyh[side, 0], hzh[side, 0])
-        resh[side, 2] = rsh[side, 0] - image
-
-        def third(j, carry):
-            image = operate(dgh[side, j], p2h[side, j + 2], hxh[side, j], p2h[side, j + 3], hxh[side, j - 1],
-                            p2h[side, j + 1], hyh[side, j], hzh[side, j])
-            resh[side, j + 2] = rsh[side, j] - image
-            return carry
-
-        lax.fori_loop(1, 5, third, 0, unroll=True)
-        for q in range(4):
-            a = res[side] if q == 0 else resh[side, 2 * q - 1]
-            pair_sums(sums, jnp.where(side == 0, 3 - q, 4 + q), a, resh[side, 2 * q], 0.5)
-        for q in range(4):
-            pair_sums(sums, 8 + jnp.where(side == 0, 3 - q, 4 + q), ch[side, 2 * q + 1], ch[side, 2 * q + 2], 0.125)
-        return carry
-
-    lax.fori_loop(0, 2, sweeps, 0)
-    store = pltpu.make_async_copy(own, phi_out, left.at[0])
-    store.start()
-    mid = halve_fine(sums, packed, 16)
-    smid[...] = mid[0:8]
-    chalo[...] = mid[8:16]
-    store.wait()
-
-
-def middle(smid, cmid, chalo, emid, out, sums):
-    s = [smid[j] for j in range(8)]
-    c = [chalo[j] for j in range(4)] + [cmid[j] for j in range(4)] + [chalo[j] for j in range(4, 8)]
+    lo = [jnp.where(first, other[j], mate[j]) for j in range(8)]
+    hi = [jnp.where(first, mate[j], other[j]) for j in range(8)]
+    s = lo[3::-1] + hi[0:4]
+    c = lo[:3:-1] + [cmid[j] for j in range(4)] + hi[4:8]
     hx = [harmonic(c[j], c[j + 1]) for j in range(1, 10)]
     hy, hz, d, r, e1 = [], [], [], [], []
     for i in range(8):
@@ -473,19 +493,19 @@
             dire[x] = res[x] + beta * dire[x]
         return new
 
-    rr = lax.fori_loop(0, BOTTOM - 1, step, norm())
     gx, gy = lax.axis_index("gx"), lax.axis_index("gy")
+    after = jnp.where(gx < 31, gathered[jnp.minimum(gx + 1, 31), 32:40, :], 0.0)
+    before = jnp.where(gx > 0, gathered[jnp.maximum(gx - 1, 0), 32:40, :], 0.0)
+    lows = elow[0:4, :] + jnp.concatenate([before[6:8, :], after[4:6, :]], axis=0)
+    finer = matmul(jnp.concatenate([lows, lows], axis=0), doubling(128, 256, 2))
+    rr = lax.fori_loop(0, BOTTOM - 1, step, norm(), unroll=True)
     xi = lax.rem(gx, 16)
     alpha = rr / dot_image()
     mine = sol[xi] + alpha * dire[xi]
     mine = jnp.where(gx >= 16, along(mine, 1, 64), mine)
     row = positions((16, 128), 0)
     mine = jnp.sum(jnp.where(row == gy, mine, 0.0), axis=0, keepdims=True)
-    after = jnp.where(gx < 31, gathered[jnp.minimum(gx + 1, 31), 32:40, :], 0.0)
-    before = jnp.where(gx > 0, gathered[jnp.maximum(gx - 1, 0), 32:40, :], 0.0)
-    lows = elow[0:4, :] + jnp.concatenate([before[6:8, :], after[4:6, :]], axis=0)
     coarse = matmul(jnp.broadcast_to(mine, (8, 128)), doubling(128, 256, 4))
-    finer = matmul(jnp.concatenate([lows, lows], axis=0), doubling(128, 256, 2))
     for x in range(4):
         k = 2 * (x // 2)
         for y in range(4):
@@ -493,11 +513,10 @@
             out[x, y:y + 1, :] = emid[x, y:y + 1, :] + add
 
 
-def swaps(near, far, axis):
+def swap(values, axis, far):
     n = lax.axis_size(axis)
-    pairs = [(i, i + 1) for i in range(1, n - 1, 2)] + [(i + 1, i) for i in range(1, n - 1, 2)]
-    far = lax.ppermute(far, axis, pairs)
-    return lax.ppermute(near, axis, [(i, i ^ 1) for i in range(n)]), far
+    pairs = [(i, i + 1) for i in range(int(far), n - 1, 2)]
+    return lax.ppermute(values, axis, pairs + [(j, i) for i, j in pairs])
 
 
 def shards(phi_start, right_side, coefficient):
@@ -505,27 +524,34 @@
     near, far = call(
         pack_y, [(8 * NROWS, 512)] * 2, [(64, 512)] * 3 + [(768, 128), (2, 8 * NROWS, 512)],
         n_in=3, copies=9, in_hbm=3, out_hbm=2, limit=64000000)(*own)
-    near, far = swaps(near, far, "gy")
-    *ext, mate, other = call(pack_x, [(192, 512)] * 3 + [(END_ROWS, 512)] * 2, [(1536, 128)], n_in=5)(*own, far, near)
-    mate, other = swaps(mate, other, "gx")
+    far = swap(far, "gy", True)
+    near = swap(near, "gy", False)
+    own = call(hold, [(64, 512)] * 3, n_in=3,
+               cost=pl.CostEstimate(flops=16_000_000, bytes_accessed=4_000_000, transcendentals=0))(*own)
+    *ext, other = call(pack_x, [(192, 512)] * 3 + [(END_ROWS, 512)], [(1536, 128)], n_in=5)(*own, far, near)
+    other = swap(other, "gx", True)
     ext = [a.reshape(8, 24, 512) for a in ext]
 
     def slabs(*n):
         return (*n, 24, 512)
 
-    *inside, cmid = call(
+    *inside, cmid, mate = call(
         inner,
-        [slabs(2, 3), slabs(1)] + [slabs(2, 4)] * 3 + [slabs(2, 3)] * 2 + [slabs(2, 2), slabs(2), (4, 16, 256)],
+        [slabs(2, 3), slabs(1)] + [slabs(2, 4)] * 3 + [slabs(2, 3)] * 2 + [slabs(2, 2), slabs(2), (4, 16, 256), (2, END_ROWS, 512)],
         [(4, 4, 24, 128), (64, 512)], n_in=3,
-        cost=pl.CostEstimate(flops=16_000_000, bytes_accessed=4_000_000, transcendentals=0),
+        cost=pl.CostEstimate(flops=1_000, bytes_accessed=1_000, transcendentals=0),
     )(*ext)
-    phi_fine, smid, chalo = call(
-        outer,
-        [(8, 8, 512), (8, 16, 256), (8, 16, 256)],
-        [slabs(2, 9)] * 11 + [(8, 8, 512), (4, 16, 24, 128), (256, 512)],
-        n_in=14, copies=1, out_hbm=1,
-    )(*ext, *inside, other, mate)
-    emid, spread = call(middle, [(4, 4, 256), (16, 16, 128)], [(128, 128)], n_in=3)(smid, cmid, chalo)
+    chips = [[i, i + 1] for i in range(0, lax.axis_size("gx"), 2)]
+    mate = lax.all_to_all(mate, "gx", 0, 0, tiled=True, axis_index_groups=chips)
+    scratch = [slabs(9)] * 11 + [(4, 8, 24, 128), (128, 512)]
+    phi_half, half = call(
+        mate_side, [(4, 8, 512), (8, 16, 256)], scratch, n_in=13,
+        cost=pl.CostEstimate(flops=1_000, bytes_accessed=1_000, transcendentals=0),
+    )(*ext, *inside, mate)
+    phi_fine, other_half = call(
+        other_side, [(8, 8, 512), (8, 16, 256)], scratch + [(4, 8, 512)], n_in=14, copies=2, out_hbm=1,
+    )(*ext, *inside, other, phi_half)
+    emid, spread = call(middle, [(4, 4, 256), (16, 16, 128)], [(128, 128)], n_in=3)(half, other_half, cmid)
     gathered = lax.all_to_all(spread, "gy", 0, 0, tiled=True)
     elow, spread = call(low, [(8, 128), (32, 40, 128)], [(64, 128), (192, 128), (128, 128)], n_in=1)(
         gathered.reshape(256, 128))

time: 88.9 us -> 87.2 us (0.981)
  waiting for transfers between devices: 11.2 us -> 3.99 us
  blocking collectives: 48.7 us -> 53.2 us
  local copies, waits for them, and re-layouts: 0.01 us -> 2.71 us
  starting transfers between devices: 15.7 us -> 13.8 us
    ppermute x4 -> x3, waiting for transfers between devices: 11.2 us -> 3.99 us  [swap(): return lax.ppermute(values, axis, pairs + [(j, i) for i, j in pairs])]
    all_to_all x0 -> x1, blocking collectives: none -> 4.48 us  [shards(): mate = lax.all_to_all(mate, 'gx', 0, 0, tiled=True, axis_index_groups=chips)]
    unnamed x6, local copies, waits for them, and re-layouts: 0.01 us -> 2.71 us
    ppermute x4 -> x3, starting transfers between devices: 15.7 us -> 13.8 us  [swap(): return lax.ppermute(values, axis, pairs + [(j, i) for i, j in pairs])]
    pallas_call x2 -> x4, Pallas kernels: 4.26 us -> 4.59 us  [the longest x1 2.35 us: shards(): call(other_side, [(8, 8, 512), (8, 16, 256)], scratch + [(4, 8, 512)], n_...]
  transfers between devices with their start and end apart: 4 -> 3, of which waited for: 2 -> 2; matrix products, arithmetic and copies ran while one was open for 0% -> 0% of each run, Pallas kernels for 2% -> 4%
where the time goes in v7:
time: 87.2 us; the launch traced here: 86.8 us
  blocking collectives  53.2 us (61%)
  starting transfers between devices  13.8 us (16%)
  Pallas kernels  12.5 us (14%)
  waiting for transfers between devices  3.99 us (5%)
  local copies, waits for them, and re-layouts  2.71 us (3%)
    all_to_all x1, blocking collectives, shards(): gathered = lax.all_to_all(spread, 'gy', 0, 0, tiled=True)  25.8 us
    all_to_all x1, blocking collectives, shards(): gathered = lax.all_to_all(spread, 'gx', 0, 0, tiled=True)  22.9 us
    ppermute x3, starting transfers between devices, swap(): return lax.ppermute(values, axis, pairs + [(j, i) for i, j in pairs])  13.8 us
    all_to_all x1, blocking collectives, shards(): mate = lax.all_to_all(mate, 'gx', 0, 0, tiled=True, axis_index_groups=chips)  4.48 us
    ppermute x3, waiting for transfers between devices, swap(): return lax.ppermute(values, axis, pairs + [(j, i) for i, j in pairs])  3.99 us
    pallas_call x1, Pallas kernels, shards(): call(bottom, [(4, 4, 256)], [(17, 16, 128)] + [(16, 16, 128)] * 7, n_in=3)  3.11 us
    unnamed x6, local copies, waits for them, and re-layouts  2.71 us
    pallas_call x1, Pallas kernels, shards(): call(other_side, [(8, 8, 512), (8, 16, 256)], scratch + [(4, 8, 512)], n_...  2.35 us
  transfers between devices with their start and end apart: 3, of which 2 were waited for; matrix products, arithmetic and copies ran while one was open for 0% of the time, Pallas kernels for 4%

profile of v7, /device:TPU:1, one launch (start us, length us, event | category | flops | bytes accessed | tf_op | source)
XLA Modules:
  0.0 86.8 jit_solution(865780346165036594)
XLA Ops:
  0.6 1.9 %shard_map.51 = (f32[160,512]{1,0:T(8,128)}, f32[160,512]{1,0:T(8,128)}) custom-call(f32[64,512]{1,0:T(8,128)} %bitcast.16, f32[64,512]{1,0:T(8,128)} %bitcast.18, f32[64,512]{1,0:T(8,128)} %bitcast.20), custom_call_target="tpu_custom_call" | custom-call | tf_op jit(solution)/shard_map/pallas_call | solution.py:524
  2.5 0.7 collective-permute-start
  3.2 7.2 %collective-permute-start.1 = (f32[160,512]{1,0:T(8,128)}, f32[160,512]{1,0:T(8,128)S(1)}, u32[]{:S(2)}, u32[]{:S(2)}) collective-permute-start(f32[160,512]{1,0:T(8,128)} %get-tuple-element.34), channel_id=1, source_target_pairs={{0,1},{2,3},{4,5},{6,7},{8,9},{10,11},{12,13},{14,15},{1,0},{3,2},... | collective-permute-start | bytes 983048 | tf_op jit(solution)/shard_map/ppermute | solution.py:519
  10.4 0.0 copy-start
  10.5 0.9 %copy-done = f32[8,8,512]{2,1,0:T(8,128)S(1)} copy-done((f32[8,8,512]{2,1,0:T(8,128)S(1)}, f32[8,8,512]{2,1,0:T(8,128)}, u32[]{:S(2)}) %copy-start) | copy-done | bytes 131096
  11.4 0.0 copy-start.1
  11.4 0.9 %copy-done.1 = f32[8,8,512]{2,1,0:T(8,128)S(1)} copy-done((f32[8,8,512]{2,1,0:T(8,128)S(1)}, f32[8,8,512]{2,1,0:T(8,128)}, u32[]{:S(2)}) %copy-start.1) | copy-done | bytes 131096
  12.3 0.0 copy-start.2
  12.3 0.9 %copy-done.2 = f32[8,8,512]{2,1,0:T(8,128)S(1)} copy-done((f32[8,8,512]{2,1,0:T(8,128)S(1)}, f32[8,8,512]{2,1,0:T(8,128)}, u32[]{:S(2)}) %copy-start.2) | copy-done | bytes 131096
  13.2 0.0 collective-permute-done.far
  13.2 3.3 %collective-permute-done.1.near = f32[160,512]{1,0:T(8,128)S(1)} collective-permute-done((f32[160,512]{1,0:T(8,128)}, f32[160,512]{1,0:T(8,128)S(1)}, u32[]{:S(2)}, u32[]{:S(2)}) %collective-permute-start.1) | collective-permute-done | bytes 327712 | tf_op jit(solution)/shard_map/ppermute | solution.py:519
  16.5 0.4 shard_map.52
  16.9 5.9 %collective-permute-start.2 = (f32[344,512]{1,0:T(8,128)S(1)}, f32[344,512]{1,0:T(8,128)S(1)}, u32[]{:S(2)}, u32[]{:S(2)}) collective-permute-start(f32[344,512]{1,0:T(8,128)S(1)} %get-tuple-element.47), channel_id=1, source_target_pairs={{16,32},{48,64},{80,96},{112,128},{144,160},{176,192},{208,224},{2... | collective-permute-start | bytes 2113544 | tf_op jit(solution)/shard_map/ppermute | solution.py:519
  22.7 1.7 %shard_map.53 = (f32[2,3,24,512]{3,2,1,0:T(8,128)S(1)}, f32[1,24,512]{2,1,0:T(8,128)S(1)}, f32[2,4,24,512]{3,2,1,0:T(8,128)S(1)}, f32[2,4,24,512]{3,2,1,0:T(8,12...) custom-call(f32[8,24,512]{2,1,0:T(8,128)S(1)} %bitcast.7, ...), custom_call_target="tpu_custom_call" | custom-call | flops 1000 | bytes 1000 | tf_op jit(solution)/shard_map/pallas_call | solution.py:538
  24.5 4.5 %all_to_all.15.refs_12_ = f32[2,344,512]{2,1,0:T(8,128)S(1)} all-to-all(f32[2,344,512]{2,1,0:T(8,128)S(1)} %get-tuple-element.48), channel_id=1, replica_groups={{0,16},{32,48},{64,80},{96,112},{128,144},{160,176},{192,208},{224,240}..., dimensions={0} | all-to-all | bytes 2818048 | tf_op jit(solution)/shard_map/all_to_all | solution.py:545
  29.0 1.8 %shard_map.54 = (f32[4,8,512]{2,1,0:T(8,128)S(1)}, f32[8,16,256]{2,1,0:T(8,128)S(1)}) custom-call(f32[8,24,512]{2,1,0:T(8,128)S(1)} %bitcast.8, f32[8,24,512]{2,1,0:T(8,128)S(1)} %bitcast.11, f32[8,24,512]{2,1,0:T(8,128)S(1)} %bitcast.14, f32[2,3,24,512]{3,2,1,0:T(8,128)S(1)} %get-tuple-element.38.refs_3_, f32[1,24,512]{2,1,0:T(8,128)S(1)} %get-tuple-element.39.refs_4_, ...), custom_call_target="tpu_custom_call" | custom-call | flops 1000 | bytes 1000 | tf_op jit(solution)/shard_map/pallas_call | solution.py:547
  30.8 0.7 collective-permute-done.2.refs_12_
  31.5 2.3 %shard_map.55 = (f32[8,8,512]{2,1,0:T(8,128)}, f32[8,16,256]{2,1,0:T(8,128)S(1)}) custom-call(f32[8,24,512]{2,1,0:T(8,128)S(1)} %bitcast.9, f32[8,24,512]{2,1,0:T(8,128)S(1)} %bitcast.12, f32[8,24,512]{2,1,0:T(8,128)S(1)} %bitcast.15, f32[2,3,24,512]{3,2,1,0:T(8,128)S(1)} %get-tuple-element.38.refs_3_, f32[1,24,512]{2,1,0:T(8,128)S(1)} %get-tuple-element.39.refs_4_, ...), custom_call_target="tpu_custom_call" | custom-call | tf_op jit(solution)/shard_map/pallas_call | solution.py:551
  33.9 0.6 shard_map.56
  34.5 25.8 %all_to_all.16 = f32[16,16,128]{2,1,0:T(8,128)S(1)} all-to-all(f32[16,16,128]{2,1,0:T(8,128)S(1)} %get-tuple-element.54), channel_id=1, replica_groups=mesh['gx'=32,'gy'=16] {'gy'}, dimensions={0} | all-to-all | bytes 262144 | tf_op jit(solution)/shard_map/all_to_all | solution.py:555
  60.3 0.5 shard_map.57
  60.8 22.9 %all_to_all.17.gathered = f32[32,40,128]{2,1,0:T(8,128)S(1)} all-to-all(f32[32,40,128]{2,1,0:T(8,128)S(1)} %get-tuple-element.55), channel_id=1, replica_groups=mesh['gx'=32,'gy'=16] {'gx'}, dimensions={0} | all-to-all | bytes 1310720 | tf_op jit(solution)/shard_map/all_to_all | solution.py:558
  83.7 3.1 %shard_map.58 = f32[4,4,256]{2,1,0:T(4,128)} custom-call(f32[32,40,128]{2,1,0:T(8,128)S(1)} %all_to_all.17.gathered, f32[8,128]{1,0:T(8,128)S(1)} %get-tuple-element.56.elow, f32[4,4,256]{2,1,0:T(4,128)S(1)} %get-tuple-element.57.emid), custom_call_target="tpu_custom_call" | custom-call | tf_op jit(solution)/shard_map/pallas_call | solution.py:559
  (1 shorter events, 0.0 us)
Async XLA Ops:
  2.5 10.7 %collective-permute-start = (f32[160,512]{1,0:T(8,128)}, f32[160,512]{1,0:T(8,128)S(1)}, u32[]{:S(2)}, u32[]{:S(2)}) collective-permute-start(f32[160,512]{1,0:T(8,128)} %get-tuple-element.33), channel_id=1, source_target_pairs={{1,2},{3,4},{5,6},{7,8},{9,10},{11,12},{13,14},{2,1},{4,3},{6,5},{... | collective-permute-start | bytes 983048 | tf_op jit(solution)/shard_map/ppermute | solution.py:519
  3.2 13.3 %collective-permute-start.1 = (f32[160,512]{1,0:T(8,128)}, f32[160,512]{1,0:T(8,128)S(1)}, u32[]{:S(2)}, u32[]{:S(2)}) collective-permute-start(f32[160,512]{1,0:T(8,128)} %get-tuple-element.34), channel_id=1, source_target_pairs={{0,1},{2,3},{4,5},{6,7},{8,9},{10,11},{12,13},{14,15},{1,0},{3,2},... | collective-permute-start | bytes 983048 | tf_op jit(solution)/shard_map/ppermute | solution.py:519
  10.4 0.9 %copy-start = (f32[8,8,512]{2,1,0:T(8,128)S(1)}, f32[8,8,512]{2,1,0:T(8,128)}, u32[]{:S(2)}) copy-start(f32[8,8,512]{2,1,0:T(8,128)} %param.3) | copy-start | bytes 393220
  11.4 0.9 %copy-start.1 = (f32[8,8,512]{2,1,0:T(8,128)S(1)}, f32[8,8,512]{2,1,0:T(8,128)}, u32[]{:S(2)}) copy-start(f32[8,8,512]{2,1,0:T(8,128)} %param.4) | copy-start | bytes 393220
  12.3 0.9 %copy-start.2 = (f32[8,8,512]{2,1,0:T(8,128)S(1)}, f32[8,8,512]{2,1,0:T(8,128)}, u32[]{:S(2)}) copy-start(f32[8,8,512]{2,1,0:T(8,128)} %param.5) | copy-start | bytes 393220
  16.9 14.6 %collective-permute-start.2 = (f32[344,512]{1,0:T(8,128)S(1)}, f32[344,512]{1,0:T(8,128)S(1)}, u32[]{:S(2)}, u32[]{:S(2)}) collective-permute-start(f32[344,512]{1,0:T(8,128)S(1)} %get-tuple-element.47), channel_id=1, source_target_pairs={{16,32},{48,64},{80,96},{112,128},{144,160},{176,192},{208,224},{2... | collective-permute-start | bytes 2113544 | tf_op jit(solution)/shard_map/ppermute | solution.py:519

commit v8 on v7

--- a/solution.py
+++ b/solution.py
@@ -91,10 +91,12 @@
 
 NP, NR, NC = 7, 6, 7
 NROWS = NP + NR + NC
-PHI_TILES = (3, 3, 2, 2, 2, 2, 1)
-RHS_TILES = (3, 2, 2, 2, 2, 1)
-COEF_TILES = (3, 3, 2, 2, 2, 2, 1, 1)
-END_ROWS = 8 * (sum(PHI_TILES) + sum(RHS_TILES) + sum(COEF_TILES))
+PHI_TILES = (2, 2, 2, 2, 2, 2, 1)
+RHS_TILES = (2, 2, 2, 2, 2, 1)
+COEF_TILES = (2, 2, 2, 2, 2, 2, 1, 1)
+PHI_MORE = 8 * (sum(PHI_TILES) + sum(RHS_TILES) + sum(COEF_TILES))
+COEF_MORE = PHI_MORE + 8
+END_ROWS = PHI_MORE + 16
 
 
 def pack_y(phi_in, rhs_in, coef_in, near, far, phi, rhs, coef, stage, ends, sem):
@@ -158,12 +160,24 @@
     for ext, tiles in ((pe, PHI_TILES), (re, RHS_TILES), (ce, COEF_TILES)):
         for k, n in enumerate(tiles):
             x = jnp.where(is_low, k, 7 - k)
-            parts = [tile(ext, x, t) for t in range(min(n + n // 2, 3))]
+            parts = [tile(ext, x, 0)]
             if n == 2:
-                parts = [parts[0], jnp.where(top, parts[1], parts[2])]
+                parts.append(jnp.where(top, tile(ext, x, 1), tile(ext, x, 2)))
             for part in parts:
                 out[row:row + 8, :] = part
                 row += 8
+
+    def beyond(ext, k):
+        x = jnp.where(is_low, k, 7 - k)
+        return jnp.where(top, tile(ext, x, 2), tile(ext, x, 1))
+
+    at = positions((8, 512), 0)
+    ends = (at == 0) | (at == 7)
+    more = jnp.where(ends, along(beyond(pe, 1), 0, 4), beyond(pe, 0))
+    source = beyond(re, 0)
+    more = jnp.where(at == 1, along(source, 0, 2), jnp.where(at == 6, along(source, 0, -2), more))
+    out[PHI_MORE:PHI_MORE + 8, :] = more
+    out[COEF_MORE:COEF_MORE + 8, :] = jnp.where(ends, along(beyond(ce, 1), 0, 4), beyond(ce, 0))
 
 
 def slab_x(side, t):
@@ -247,46 +261,50 @@
     cmid[...] = halve_fine(sums, packed, 4)
 
 
-def unpack(ref, p0, rs, c):
-    row = 0
-    for dst, tiles in ((p0, PHI_TILES), (rs, RHS_TILES), (c, COEF_TILES)):
-        for k, n in enumerate(tiles):
-            parts = [ref[row + 8 * t:row + 8 * t + 8, :] for t in range(n)]
-            row += 8 * n
+def one_side(side, received, pe, re, ce, hx, hc, hy, hz, dg, rd, p1, p2, res, phi, half,
+             hxh, hyh, hzh, dgh, rdh, p1h, p2h, resh, sums, packed):
+    at = positions((8, 512), 0)
+    top = at < 4
+
+    def slabs_of(own, first_row, tiles, more):
+        def load(j):
+            if j == 0:
+                return own[slab_x(side, 3)]
+            n, row = tiles[j - 1], first_row + 8 * sum(tiles[:j - 1])
+            parts = [received[row + 8 * t:row + 8 * t + 8, :] for t in range(n)]
             if n == 1:
                 parts += [jnp.zeros((8, 512), F32)] * 2
-            if n == 2:
+            elif j <= len(more):
+                parts += [jnp.where(top, more[j - 1], parts[1])]
+                parts[1] = jnp.where(top, parts[1], more[j - 1])
+            else:
                 parts += [parts[1]]
-            for t in range(3):
-                dst[k + 1, 8 * t:8 * t + 8, :] = parts[t]
-
-
-def one_side(side, received, done, pe, re, ce, hx, hc, hy, hz, dg, rd, p1, p2, res, phi, half,
-             p0h, rsh, ch, hxh, hyh, hzh, dgh, rdh, p1h, p2h, resh, sums, packed):
-    unpack(received, p0h, rsh, ch)
-    x0 = slab_x(side, 3)
-    p0h[0], rsh[0], ch[0] = pe[x0], re[x0], ce[x0]
-    c = ch[0]
-    xp = harmonic(c, ch[1])
+            return jnp.concatenate(parts, axis=0)
+        return load
+
+    more_p, more_c = received[PHI_MORE:PHI_MORE + 8, :], received[COEF_MORE:COEF_MORE + 8, :]
+    more_r = jnp.where(top, along(more_p, 0, -2), along(more_p, 0, 2))
+    p0h = slabs_of(pe, 0, PHI_TILES, (more_p, along(more_p, 0, 4)))
+    rsh = slabs_of(re, 8 * sum(PHI_TILES), RHS_TILES, (more_r,))
+    ch = slabs_of(ce, 8 * (sum(PHI_TILES) + sum(RHS_TILES)), COEF_TILES, (more_c, along(more_c, 0, 4)))
+    c = ch(0)
+    xp = harmonic(c, ch(1))
     d = dg[side, 3] + weight(xp, c)
     r = inverse(d)
     hxh[0], hyh[0], hzh[0], dgh[0], rdh[0] = xp, hy[side, 3], hz[side, 3], d, r
-    v = p0h[0]
-    image = operate(d, v, xp, p0h[1], hx[side, 2], pe[slab_x(side, 2)], hy[side, 3], hz[side, 3])
-    p1h[0] = v + (rsh[0] - image) * r
-
-    def start(j, carry):
-        c = ch[j]
-        xp, xm = harmonic(c, ch[j + 1]), hxh[j - 1]
+    v = p0h(0)
+    image = operate(d, v, xp, p0h(1), hx[side, 2], pe[slab_x(side, 2)], hy[side, 3], hz[side, 3])
+    p1h[0] = v + (rsh(0) - image) * r
+
+    for j in range(1, 7):
+        c = ch(j)
+        xp, xm = harmonic(c, ch(j + 1)), hxh[j - 1]
         hyj, hzj, d = first_weights(c, xp, xm)
         r = inverse(d)
         hxh[j], hyh[j], hzh[j], dgh[j], rdh[j] = xp, hyj, hzj, d, r
-        v = p0h[j]
-        image = operate(d, v, xp, p0h[j + 1], xm, p0h[j - 1], hyj, hzj)
-        p1h[j] = v + (rsh[j] - image) * r
-        return carry
-
-    lax.fori_loop(1, 7, start, 0, unroll=True)
+        v = p0h(j)
+        image = operate(d, v, xp, p0h(j + 1), xm, p0h(j - 1), hyj, hzj)
+        p1h[j] = v + (rsh(j) - image) * r
 
     image = operate(dg[side, 2], p1[side, 2], hx[side, 2], p1h[0], hx[side, 1], p1[side, 1],
                     hy[side, 2], hz[side, 2])
@@ -294,16 +312,13 @@
     p2h[0] = p2[side, 1]
     image = operate(dgh[0], p1h[0], hxh[0], p1h[1], hx[side, 2], p1[side, 2],
                     hyh[0], hzh[0])
-    p2h[2] = p1h[0] + (rsh[0] - image) * rdh[0]
-
-    def second(j, carry):
+    p2h[2] = p1h[0] + (rsh(0) - image) * rdh[0]
+
+    for j in range(1, 6):
         v = p1h[j]
         image = operate(dgh[j], v, hxh[j], p1h[j + 1], hxh[j - 1], p1h[j - 1],
                         hyh[j], hzh[j])
-        p2h[j + 2] = v + (rsh[j] - image) * rdh[j]
-        return carry
-
-    lax.fori_loop(1, 6, second, 0, unroll=True)
+        p2h[j + 2] = v + (rsh(j) - image) * rdh[j]
     for t in range(4):
         phi[jnp.where(side == 0, 3 - t, t)] = (p2[side, t] if t < 2 else p2h[t - 1])[0:8, :]
 
@@ -313,43 +328,34 @@
         resh[t - 1] = re[slab_x(side, t)] - image
     image = operate(dgh[0], p2h[2], hxh[0], p2h[3], hx[side, 2], p2h[1],
                     hyh[0], hzh[0])
-    resh[2] = rsh[0] - image
-
-    def third(j, carry):
+    resh[2] = rsh(0) - image
+
+    for j in range(1, 5):
         image = operate(dgh[j], p2h[j + 2], hxh[j], p2h[j + 3], hxh[j - 1],
                         p2h[j + 1], hyh[j], hzh[j])
-        resh[j + 2] = rsh[j] - image
-        return carry
-
-    lax.fori_loop(1, 5, third, 0, unroll=True)
-    if done is not None:
-        done()
+        resh[j + 2] = rsh(j) - image
     for q in range(4):
         a = res[side] if q == 0 else resh[2 * q - 1]
         pair_sums(sums, q, a, resh[2 * q], 0.5)
-        pair_sums(sums, 4 + q, ch[2 * q + 1], ch[2 * q + 2], 0.125)
+        pair_sums(sums, 4 + q, ch(2 * q + 1), ch(2 * q + 2), 0.125)
     half[...] = halve_fine(sums, packed, 8)
 
 
 def mate_side(*refs):
-    inputs, received, rest = refs[:12], refs[12], refs[13:]
     side = jnp.where(is_first(), 1, 0)
-    one_side(side, received.at[side], None, *inputs, *rest)
+    one_side(side, refs[12].at[side], *refs[:12], *refs[13:])
 
 
 def other_side(*refs):
-    inputs, (received, phi_mate, phi_out, half), scratch = refs[:12], refs[12:16], refs[16:-2]
-    phi, left = refs[-2:]
-    side = jnp.where(is_first(), 0, 1)
+    one_side(jnp.where(is_first(), 0, 1), refs[12], *refs[:12], *refs[13:])
+
+
+def middle(mate, other, cmid, phi_mate, phi_other, phi_out, emid, out, sums, left):
+    side = jnp.where(is_first(), 1, 0)
     stores = [pltpu.make_async_copy(src, phi_out.at[pl.ds(4 * at, 4)], left.at[k])
-              for k, (src, at) in enumerate(((phi_mate, 1 - side), (phi, side)))]
-    stores[0].start()
-    one_side(side, received, stores[1].start, *inputs, phi, half, *scratch)
+              for k, (src, at) in enumerate(((phi_mate, side), (phi_other, 1 - side)))]
     for store in stores:
-        store.wait()
-
-
-def middle(mate, other, cmid, emid, out, sums):
+        store.start()
     first = is_first()
     lo = [jnp.where(first, other[j], mate[j]) for j in range(8)]
     hi = [jnp.where(first, mate[j], other[j]) for j in range(8)]
@@ -387,6 +393,8 @@
     for n in range(16):
         out[n, 0:8, :] = low0
         out[n, 8:16, :] = low1
+    for store in stores:
+        store.wait()
 
 
 def y_face(c):
@@ -543,15 +551,16 @@
     )(*ext)
     chips = [[i, i + 1] for i in range(0, lax.axis_size("gx"), 2)]
     mate = lax.all_to_all(mate, "gx", 0, 0, tiled=True, axis_index_groups=chips)
-    scratch = [slabs(9)] * 11 + [(4, 8, 24, 128), (128, 512)]
-    phi_half, half = call(
+    scratch = [slabs(9)] * 8 + [(4, 8, 24, 128), (128, 512)]
+    phi_mate, half = call(
         mate_side, [(4, 8, 512), (8, 16, 256)], scratch, n_in=13,
         cost=pl.CostEstimate(flops=1_000, bytes_accessed=1_000, transcendentals=0),
     )(*ext, *inside, mate)
-    phi_fine, other_half = call(
-        other_side, [(8, 8, 512), (8, 16, 256)], scratch + [(4, 8, 512)], n_in=14, copies=2, out_hbm=1,
-    )(*ext, *inside, other, phi_half)
-    emid, spread = call(middle, [(4, 4, 256), (16, 16, 128)], [(128, 128)], n_in=3)(half, other_half, cmid)
+    phi_other, other_half = call(
+        other_side, [(4, 8, 512), (8, 16, 256)], scratch, n_in=13)(*ext, *inside, other)
+    phi_fine, emid, spread = call(
+        middle, [(8, 8, 512), (4, 4, 256), (16, 16, 128)], [(128, 128)], n_in=5, copies=2, out_hbm=1)(
+        half, other_half, cmid, phi_mate, phi_other)
     gathered = lax.all_to_all(spread, "gy", 0, 0, tiled=True)
     elow, spread = call(low, [(8, 128), (32, 40, 128)], [(64, 128), (192, 128), (128, 128)], n_in=1)(
         gathered.reshape(256, 128))

time: 87.2 us -> 86.5 us (level)
  no operation moved by 1% of the time
where the time goes in v8:
time: 86.5 us; the launch traced here: 86.2 us
  blocking collectives  53.1 us (61%)
  starting transfers between devices  13.8 us (16%)
  Pallas kernels  12.3 us (14%)
  waiting for transfers between devices  3.54 us (4%)
  local copies, waits for them, and re-layouts  2.71 us (3%)
    all_to_all x1, blocking collectives, shards(): gathered = lax.all_to_all(spread, 'gy', 0, 0, tiled=True)  25.6 us
    all_to_all x1, blocking collectives, shards(): gathered = lax.all_to_all(spread, 'gx', 0, 0, tiled=True)  23.1 us
    ppermute x3, starting transfers between devices, swap(): return lax.ppermute(values, axis, pairs + [(j, i) for i, j in pairs])  13.8 us
    all_to_all x1, blocking collectives, shards(): mate = lax.all_to_all(mate, 'gx', 0, 0, tiled=True, axis_index_groups=chips)  4.42 us
    ppermute x3, waiting for transfers between devices, swap(): return lax.ppermute(values, axis, pairs + [(j, i) for i, j in pairs])  3.54 us
    pallas_call x1, Pallas kernels, shards(): call(bottom, [(4, 4, 256)], [(17, 16, 128)] + [(16, 16, 128)] * 7, n_in=3)  3.11 us
    unnamed x6, local copies, waits for them, and re-layouts  2.71 us
    pallas_call x1, Pallas kernels, shards(): call(pack_y, [(8 * NROWS, 512)] * 2, [(64, 512)] * 3 + [(768, 128), (2, 8...  1.87 us
  transfers between devices with their start and end apart: 3, of which 2 were waited for; matrix products, arithmetic and copies ran while one was open for 0% of the time, Pallas kernels for 4%

profile of v8, /device:TPU:1, one launch (start us, length us, event | category | flops | bytes accessed | tf_op | source)
XLA Modules:
  0.0 86.2 jit_solution(8672188894937970403)
XLA Ops:
  0.6 1.9 %shard_map.51 = (f32[160,512]{1,0:T(8,128)}, f32[160,512]{1,0:T(8,128)}) custom-call(f32[64,512]{1,0:T(8,128)} %bitcast.16, f32[64,512]{1,0:T(8,128)} %bitcast.18, f32[64,512]{1,0:T(8,128)} %bitcast.20), custom_call_target="tpu_custom_call" | custom-call | tf_op jit(solution)/shard_map/pallas_call | solution.py:532
  2.5 0.7 collective-permute-start
  3.2 7.2 %collective-permute-start.1 = (f32[160,512]{1,0:T(8,128)}, f32[160,512]{1,0:T(8,128)S(1)}, u32[]{:S(2)}, u32[]{:S(2)}) collective-permute-start(f32[160,512]{1,0:T(8,128)} %get-tuple-element.35), channel_id=1, source_target_pairs={{0,1},{2,3},{4,5},{6,7},{8,9},{10,11},{12,13},{14,15},{1,0},{3,2},... | collective-permute-start | bytes 983048 | tf_op jit(solution)/shard_map/ppermute | solution.py:527
  10.4 0.0 copy-start
  10.5 0.9 %copy-done = f32[8,8,512]{2,1,0:T(8,128)S(1)} copy-done((f32[8,8,512]{2,1,0:T(8,128)S(1)}, f32[8,8,512]{2,1,0:T(8,128)}, u32[]{:S(2)}) %copy-start) | copy-done | bytes 131096
  11.4 0.0 copy-start.1
  11.4 0.9 %copy-done.1 = f32[8,8,512]{2,1,0:T(8,128)S(1)} copy-done((f32[8,8,512]{2,1,0:T(8,128)S(1)}, f32[8,8,512]{2,1,0:T(8,128)}, u32[]{:S(2)}) %copy-start.1) | copy-done | bytes 131096
  12.3 0.0 copy-start.2
  12.3 0.9 %copy-done.2 = f32[8,8,512]{2,1,0:T(8,128)S(1)} copy-done((f32[8,8,512]{2,1,0:T(8,128)S(1)}, f32[8,8,512]{2,1,0:T(8,128)}, u32[]{:S(2)}) %copy-start.2) | copy-done | bytes 131096
  13.2 0.0 collective-permute-done.far
  13.2 3.3 %collective-permute-done.1.near = f32[160,512]{1,0:T(8,128)S(1)} collective-permute-done((f32[160,512]{1,0:T(8,128)}, f32[160,512]{1,0:T(8,128)S(1)}, u32[]{:S(2)}, u32[]{:S(2)}) %collective-permute-start.1) | collective-permute-done | bytes 327712 | tf_op jit(solution)/shard_map/ppermute | solution.py:527
  16.5 0.4 shard_map.52
  16.9 5.9 %collective-permute-start.2 = (f32[320,512]{1,0:T(8,128)S(1)}, f32[320,512]{1,0:T(8,128)S(1)}, u32[]{:S(2)}, u32[]{:S(2)}) collective-permute-start(f32[320,512]{1,0:T(8,128)S(1)} %get-tuple-element.50), channel_id=1, source_target_pairs={{16,32},{48,64},{80,96},{112,128},{144,160},{176,192},{208,224},{2... | collective-permute-start | bytes 1966088 | tf_op jit(solution)/shard_map/ppermute | solution.py:527
  22.7 1.7 %shard_map.53 = (f32[2,3,24,512]{3,2,1,0:T(8,128)S(1)}, f32[1,24,512]{2,1,0:T(8,128)S(1)}, f32[2,4,24,512]{3,2,1,0:T(8,128)S(1)}, f32[2,4,24,512]{3,2,1,0:T(8,12...) custom-call(f32[8,24,512]{2,1,0:T(8,128)S(1)} %bitcast.7, ...), custom_call_target="tpu_custom_call" | custom-call | flops 1000 | bytes 1000 | tf_op jit(solution)/shard_map/pallas_call | solution.py:546
  24.5 4.4 %all_to_all.15.refs_12_ = f32[2,320,512]{2,1,0:T(8,128)S(1)} all-to-all(f32[2,320,512]{2,1,0:T(8,128)S(1)} %get-tuple-element.48), channel_id=1, replica_groups={{0,16},{32,48},{64,80},{96,112},{128,144},{160,176},{192,208},{224,240}..., dimensions={0} | all-to-all | bytes 2621440 | tf_op jit(solution)/shard_map/all_to_all | solution.py:553
  28.9 1.8 %shard_map.54 = (f32[4,8,512]{2,1,0:T(8,128)S(1)}, f32[8,16,256]{2,1,0:T(8,128)S(1)}) custom-call(f32[8,24,512]{2,1,0:T(8,128)S(1)} %bitcast.8, f32[8,24,512]{2,1,0:T(8,128)S(1)} %bitcast.11, f32[8,24,512]{2,1,0:T(8,128)S(1)} %bitcast.14, f32[2,3,24,512]{3,2,1,0:T(8,128)S(1)} %get-tuple-element.39.refs_3_, f32[1,24,512]{2,1,0:T(8,128)S(1)} %get-tuple-element.40.refs_4_, ...), custom_call_target="tpu_custom_call" | custom-call | flops 1000 | bytes 1000 | tf_op jit(solution)/shard_map/pallas_call | solution.py:555
  30.7 0.3 collective-permute-done.2.refs_12_
  31.0 1.8 %shard_map.55 = (f32[4,8,512]{2,1,0:T(8,128)S(1)}, f32[8,16,256]{2,1,0:T(8,128)S(1)}) custom-call(f32[8,24,512]{2,1,0:T(8,128)S(1)} %bitcast.9, f32[8,24,512]{2,1,0:T(8,128)S(1)} %bitcast.12, f32[8,24,512]{2,1,0:T(8,128)S(1)} %bitcast.15, f32[2,3,24,512]{3,2,1,0:T(8,128)S(1)} %get-tuple-element.39.refs_3_, f32[1,24,512]{2,1,0:T(8,128)S(1)} %get-tuple-element.40.refs_4_, ...), custom_call_target="tpu_custom_call" | custom-call | tf_op jit(solution)/shard_map/pallas_call | solution.py:559
  32.8 1.0 %shard_map.56 = (f32[8,8,512]{2,1,0:T(8,128)}, f32[4,4,256]{2,1,0:T(4,128)S(1)}, f32[16,16,128]{2,1,0:T(8,128)S(1)}) custom-call(f32[8,16,256]{2,1,0:T(8,128)S(1)} %get-tuple-element.49.mate, f32[8,16,256]{2,1,0:T(8,128)S(1)} %get-tuple-element.51.other, f32[4,16,256]{2,1,0:T(8,128)S(1)} %get-tuple-element.52.cmid, ...), custom_call_target="tpu_custom_call" | custom-call | tf_op jit(solution)/shard_map/pallas_call | solution.py:561
  33.8 25.6 %all_to_all.16 = f32[16,16,128]{2,1,0:T(8,128)S(1)} all-to-all(f32[16,16,128]{2,1,0:T(8,128)S(1)} %get-tuple-element.56), channel_id=1, replica_groups=mesh['gx'=32,'gy'=16] {'gy'}, dimensions={0} | all-to-all | bytes 262144 | tf_op jit(solution)/shard_map/all_to_all | solution.py:564
  59.4 0.5 shard_map.57
  60.0 23.1 %all_to_all.17.gathered = f32[32,40,128]{2,1,0:T(8,128)S(1)} all-to-all(f32[32,40,128]{2,1,0:T(8,128)S(1)} %get-tuple-element.57), channel_id=1, replica_groups=mesh['gx'=32,'gy'=16] {'gx'}, dimensions={0} | all-to-all | bytes 1310720 | tf_op jit(solution)/shard_map/all_to_all | solution.py:567
  83.1 3.1 %shard_map.58 = f32[4,4,256]{2,1,0:T(4,128)} custom-call(f32[32,40,128]{2,1,0:T(8,128)S(1)} %all_to_all.17.gathered, f32[8,128]{1,0:T(8,128)S(1)} %get-tuple-element.58.elow, f32[4,4,256]{2,1,0:T(4,128)S(1)} %get-tuple-element.59.emid), custom_call_target="tpu_custom_call" | custom-call | tf_op jit(solution)/shard_map/pallas_call | solution.py:568
  (1 shorter events, 0.0 us)
Async XLA Ops:
  2.5 10.7 %collective-permute-start = (f32[160,512]{1,0:T(8,128)}, f32[160,512]{1,0:T(8,128)S(1)}, u32[]{:S(2)}, u32[]{:S(2)}) collective-permute-start(f32[160,512]{1,0:T(8,128)} %get-tuple-element.34), channel_id=1, source_target_pairs={{1,2},{3,4},{5,6},{7,8},{9,10},{11,12},{13,14},{2,1},{4,3},{6,5},{... | collective-permute-start | bytes 983048 | tf_op jit(solution)/shard_map/ppermute | solution.py:527
  3.2 13.3 %collective-permute-start.1 = (f32[160,512]{1,0:T(8,128)}, f32[160,512]{1,0:T(8,128)S(1)}, u32[]{:S(2)}, u32[]{:S(2)}) collective-permute-start(f32[160,512]{1,0:T(8,128)} %get-tuple-element.35), channel_id=1, source_target_pairs={{0,1},{2,3},{4,5},{6,7},{8,9},{10,11},{12,13},{14,15},{1,0},{3,2},... | collective-permute-start | bytes 983048 | tf_op jit(solution)/shard_map/ppermute | solution.py:527
  10.4 0.9 %copy-start = (f32[8,8,512]{2,1,0:T(8,128)S(1)}, f32[8,8,512]{2,1,0:T(8,128)}, u32[]{:S(2)}) copy-start(f32[8,8,512]{2,1,0:T(8,128)} %param.3) | copy-start | bytes 393220
  11.4 0.9 %copy-start.1 = (f32[8,8,512]{2,1,0:T(8,128)S(1)}, f32[8,8,512]{2,1,0:T(8,128)}, u32[]{:S(2)}) copy-start(f32[8,8,512]{2,1,0:T(8,128)} %param.4) | copy-start | bytes 393220
  12.3 0.9 %copy-start.2 = (f32[8,8,512]{2,1,0:T(8,128)S(1)}, f32[8,8,512]{2,1,0:T(8,128)}, u32[]{:S(2)}) copy-start(f32[8,8,512]{2,1,0:T(8,128)} %param.5) | copy-start | bytes 393220
  16.9 14.1 %collective-permute-start.2 = (f32[320,512]{1,0:T(8,128)S(1)}, f32[320,512]{1,0:T(8,128)S(1)}, u32[]{:S(2)}, u32[]{:S(2)}) collective-permute-start(f32[320,512]{1,0:T(8,128)S(1)} %get-tuple-element.50), channel_id=1, source_target_pairs={{16,32},{48,64},{80,96},{112,128},{144,160},{176,192},{208,224},{2... | collective-permute-start | bytes 1966088 | tf_op jit(solution)/shard_map/ppermute | solution.py:527

commit v9 on v8

--- a/solution.py
+++ b/solution.py
@@ -402,7 +402,7 @@
     return harmonic(c, jnp.where(positions(c.shape, 0) < n - 1, along(c, 0, 1), 0.0))
 
 
-def low(gathered, elow, out, scol, ccol, sums):
+def low(gathered, elow, cnear, out, scol, ccol, sums):
     for g in range(8):
         for y in range(2):
             ref, k = (scol, g) if g < 2 else (ccol, g - 2)
@@ -428,29 +428,41 @@
     res = [hx[0] * e2[1]] + [s[j] - image(j, e2) for j in range(1, 5)] + [hx[4] * e2[4]]
 
     quads = [(res[2] + res[3]) * 0.5, (c[2] + c[3]) * 0.125, (res[0] + res[1]) * 0.5, (res[4] + res[5]) * 0.5]
-    for k in range(4):
+    quads += [(c[0] + c[1]) * 0.125, (c[4] + c[5]) * 0.125]
+    for k in range(6):
         sums[32 * k:32 * k + 32, :] = quads[k] + along(quads[k], 0, 1)
-    rows = [sums[pl.ds(32 * k, 16, stride=2), :] for k in range(4)]
-    both = matmul(jnp.concatenate([jnp.concatenate(rows[0:2], axis=1), jnp.concatenate(rows[2:4], axis=1)], axis=0),
-                  halving(256, 128))
+    rows = [sums[pl.ds(32 * k, 16, stride=2), :] for k in range(6)]
+    rows = [jnp.concatenate(rows[k:k + 2], axis=1) for k in (0, 2, 4)]
+    both = matmul(jnp.concatenate(rows, axis=0), halving(256, 128))
+    cnear[...] = both[32:48, :]
     row = positions((32, 128), 0) - 2 * lax.axis_index("gy")
     errors = [jnp.sum(jnp.where(row == y, e2[j], 0.0), axis=0, keepdims=True) for j in (2, 3, 1, 4) for y in range(2)]
     errors = jnp.concatenate(errors, axis=0)
     elow[...] = errors
     for n in range(32):
-        out[n, 0:32, :] = both
-        out[n, 32:40, :] = errors
-
-
-def bottom(gathered, elow, emid, out, hx, hy, hz, dg, sol, res, dire, img):
+        out[n] = both[0:32, :]
+    send = errors[4:8, :]
+    send = jnp.concatenate([along(send, 1, 64), send], axis=0)
+    send = jnp.where(positions((8, 128), 1) < 64, both[0:8, :], send)
+    gx = lax.axis_index("gx")
+
+    @pl.when(gx > 0)
+    def _():
+        out[gx - 1, 0:8, :] = send
+
+    @pl.when(gx < 31)
+    def _():
+        out[gx + 1, 0:8, :] = send
+
+
+def bottom(gathered, elow, cnear, emid, out, cc, hx, hy, hz, dg, sol, res, dire, img):
     half = positions((16, 128), 1) < 64
     last_z = positions((16, 128), 1) % 64 == 63
     last_y = positions((16, 128), 0) == 15
-    c = []
     for x in range(16):
         a, b = gathered[x, 0:16, :], gathered[x + 16, 0:16, :]
         source = jnp.where(half, a, along(b, 1, 64))
-        c.append(jnp.where(half, along(a, 1, 64), b))
+        cc[x] = jnp.where(half, along(a, 1, 64), b)
         b = along(gathered[x + 17, 16:32, :], 1, 64) if x < 15 else 0.0
         source = source + jnp.where(half, gathered[x + 1, 16:32, :], b)
         a = along(gathered[x - 1, 16:32, :], 1, 64) if x > 0 else 0.0
@@ -458,6 +470,23 @@
         res[x] = source
         dire[x] = source
         sol[x] = jnp.zeros((16, 128), F32)
+    gx, gy = lax.axis_index("gx"), lax.axis_index("gy")
+
+    def put_coefficient(x, where_from):
+        at = x // 16
+        value = jnp.where(at == where_from, cnear[...], along(cnear[...], 1, 64))
+        i = lax.rem(x, 16)
+        cc[i] = jnp.where(positions((16, 128), 1) // 64 == at, value, cc[i])
+
+    @pl.when(gx > 0)
+    def _():
+        put_coefficient(gx - 1, 0)
+
+    @pl.when(gx < 31)
+    def _():
+        put_coefficient(gx + 1, 1)
+
+    c = [cc[x] for x in range(16)]
     for x in range(16):
         nxt = c[x + 1] if x < 15 else jnp.where(half, along(c[0], 1, 64), 0.0)
         hx[x + 1] = harmonic(c[x], nxt)
@@ -502,9 +531,13 @@
         return new
 
     gx, gy = lax.axis_index("gx"), lax.axis_index("gy")
-    after = jnp.where(gx < 31, gathered[jnp.minimum(gx + 1, 31), 32:40, :], 0.0)
-    before = jnp.where(gx > 0, gathered[jnp.maximum(gx - 1, 0), 32:40, :], 0.0)
-    lows = elow[0:4, :] + jnp.concatenate([before[6:8, :], after[4:6, :]], axis=0)
+    def errors_from(x, row):
+        rows = gathered[x, 0:8, :]
+        return jnp.where(positions((2, 128), 1) < 64, along(rows, 1, 64)[row:row + 2, :], rows[row + 4:row + 6, :])
+
+    after = jnp.where(gx < 31, errors_from(jnp.minimum(gx + 1, 31), 0), 0.0)
+    before = jnp.where(gx > 0, errors_from(jnp.maximum(gx - 1, 0), 2), 0.0)
+    lows = elow[0:4, :] + jnp.concatenate([before, after], axis=0)
     finer = matmul(jnp.concatenate([lows, lows], axis=0), doubling(128, 256, 2))
     rr = lax.fori_loop(0, BOTTOM - 1, step, norm(), unroll=True)
     xi = lax.rem(gx, 16)
@@ -562,11 +595,11 @@
         middle, [(8, 8, 512), (4, 4, 256), (16, 16, 128)], [(128, 128)], n_in=5, copies=2, out_hbm=1)(
         half, other_half, cmid, phi_mate, phi_other)
     gathered = lax.all_to_all(spread, "gy", 0, 0, tiled=True)
-    elow, spread = call(low, [(8, 128), (32, 40, 128)], [(64, 128), (192, 128), (128, 128)], n_in=1)(
-        gathered.reshape(256, 128))
+    elow, cnear, spread = call(
+        low, [(8, 128), (16, 128), (32, 32, 128)], [(64, 128), (192, 128), (192, 128)], n_in=1)(gathered.reshape(256, 128))
     gathered = lax.all_to_all(spread, "gx", 0, 0, tiled=True)
-    (correction,) = call(bottom, [(4, 4, 256)], [(17, 16, 128)] + [(16, 16, 128)] * 7, n_in=3)(
-        gathered, elow, emid)
+    (correction,) = call(bottom, [(4, 4, 256)], [(16, 16, 128), (17, 16, 128)] + [(16, 16, 128)] * 7, n_in=4)(
+        gathered, elow, cnear, emid)
     return phi_fine, correction
 
 

time: 86.5 us -> 85.4 us (0.987)
  blocking collectives: 53.1 us -> 51.7 us
    all_to_all x1, blocking collectives: 23.1 us -> 21.8 us  [shards(): gathered = lax.all_to_all(spread, 'gx', 0, 0, tiled=True)]
where the time goes in v9:
time: 85.4 us; the launch traced here: 85.1 us
  blocking collectives  51.7 us (61%)
  starting transfers between devices  13.8 us (16%)
  Pallas kernels  12.6 us (15%)
  waiting for transfers between devices  3.54 us (4%)
  local copies, waits for them, and re-layouts  2.71 us (3%)
    all_to_all x1, blocking collectives, shards(): gathered = lax.all_to_all(spread, 'gy', 0, 0, tiled=True)  25.6 us
    all_to_all x1, blocking collectives, shards(): gathered = lax.all_to_all(spread, 'gx', 0, 0, tiled=True)  21.8 us
    ppermute x3, starting transfers between devices, swap(): return lax.ppermute(values, axis, pairs + [(j, i) for i, j in pairs])  13.8 us
    all_to_all x1, blocking collectives, shards(): mate = lax.all_to_all(mate, 'gx', 0, 0, tiled=True, axis_index_groups=chips)  4.42 us
    ppermute x3, waiting for transfers between devices, swap(): return lax.ppermute(values, axis, pairs + [(j, i) for i, j in pairs])  3.54 us
    pallas_call x1, Pallas kernels, shards(): call(bottom, [(4, 4, 256)], [(16, 16, 128), (17, 16, 128)] + [(16, 16, 12...  3.32 us
    unnamed x6, local copies, waits for them, and re-layouts  2.71 us
    pallas_call x1, Pallas kernels, shards(): call(pack_y, [(8 * NROWS, 512)] * 2, [(64, 512)] * 3 + [(768, 128), (2, 8...  1.87 us
  transfers between devices with their start and end apart: 3, of which 2 were waited for; matrix products, arithmetic and copies ran while one was open for 0% of the time, Pallas kernels for 4%

profile of v9, /device:TPU:1, one launch (start us, length us, event | category | flops | bytes accessed | tf_op | source)
XLA Modules:
  0.0 85.1 jit_solution(13128429682788277341)
XLA Ops:
  0.6 1.9 %shard_map.51 = (f32[160,512]{1,0:T(8,128)}, f32[160,512]{1,0:T(8,128)}) custom-call(f32[64,512]{1,0:T(8,128)} %bitcast.16, f32[64,512]{1,0:T(8,128)} %bitcast.18, f32[64,512]{1,0:T(8,128)} %bitcast.20), custom_call_target="tpu_custom_call" | custom-call | tf_op jit(solution)/shard_map/pallas_call | solution.py:565
  2.5 0.7 collective-permute-start
  3.2 7.2 %collective-permute-start.1 = (f32[160,512]{1,0:T(8,128)}, f32[160,512]{1,0:T(8,128)S(1)}, u32[]{:S(2)}, u32[]{:S(2)}) collective-permute-start(f32[160,512]{1,0:T(8,128)} %get-tuple-element.36), channel_id=1, source_target_pairs={{0,1},{2,3},{4,5},{6,7},{8,9},{10,11},{12,13},{14,15},{1,0},{3,2},... | collective-permute-start | bytes 983048 | tf_op jit(solution)/shard_map/ppermute | solution.py:560
  10.4 0.0 copy-start
  10.5 0.9 %copy-done = f32[8,8,512]{2,1,0:T(8,128)S(1)} copy-done((f32[8,8,512]{2,1,0:T(8,128)S(1)}, f32[8,8,512]{2,1,0:T(8,128)}, u32[]{:S(2)}) %copy-start) | copy-done | bytes 131096
  11.4 0.0 copy-start.1
  11.4 0.9 %copy-done.1 = f32[8,8,512]{2,1,0:T(8,128)S(1)} copy-done((f32[8,8,512]{2,1,0:T(8,128)S(1)}, f32[8,8,512]{2,1,0:T(8,128)}, u32[]{:S(2)}) %copy-start.1) | copy-done | bytes 131096
  12.3 0.0 copy-start.2
  12.3 0.9 %copy-done.2 = f32[8,8,512]{2,1,0:T(8,128)S(1)} copy-done((f32[8,8,512]{2,1,0:T(8,128)S(1)}, f32[8,8,512]{2,1,0:T(8,128)}, u32[]{:S(2)}) %copy-start.2) | copy-done | bytes 131096
  13.2 0.0 collective-permute-done.far
  13.2 3.3 %collective-permute-done.1.near = f32[160,512]{1,0:T(8,128)S(1)} collective-permute-done((f32[160,512]{1,0:T(8,128)}, f32[160,512]{1,0:T(8,128)S(1)}, u32[]{:S(2)}, u32[]{:S(2)}) %collective-permute-start.1) | collective-permute-done | bytes 327712 | tf_op jit(solution)/shard_map/ppermute | solution.py:560
  16.5 0.4 shard_map.52
  16.9 5.9 %collective-permute-start.2 = (f32[320,512]{1,0:T(8,128)S(1)}, f32[320,512]{1,0:T(8,128)S(1)}, u32[]{:S(2)}, u32[]{:S(2)}) collective-permute-start(f32[320,512]{1,0:T(8,128)S(1)} %get-tuple-element.51), channel_id=1, source_target_pairs={{16,32},{48,64},{80,96},{112,128},{144,160},{176,192},{208,224},{2... | collective-permute-start | bytes 1966088 | tf_op jit(solution)/shard_map/ppermute | solution.py:560
  22.7 1.7 %shard_map.53 = (f32[2,3,24,512]{3,2,1,0:T(8,128)S(1)}, f32[1,24,512]{2,1,0:T(8,128)S(1)}, f32[2,4,24,512]{3,2,1,0:T(8,128)S(1)}, f32[2,4,24,512]{3,2,1,0:T(8,12...) custom-call(f32[8,24,512]{2,1,0:T(8,128)S(1)} %bitcast.7, ...), custom_call_target="tpu_custom_call" | custom-call | flops 1000 | bytes 1000 | tf_op jit(solution)/shard_map/pallas_call | solution.py:579
  24.5 4.4 %all_to_all.15.refs_12_ = f32[2,320,512]{2,1,0:T(8,128)S(1)} all-to-all(f32[2,320,512]{2,1,0:T(8,128)S(1)} %get-tuple-element.49), channel_id=1, replica_groups={{0,16},{32,48},{64,80},{96,112},{128,144},{160,176},{192,208},{224,240}..., dimensions={0} | all-to-all | bytes 2621440 | tf_op jit(solution)/shard_map/all_to_all | solution.py:586
  28.9 1.8 %shard_map.54 = (f32[4,8,512]{2,1,0:T(8,128)S(1)}, f32[8,16,256]{2,1,0:T(8,128)S(1)}) custom-call(f32[8,24,512]{2,1,0:T(8,128)S(1)} %bitcast.8, f32[8,24,512]{2,1,0:T(8,128)S(1)} %bitcast.11, f32[8,24,512]{2,1,0:T(8,128)S(1)} %bitcast.14, f32[2,3,24,512]{3,2,1,0:T(8,128)S(1)} %get-tuple-element.40.refs_3_, f32[1,24,512]{2,1,0:T(8,128)S(1)} %get-tuple-element.41.refs_4_, ...), custom_call_target="tpu_custom_call" | custom-call | flops 1000 | bytes 1000 | tf_op jit(solution)/shard_map/pallas_call | solution.py:588
  30.7 0.3 collective-permute-done.2.refs_12_
  31.0 1.8 %shard_map.55 = (f32[4,8,512]{2,1,0:T(8,128)S(1)}, f32[8,16,256]{2,1,0:T(8,128)S(1)}) custom-call(f32[8,24,512]{2,1,0:T(8,128)S(1)} %bitcast.9, f32[8,24,512]{2,1,0:T(8,128)S(1)} %bitcast.12, f32[8,24,512]{2,1,0:T(8,128)S(1)} %bitcast.15, f32[2,3,24,512]{3,2,1,0:T(8,128)S(1)} %get-tuple-element.40.refs_3_, f32[1,24,512]{2,1,0:T(8,128)S(1)} %get-tuple-element.41.refs_4_, ...), custom_call_target="tpu_custom_call" | custom-call | tf_op jit(solution)/shard_map/pallas_call | solution.py:592
  32.8 1.0 %shard_map.56 = (f32[8,8,512]{2,1,0:T(8,128)}, f32[4,4,256]{2,1,0:T(4,128)S(1)}, f32[16,16,128]{2,1,0:T(8,128)S(1)}) custom-call(f32[8,16,256]{2,1,0:T(8,128)S(1)} %get-tuple-element.50.mate, f32[8,16,256]{2,1,0:T(8,128)S(1)} %get-tuple-element.52.other, f32[4,16,256]{2,1,0:T(8,128)S(1)} %get-tuple-element.53.cmid, ...), custom_call_target="tpu_custom_call" | custom-call | tf_op jit(solution)/shard_map/pallas_call | solution.py:594
  33.8 25.6 %all_to_all.16 = f32[16,16,128]{2,1,0:T(8,128)S(1)} all-to-all(f32[16,16,128]{2,1,0:T(8,128)S(1)} %get-tuple-element.57), channel_id=1, replica_groups=mesh['gx'=32,'gy'=16] {'gy'}, dimensions={0} | all-to-all | bytes 262144 | tf_op jit(solution)/shard_map/all_to_all | solution.py:597
  59.4 0.6 shard_map.57
  60.0 21.8 %all_to_all.17.gathered = f32[32,32,128]{2,1,0:T(8,128)S(1)} all-to-all(f32[32,32,128]{2,1,0:T(8,128)S(1)} %get-tuple-element.58), channel_id=1, replica_groups=mesh['gx'=32,'gy'=16] {'gx'}, dimensions={0} | all-to-all | bytes 1048576 | tf_op jit(solution)/shard_map/all_to_all | solution.py:600
  81.8 3.3 %shard_map.58 = f32[4,4,256]{2,1,0:T(4,128)} custom-call(f32[32,32,128]{2,1,0:T(8,128)S(1)} %all_to_all.17.gathered, f32[8,128]{1,0:T(8,128)S(1)} %get-tuple-element.59.elow, f32[16,128]{1,0:T(8,128)S(1)} %get-tuple-element.60.cnear, f32[4,4,256]{2,1,0:T(4,128)S(1)} %get-tuple-element.61.emid), custom_call_target="tpu_custom_call" | custom-call | tf_op jit(solution)/shard_map/pallas_call | solution.py:601
  (1 shorter events, 0.0 us)
Async XLA Ops:
  2.5 10.7 %collective-permute-start = (f32[160,512]{1,0:T(8,128)}, f32[160,512]{1,0:T(8,128)S(1)}, u32[]{:S(2)}, u32[]{:S(2)}) collective-permute-start(f32[160,512]{1,0:T(8,128)} %get-tuple-element.35), channel_id=1, source_target_pairs={{1,2},{3,4},{5,6},{7,8},{9,10},{11,12},{13,14},{2,1},{4,3},{6,5},{... | collective-permute-start | bytes 983048 | tf_op jit(solution)/shard_map/ppermute | solution.py:560
  3.2 13.3 %collective-permute-start.1 = (f32[160,512]{1,0:T(8,128)}, f32[160,512]{1,0:T(8,128)S(1)}, u32[]{:S(2)}, u32[]{:S(2)}) collective-permute-start(f32[160,512]{1,0:T(8,128)} %get-tuple-element.36), channel_id=1, source_target_pairs={{0,1},{2,3},{4,5},{6,7},{8,9},{10,11},{12,13},{14,15},{1,0},{3,2},... | collective-permute-start | bytes 983048 | tf_op jit(solution)/shard_map/ppermute | solution.py:560
  10.4 0.9 %copy-start = (f32[8,8,512]{2,1,0:T(8,128)S(1)}, f32[8,8,512]{2,1,0:T(8,128)}, u32[]{:S(2)}) copy-start(f32[8,8,512]{2,1,0:T(8,128)} %param.3) | copy-start | bytes 393220
  11.4 0.9 %copy-start.1 = (f32[8,8,512]{2,1,0:T(8,128)S(1)}, f32[8,8,512]{2,1,0:T(8,128)}, u32[]{:S(2)}) copy-start(f32[8,8,512]{2,1,0:T(8,128)} %param.4) | copy-start | bytes 393220
  12.3 0.9 %copy-start.2 = (f32[8,8,512]{2,1,0:T(8,128)S(1)}, f32[8,8,512]{2,1,0:T(8,128)}, u32[]{:S(2)}) copy-start(f32[8,8,512]{2,1,0:T(8,128)} %param.5) | copy-start | bytes 393220
  16.9 14.1 %collective-permute-start.2 = (f32[320,512]{1,0:T(8,128)S(1)}, f32[320,512]{1,0:T(8,128)S(1)}, u32[]{:S(2)}, u32[]{:S(2)}) collective-permute-start(f32[320,512]{1,0:T(8,128)S(1)} %get-tuple-element.51), channel_id=1, source_target_pairs={{16,32},{48,64},{80,96},{112,128},{144,160},{176,192},{208,224},{2... | collective-permute-start | bytes 1966088 | tf_op jit(solution)/shard_map/ppermute | solution.py:560

commit v10 on v9

--- a/solution.py
+++ b/solution.py
@@ -94,20 +94,27 @@
 PHI_TILES = (2, 2, 2, 2, 2, 2, 1)
 RHS_TILES = (2, 2, 2, 2, 2, 1)
 COEF_TILES = (2, 2, 2, 2, 2, 2, 1, 1)
+TILES = (PHI_TILES, RHS_TILES, COEF_TILES)
 PHI_MORE = 8 * (sum(PHI_TILES) + sum(RHS_TILES) + sum(COEF_TILES))
 COEF_MORE = PHI_MORE + 8
 END_ROWS = PHI_MORE + 16
-
-
-def pack_y(phi_in, rhs_in, coef_in, near, far, phi, rhs, coef, stage, ends, sem):
+OWN_ROWS = 8 * (len(PHI_TILES) + len(RHS_TILES) + len(COEF_TILES))
+
+
+def pack_y(phi_in, rhs_in, coef_in, near, far, own_end, phi, rhs, coef, stage, ends, sem):
     loads = [pltpu.make_async_copy(src, dst, sem.at[a])
              for a, (src, dst) in enumerate(((phi_in, phi), (rhs_in, rhs), (coef_in, coef)))]
     for load in loads:
         load.start()
-    stores = []
+    stores, row = [], 0
     k = 0
     for a, (ref, n) in enumerate(((phi, NP), (rhs, NR), (coef, NC))):
         loads[a].wait()
+        slabs = 8 * len(TILES[a])
+        first_row = pl.multiple_of(jnp.where(is_first(), 0, 64 - slabs), 8)
+        stores.append(pltpu.make_async_copy(ref.at[pl.ds(first_row, slabs)], own_end.at[pl.ds(row, slabs)], sem.at[9 + a]))
+        stores[-1].start()
+        row += slabs
         for q in range(4):
             lanes = slice(128 * q, 128 * q + 128)
             base = 64 * (4 * a + q)
@@ -151,16 +158,16 @@
                 ext[24 * x + 8:24 * x + 24, lanes] = stage[base + 16 * x:base + 16 * x + 16, :]
         k += n
     first = is_first()
-    pack_end(other, lambda ext, x, t: ext[pl.ds(pl.multiple_of(24 * x + 8 * t, 8), 8), :], pe, re, ce, first)
-
-
-def pack_end(out, tile, pe, re, ce, is_low):
+    pack_end(other, lambda ext, x, t: ext[pl.ds(pl.multiple_of(24 * x + 8 * t, 8), 8), :], pe, re, ce, first, False)
+
+
+def pack_end(out, tile, pe, re, ce, is_low, with_own=True):
     top = positions((8, 512), 0) < 4
     row = 0
     for ext, tiles in ((pe, PHI_TILES), (re, RHS_TILES), (ce, COEF_TILES)):
         for k, n in enumerate(tiles):
             x = jnp.where(is_low, k, 7 - k)
-            parts = [tile(ext, x, 0)]
+            parts = [tile(ext, x, 0)] if with_own else []
             if n == 2:
                 parts.append(jnp.where(top, tile(ext, x, 1), tile(ext, x, 2)))
             for part in parts:
@@ -176,8 +183,8 @@
     more = jnp.where(ends, along(beyond(pe, 1), 0, 4), beyond(pe, 0))
     source = beyond(re, 0)
     more = jnp.where(at == 1, along(source, 0, 2), jnp.where(at == 6, along(source, 0, -2), more))
-    out[PHI_MORE:PHI_MORE + 8, :] = more
-    out[COEF_MORE:COEF_MORE + 8, :] = jnp.where(ends, along(beyond(ce, 1), 0, 4), beyond(ce, 0))
+    out[row:row + 8, :] = more
+    out[row + 8:row + 16, :] = jnp.where(ends, along(beyond(ce, 1), 0, 4), beyond(ce, 0))
 
 
 def slab_x(side, t):
@@ -261,17 +268,27 @@
     cmid[...] = halve_fine(sums, packed, 4)
 
 
-def one_side(side, received, pe, re, ce, hx, hc, hy, hz, dg, rd, p1, p2, res, phi, half,
+def one_side(side, received, own_end, pe, re, ce, hx, hc, hy, hz, dg, rd, p1, p2, res, phi, half,
              hxh, hyh, hzh, dgh, rdh, p1h, p2h, resh, sums, packed):
     at = positions((8, 512), 0)
     top = at < 4
 
-    def slabs_of(own, first_row, tiles, more):
+    def slabs_of(own, a, more):
+        tiles = TILES[a]
+        first_row = 8 * sum(sum(t) if own_end is None else sum(t) - len(t) for t in TILES[:a])
+        own_row = 8 * sum(len(t) for t in TILES[:a])
         def load(j):
             if j == 0:
                 return own[slab_x(side, 3)]
-            n, row = tiles[j - 1], first_row + 8 * sum(tiles[:j - 1])
-            parts = [received[row + 8 * t:row + 8 * t + 8, :] for t in range(n)]
+            n = tiles[j - 1]
+            if own_end is None:
+                row = first_row + 8 * sum(tiles[:j - 1])
+                parts = [received[row + 8 * t:row + 8 * t + 8, :] for t in range(n)]
+            else:
+                row = own_row + 8 * jnp.where(side == 1, j - 1, len(tiles) - j)
+                parts = [own_end[pl.ds(pl.multiple_of(row, 8), 8), :]]
+                row = first_row + 8 * (j - 1)
+                parts += [received[row:row + 8, :]] * (n - 1)
             if n == 1:
                 parts += [jnp.zeros((8, 512), F32)] * 2
             elif j <= len(more):
@@ -282,11 +299,12 @@
             return jnp.concatenate(parts, axis=0)
         return load
 
-    more_p, more_c = received[PHI_MORE:PHI_MORE + 8, :], received[COEF_MORE:COEF_MORE + 8, :]
+    row = received.shape[0] - 16
+    more_p, more_c = received[row:row + 8, :], received[row + 8:row + 16, :]
     more_r = jnp.where(top, along(more_p, 0, -2), along(more_p, 0, 2))
-    p0h = slabs_of(pe, 0, PHI_TILES, (more_p, along(more_p, 0, 4)))
-    rsh = slabs_of(re, 8 * sum(PHI_TILES), RHS_TILES, (more_r,))
-    ch = slabs_of(ce, 8 * (sum(PHI_TILES) + sum(RHS_TILES)), COEF_TILES, (more_c, along(more_c, 0, 4)))
+    p0h = slabs_of(pe, 0, (more_p, along(more_p, 0, 4)))
+    rsh = slabs_of(re, 1, (more_r,))
+    ch = slabs_of(ce, 2, (more_c, along(more_c, 0, 4)))
     c = ch(0)
     xp = harmonic(c, ch(1))
     d = dg[side, 3] + weight(xp, c)
@@ -343,11 +361,11 @@
 
 def mate_side(*refs):
     side = jnp.where(is_first(), 1, 0)
-    one_side(side, refs[12].at[side], *refs[:12], *refs[13:])
+    one_side(side, refs[12].at[side], None, *refs[:12], *refs[13:])
 
 
 def other_side(*refs):
-    one_side(jnp.where(is_first(), 0, 1), refs[12], *refs[:12], *refs[13:])
+    one_side(jnp.where(is_first(), 0, 1), refs[12], refs[13], *refs[:12], *refs[14:])
 
 
 def middle(mate, other, cmid, phi_mate, phi_other, phi_out, emid, out, sums, left):
@@ -455,14 +473,21 @@
         out[gx + 1, 0:8, :] = send
 
 
-def bottom(gathered, elow, cnear, emid, out, cc, hx, hy, hz, dg, sol, res, dire, img):
+def bottom(gathered, elow, cnear, emid, out, hx, hy, hz, dg, sol, res, dire, img):
     half = positions((16, 128), 1) < 64
     last_z = positions((16, 128), 1) % 64 == 63
     last_y = positions((16, 128), 0) == 15
+    gx, gy = lax.axis_index("gx"), lax.axis_index("gy")
+    before = jnp.where(half, cnear[...], along(cnear[...], 1, 64))
+    after = jnp.where(half, along(cnear[...], 1, 64), cnear[...])
+    column = positions((16, 128), 1) // 64 * 16
+    c = []
     for x in range(16):
         a, b = gathered[x, 0:16, :], gathered[x + 16, 0:16, :]
         source = jnp.where(half, a, along(b, 1, 64))
-        cc[x] = jnp.where(half, along(a, 1, 64), b)
+        value = jnp.where(half, along(a, 1, 64), b)
+        value = jnp.where(column == gx - 1 - x, before, value)
+        c.append(jnp.where(column == gx + 1 - x, after, value))
         b = along(gathered[x + 17, 16:32, :], 1, 64) if x < 15 else 0.0
         source = source + jnp.where(half, gathered[x + 1, 16:32, :], b)
         a = along(gathered[x - 1, 16:32, :], 1, 64) if x > 0 else 0.0
@@ -470,23 +495,6 @@
         res[x] = source
         dire[x] = source
         sol[x] = jnp.zeros((16, 128), F32)
-    gx, gy = lax.axis_index("gx"), lax.axis_index("gy")
-
-    def put_coefficient(x, where_from):
-        at = x // 16
-        value = jnp.where(at == where_from, cnear[...], along(cnear[...], 1, 64))
-        i = lax.rem(x, 16)
-        cc[i] = jnp.where(positions((16, 128), 1) // 64 == at, value, cc[i])
-
-    @pl.when(gx > 0)
-    def _():
-        put_coefficient(gx - 1, 0)
-
-    @pl.when(gx < 31)
-    def _():
-        put_coefficient(gx + 1, 1)
-
-    c = [cc[x] for x in range(16)]
     for x in range(16):
         nxt = c[x + 1] if x < 15 else jnp.where(half, along(c[0], 1, 64), 0.0)
         hx[x + 1] = harmonic(c[x], nxt)
@@ -562,14 +570,15 @@
 
 def shards(phi_start, right_side, coefficient):
     own = [a.reshape(64, 512) for a in (phi_start, right_side, coefficient)]
-    near, far = call(
-        pack_y, [(8 * NROWS, 512)] * 2, [(64, 512)] * 3 + [(768, 128), (2, 8 * NROWS, 512)],
-        n_in=3, copies=9, in_hbm=3, out_hbm=2, limit=64000000)(*own)
+    near, far, own_end = call(
+        pack_y, [(8 * NROWS, 512)] * 2 + [(OWN_ROWS, 512)], [(64, 512)] * 3 + [(768, 128), (2, 8 * NROWS, 512)],
+        n_in=3, copies=12, in_hbm=3, out_hbm=3, limit=64000000)(*own)
     far = swap(far, "gy", True)
     near = swap(near, "gy", False)
+    own_end = swap(own_end, "gx", True)
     own = call(hold, [(64, 512)] * 3, n_in=3,
                cost=pl.CostEstimate(flops=16_000_000, bytes_accessed=4_000_000, transcendentals=0))(*own)
-    *ext, other = call(pack_x, [(192, 512)] * 3 + [(END_ROWS, 512)], [(1536, 128)], n_in=5)(*own, far, near)
+    *ext, other = call(pack_x, [(192, 512)] * 3 + [(END_ROWS - OWN_ROWS, 512)], [(1536, 128)], n_in=5)(*own, far, near)
     other = swap(other, "gx", True)
     ext = [a.reshape(8, 24, 512) for a in ext]
 
@@ -590,7 +599,7 @@
         cost=pl.CostEstimate(flops=1_000, bytes_accessed=1_000, transcendentals=0),
     )(*ext, *inside, mate)
     phi_other, other_half = call(
-        other_side, [(4, 8, 512), (8, 16, 256)], scratch, n_in=13)(*ext, *inside, other)
+        other_side, [(4, 8, 512), (8, 16, 256)], scratch, n_in=14)(*ext, *inside, other, own_end)
     phi_fine, emid, spread = call(
         middle, [(8, 8, 512), (4, 4, 256), (16, 16, 128)], [(128, 128)], n_in=5, copies=2, out_hbm=1)(
         half, other_half, cmid, phi_mate, phi_other)
@@ -598,7 +607,7 @@
     elow, cnear, spread = call(
         low, [(8, 128), (16, 128), (32, 32, 128)], [(64, 128), (192, 128), (192, 128)], n_in=1)(gathered.reshape(256, 128))
     gathered = lax.all_to_all(spread, "gx", 0, 0, tiled=True)
-    (correction,) = call(bottom, [(4, 4, 256)], [(16, 16, 128), (17, 16, 128)] + [(16, 16, 128)] * 7, n_in=4)(
+    (correction,) = call(bottom, [(4, 4, 256)], [(17, 16, 128)] + [(16, 16, 128)] * 7, n_in=4)(
         gathered, elow, cnear, emid)
     return phi_fine, correction
 

time: 85.4 us -> 84.4 us (0.988)
  waiting for transfers between devices: 3.54 us -> 0.01 us
  starting transfers between devices: 13.8 us -> 17 us
    ppermute x3 -> x4, waiting for transfers between devices: 3.54 us -> 0.01 us  [swap(): return lax.ppermute(values, axis, pairs + [(j, i) for i, j in pairs])]
    ppermute x3 -> x4, starting transfers between devices: 13.8 us -> 17 us  [swap(): return lax.ppermute(values, axis, pairs + [(j, i) for i, j in pairs])]
  transfers between devices with their start and end apart: 3 -> 4, of which waited for: 2 -> 0; matrix products, arithmetic and copies ran while one was open for 0% -> 0% of each run, Pallas kernels for 4% -> 5%
where the time goes in v10:
time: 84.4 us; the launch traced here: 84.1 us
  blocking collectives  51.1 us (61%)
  starting transfers between devices  17 us (20%)
  Pallas kernels  12.5 us (15%)
  local copies, waits for them, and re-layouts  2.71 us (3%)
    all_to_all x1, blocking collectives, shards(): gathered = lax.all_to_all(spread, 'gy', 0, 0, tiled=True)  25.3 us
    all_to_all x1, blocking collectives, shards(): gathered = lax.all_to_all(spread, 'gx', 0, 0, tiled=True)  21.4 us
    ppermute x4, starting transfers between devices, swap(): return lax.ppermute(values, axis, pairs + [(j, i) for i, j in pairs])  17 us
    all_to_all x1, blocking collectives, shards(): mate = lax.all_to_all(mate, 'gx', 0, 0, tiled=True, axis_index_groups=chips)  4.42 us
    pallas_call x1, Pallas kernels, shards(): call(bottom, [(4, 4, 256)], [(17, 16, 128)] + [(16, 16, 128)] * 7, n_in=4)  3.12 us
    unnamed x6, local copies, waits for them, and re-layouts  2.71 us
    pallas_call x1, Pallas kernels, shards(): call(pack_y, [(8 * NROWS, 512)] * 2 + [(OWN_ROWS, 512)], [(64, 512)] * 3...  1.98 us
    pallas_call x1, Pallas kernels, shards(): call(mate_side, [(4, 8, 512), (8, 16, 256)], scratch, n_in=13, cost=pl.Co...  1.79 us
  transfers between devices with their start and end apart: 4, of which 0 were waited for; matrix products, arithmetic and copies ran while one was open for 0% of the time, Pallas kernels for 5%

profile of v10, /device:TPU:1, one launch (start us, length us, event | category | flops | bytes accessed | tf_op | source)
XLA Modules:
  0.0 84.1 jit_solution(15235594257274872168)
XLA Ops:
  0.6 2.0 %shard_map.51 = (f32[160,512]{1,0:T(8,128)}, f32[160,512]{1,0:T(8,128)}, f32[168,512]{1,0:T(8,128)}) custom-call(f32[64,512]{1,0:T(8,128)} %bitcast.16, f32[64,512]{1,0:T(8,128)} %bitcast.18, f32[64,512]{1,0:T(8,128)} %bitcast.20), custom_call_target="tpu_custom_call" | custom-call | tf_op jit(solution)/shard_map/pallas_call | solution.py:573
  2.6 0.7 collective-permute-start
  3.3 7.2 %collective-permute-start.1 = (f32[160,512]{1,0:T(8,128)}, f32[160,512]{1,0:T(8,128)S(1)}, u32[]{:S(2)}, u32[]{:S(2)}) collective-permute-start(f32[160,512]{1,0:T(8,128)} %get-tuple-element.37), channel_id=1, source_target_pairs={{0,1},{2,3},{4,5},{6,7},{8,9},{10,11},{12,13},{14,15},{1,0},{3,2},... | collective-permute-start | bytes 983048 | tf_op jit(solution)/shard_map/ppermute | solution.py:568
  10.6 4.2 %collective-permute-start.3 = (f32[168,512]{1,0:T(8,128)}, f32[168,512]{1,0:T(8,128)S(1)}, u32[]{:S(2)}, u32[]{:S(2)}) collective-permute-start(f32[168,512]{1,0:T(8,128)} %get-tuple-element.53), channel_id=1, source_target_pairs={{16,32},{48,64},{80,96},{112,128},{144,160},{176,192},{208,224},{2... | collective-permute-start | bytes 1032200 | tf_op jit(solution)/shard_map/ppermute | solution.py:568
  14.8 0.0 copy-start
  14.8 0.9 %copy-done = f32[8,8,512]{2,1,0:T(8,128)S(1)} copy-done((f32[8,8,512]{2,1,0:T(8,128)S(1)}, f32[8,8,512]{2,1,0:T(8,128)}, u32[]{:S(2)}) %copy-start) | copy-done | bytes 131096
  15.7 0.0 copy-start.1
  15.7 0.9 %copy-done.1 = f32[8,8,512]{2,1,0:T(8,128)S(1)} copy-done((f32[8,8,512]{2,1,0:T(8,128)S(1)}, f32[8,8,512]{2,1,0:T(8,128)}, u32[]{:S(2)}) %copy-start.1) | copy-done | bytes 131096
  16.6 0.0 copy-start.2
  16.6 0.9 %copy-done.2 = f32[8,8,512]{2,1,0:T(8,128)S(1)} copy-done((f32[8,8,512]{2,1,0:T(8,128)S(1)}, f32[8,8,512]{2,1,0:T(8,128)}, u32[]{:S(2)}) %copy-start.2) | copy-done | bytes 131096
  17.5 0.0 collective-permute-done.far
  17.6 0.0 collective-permute-done.1.near
  17.6 0.4 shard_map.52
  18.0 4.8 %collective-permute-start.2 = (f32[152,512]{1,0:T(8,128)S(1)}, f32[152,512]{1,0:T(8,128)S(1)}, u32[]{:S(2)}, u32[]{:S(2)}) collective-permute-start(f32[152,512]{1,0:T(8,128)S(1)} %get-tuple-element.52), channel_id=1, source_target_pairs={{16,32},{48,64},{80,96},{112,128},{144,160},{176,192},{208,224},{2... | collective-permute-start | bytes 933896 | tf_op jit(solution)/shard_map/ppermute | solution.py:568
  22.8 1.7 %shard_map.53 = (f32[2,3,24,512]{3,2,1,0:T(8,128)S(1)}, f32[1,24,512]{2,1,0:T(8,128)S(1)}, f32[2,4,24,512]{3,2,1,0:T(8,128)S(1)}, f32[2,4,24,512]{3,2,1,0:T(8,12...) custom-call(f32[8,24,512]{2,1,0:T(8,128)S(1)} %bitcast.7, ...), custom_call_target="tpu_custom_call" | custom-call | flops 1000 | bytes 1000 | tf_op jit(solution)/shard_map/pallas_call | solution.py:588
  24.6 4.4 %all_to_all.15.refs_12_ = f32[2,320,512]{2,1,0:T(8,128)S(1)} all-to-all(f32[2,320,512]{2,1,0:T(8,128)S(1)} %get-tuple-element.50), channel_id=1, replica_groups={{0,16},{32,48},{64,80},{96,112},{128,144},{160,176},{192,208},{224,240}..., dimensions={0} | all-to-all | bytes 2621440 | tf_op jit(solution)/shard_map/all_to_all | solution.py:595
  29.0 1.8 %shard_map.54 = (f32[4,8,512]{2,1,0:T(8,128)S(1)}, f32[8,16,256]{2,1,0:T(8,128)S(1)}) custom-call(f32[8,24,512]{2,1,0:T(8,128)S(1)} %bitcast.8, f32[8,24,512]{2,1,0:T(8,128)S(1)} %bitcast.11, f32[8,24,512]{2,1,0:T(8,128)S(1)} %bitcast.14, f32[2,3,24,512]{3,2,1,0:T(8,128)S(1)} %get-tuple-element.41.refs_3_, f32[1,24,512]{2,1,0:T(8,128)S(1)} %get-tuple-element.42.refs_4_, ...), custom_call_target="tpu_custom_call" | custom-call | flops 1000 | bytes 1000 | tf_op jit(solution)/shard_map/pallas_call | solution.py:597
  30.8 0.0 collective-permute-done.3.refs_13_
  30.8 0.0 collective-permute-done.2.refs_12_
  30.8 1.8 %shard_map.55 = (f32[4,8,512]{2,1,0:T(8,128)S(1)}, f32[8,16,256]{2,1,0:T(8,128)S(1)}) custom-call(f32[8,24,512]{2,1,0:T(8,128)S(1)} %bitcast.9, f32[8,24,512]{2,1,0:T(8,128)S(1)} %bitcast.12, f32[8,24,512]{2,1,0:T(8,128)S(1)} %bitcast.15, f32[2,3,24,512]{3,2,1,0:T(8,128)S(1)} %get-tuple-element.41.refs_3_, f32[1,24,512]{2,1,0:T(8,128)S(1)} %get-tuple-element.42.refs_4_, ...), custom_call_target="tpu_custom_call" | custom-call | tf_op jit(solution)/shard_map/pallas_call | solution.py:601
  32.6 1.0 %shard_map.56 = (f32[8,8,512]{2,1,0:T(8,128)}, f32[4,4,256]{2,1,0:T(4,128)S(1)}, f32[16,16,128]{2,1,0:T(8,128)S(1)}) custom-call(f32[8,16,256]{2,1,0:T(8,128)S(1)} %get-tuple-element.51.mate, f32[8,16,256]{2,1,0:T(8,128)S(1)} %get-tuple-element.54.other, f32[4,16,256]{2,1,0:T(8,128)S(1)} %get-tuple-element.55.cmid, ...), custom_call_target="tpu_custom_call" | custom-call | tf_op jit(solution)/shard_map/pallas_call | solution.py:603
  33.7 25.3 %all_to_all.16 = f32[16,16,128]{2,1,0:T(8,128)S(1)} all-to-all(f32[16,16,128]{2,1,0:T(8,128)S(1)} %get-tuple-element.59), channel_id=1, replica_groups=mesh['gx'=32,'gy'=16] {'gy'}, dimensions={0} | all-to-all | bytes 262144 | tf_op jit(solution)/shard_map/all_to_all | solution.py:606
  59.0 0.6 shard_map.57
  59.6 21.4 %all_to_all.17.gathered = f32[32,32,128]{2,1,0:T(8,128)S(1)} all-to-all(f32[32,32,128]{2,1,0:T(8,128)S(1)} %get-tuple-element.60), channel_id=1, replica_groups=mesh['gx'=32,'gy'=16] {'gx'}, dimensions={0} | all-to-all | bytes 1048576 | tf_op jit(solution)/shard_map/all_to_all | solution.py:609
  81.0 3.1 %shard_map.58 = f32[4,4,256]{2,1,0:T(4,128)} custom-call(f32[32,32,128]{2,1,0:T(8,128)S(1)} %all_to_all.17.gathered, f32[8,128]{1,0:T(8,128)S(1)} %get-tuple-element.61.elow, f32[16,128]{1,0:T(8,128)S(1)} %get-tuple-element.62.cnear, f32[4,4,256]{2,1,0:T(4,128)S(1)} %get-tuple-element.63.emid), custom_call_target="tpu_custom_call" | custom-call | tf_op jit(solution)/shard_map/pallas_call | solution.py:610
  (1 shorter events, 0.0 us)
Async XLA Ops:
  2.6 14.9 %collective-permute-start = (f32[160,512]{1,0:T(8,128)}, f32[160,512]{1,0:T(8,128)S(1)}, u32[]{:S(2)}, u32[]{:S(2)}) collective-permute-start(f32[160,512]{1,0:T(8,128)} %get-tuple-element.36), channel_id=1, source_target_pairs={{1,2},{3,4},{5,6},{7,8},{9,10},{11,12},{13,14},{2,1},{4,3},{6,5},{... | collective-permute-start | bytes 983048 | tf_op jit(solution)/shard_map/ppermute | solution.py:568
  3.3 14.3 %collective-permute-start.1 = (f32[160,512]{1,0:T(8,128)}, f32[160,512]{1,0:T(8,128)S(1)}, u32[]{:S(2)}, u32[]{:S(2)}) collective-permute-start(f32[160,512]{1,0:T(8,128)} %get-tuple-element.37), channel_id=1, source_target_pairs={{0,1},{2,3},{4,5},{6,7},{8,9},{10,11},{12,13},{14,15},{1,0},{3,2},... | collective-permute-start | bytes 983048 | tf_op jit(solution)/shard_map/ppermute | solution.py:568
  10.6 20.2 %collective-permute-start.3 = (f32[168,512]{1,0:T(8,128)}, f32[168,512]{1,0:T(8,128)S(1)}, u32[]{:S(2)}, u32[]{:S(2)}) collective-permute-start(f32[168,512]{1,0:T(8,128)} %get-tuple-element.53), channel_id=1, source_target_pairs={{16,32},{48,64},{80,96},{112,128},{144,160},{176,192},{208,224},{2... | collective-permute-start | bytes 1032200 | tf_op jit(solution)/shard_map/ppermute | solution.py:568
  14.8 0.9 %copy-start = (f32[8,8,512]{2,1,0:T(8,128)S(1)}, f32[8,8,512]{2,1,0:T(8,128)}, u32[]{:S(2)}) copy-start(f32[8,8,512]{2,1,0:T(8,128)} %param.3) | copy-start | bytes 393220
  15.7 0.9 %copy-start.1 = (f32[8,8,512]{2,1,0:T(8,128)S(1)}, f32[8,8,512]{2,1,0:T(8,128)}, u32[]{:S(2)}) copy-start(f32[8,8,512]{2,1,0:T(8,128)} %param.4) | copy-start | bytes 393220
  16.6 0.9 %copy-start.2 = (f32[8,8,512]{2,1,0:T(8,128)S(1)}, f32[8,8,512]{2,1,0:T(8,128)}, u32[]{:S(2)}) copy-start(f32[8,8,512]{2,1,0:T(8,128)} %param.5) | copy-start | bytes 393220
  18.0 12.8 %collective-permute-start.2 = (f32[152,512]{1,0:T(8,128)S(1)}, f32[152,512]{1,0:T(8,128)S(1)}, u32[]{:S(2)}, u32[]{:S(2)}) collective-permute-start(f32[152,512]{1,0:T(8,128)S(1)} %get-tuple-element.52), channel_id=1, source_target_pairs={{16,32},{48,64},{80,96},{112,128},{144,160},{176,192},{208,224},{2... | collective-permute-start | bytes 933896 | tf_op jit(solution)/shard_map/ppermute | solution.py:568

commit v11 on v10

--- a/solution.py
+++ b/solution.py
@@ -138,7 +138,7 @@
         dst[...] = src[...]
 
 
-def pack_x(phi, rhs, coef, far, near, pe, re, ce, other, stage):
+def pack_x(phi, rhs, coef, _own_end, far, near, pe, re, ce, other, mate, stage):
     zero = jnp.zeros((8, 128), F32)
     odd = lax.rem(lax.axis_index("gy"), 2)
     k = 0
@@ -159,6 +159,7 @@
         k += n
     first = is_first()
     pack_end(other, lambda ext, x, t: ext[pl.ds(pl.multiple_of(24 * x + 8 * t, 8), 8), :], pe, re, ce, first, False)
+    pack_end(mate, lambda ext, x, t: ext[pl.ds(pl.multiple_of(24 * x + 8 * t, 8), 8), :], pe, re, ce, jnp.logical_not(first))
 
 
 def pack_end(out, tile, pe, re, ce, is_low, with_own=True):
@@ -219,10 +220,7 @@
     return exact_matmul(packed[...], halving(512, 256)).reshape(n, 16, 256)
 
 
-def inner(pe, re, ce, hx, hc, hy, hz, dg, rd, p1, p2, res, cmid, mate, sums, packed):
-    first = is_first()
-    block = mate.at[jnp.where(first, 1, 0)]
-    pack_end(block, lambda ext, x, t: ext[x, 8 * t:8 * t + 8, :], pe, re, ce, jnp.logical_not(first))
+def inner(pe, re, ce, hx, hc, hy, hz, dg, rd, p1, p2, res, cmid, sums, packed):
     hc[0] = harmonic(ce[3], ce[4])
 
     def start(side, carry):
@@ -361,11 +359,11 @@
 
 def mate_side(*refs):
     side = jnp.where(is_first(), 1, 0)
-    one_side(side, refs[12].at[side], None, *refs[:12], *refs[13:])
+    one_side(side, refs[12], None, *refs[:12], *refs[14:])
 
 
 def other_side(*refs):
-    one_side(jnp.where(is_first(), 0, 1), refs[12], refs[13], *refs[:12], *refs[14:])
+    one_side(jnp.where(is_first(), 0, 1), refs[12], refs[13], *refs[:12], *refs[15:])
 
 
 def middle(mate, other, cmid, phi_mate, phi_other, phi_out, emid, out, sums, left):
@@ -578,28 +576,27 @@
     own_end = swap(own_end, "gx", True)
     own = call(hold, [(64, 512)] * 3, n_in=3,
                cost=pl.CostEstimate(flops=16_000_000, bytes_accessed=4_000_000, transcendentals=0))(*own)
-    *ext, other = call(pack_x, [(192, 512)] * 3 + [(END_ROWS - OWN_ROWS, 512)], [(1536, 128)], n_in=5)(*own, far, near)
+    *ext, other, mate = call(pack_x, [(192, 512)] * 3 + [(END_ROWS - OWN_ROWS, 512), (END_ROWS, 512)], [(1536, 128)], n_in=6)(*own, own_end, far, near)
     other = swap(other, "gx", True)
+    mate = swap(mate, "gx", False)
     ext = [a.reshape(8, 24, 512) for a in ext]
 
     def slabs(*n):
         return (*n, 24, 512)
 
-    *inside, cmid, mate = call(
+    *inside, cmid = call(
         inner,
-        [slabs(2, 3), slabs(1)] + [slabs(2, 4)] * 3 + [slabs(2, 3)] * 2 + [slabs(2, 2), slabs(2), (4, 16, 256), (2, END_ROWS, 512)],
+        [slabs(2, 3), slabs(1)] + [slabs(2, 4)] * 3 + [slabs(2, 3)] * 2 + [slabs(2, 2), slabs(2), (4, 16, 256)],
         [(4, 4, 24, 128), (64, 512)], n_in=3,
-        cost=pl.CostEstimate(flops=1_000, bytes_accessed=1_000, transcendentals=0),
+        cost=pl.CostEstimate(flops=16_000_000, bytes_accessed=4_000_000, transcendentals=0),
     )(*ext)
-    chips = [[i, i + 1] for i in range(0, lax.axis_size("gx"), 2)]
-    mate = lax.all_to_all(mate, "gx", 0, 0, tiled=True, axis_index_groups=chips)
     scratch = [slabs(9)] * 8 + [(4, 8, 24, 128), (128, 512)]
     phi_mate, half = call(
-        mate_side, [(4, 8, 512), (8, 16, 256)], scratch, n_in=13,
+        mate_side, [(4, 8, 512), (8, 16, 256)], scratch, n_in=14,
         cost=pl.CostEstimate(flops=1_000, bytes_accessed=1_000, transcendentals=0),
-    )(*ext, *inside, mate)
+    )(*ext, *inside, mate, other)
     phi_other, other_half = call(
-        other_side, [(4, 8, 512), (8, 16, 256)], scratch, n_in=14)(*ext, *inside, other, own_end)
+        other_side, [(4, 8, 512), (8, 16, 256)], scratch, n_in=15)(*ext, *inside, other, own_end, phi_mate)
     phi_fine, emid, spread = call(
         middle, [(8, 8, 512), (4, 4, 256), (16, 16, 128)], [(128, 128)], n_in=5, copies=2, out_hbm=1)(
         half, other_half, cmid, phi_mate, phi_other)

time: 84.4 us -> 89.4 us (1.059)
  waiting for transfers between devices: 0.01 us -> 12.3 us
  blocking collectives: 51.1 us -> 46.9 us
  local copies, waits for them, and re-layouts: 2.71 us -> 0.01 us
    ppermute x4 -> x5, waiting for transfers between devices: 0.01 us -> 12.3 us  [swap(): return lax.ppermute(values, axis, pairs + [(j, i) for i, j in pairs])]
    all_to_all x1 -> x0, blocking collectives: 4.42 us -> none  [shards(): mate = lax.all_to_all(mate, 'gx', 0, 0, tiled=True, axis_index_groups=chips)]
    unnamed x6, local copies, waits for them, and re-layouts: 2.71 us -> 0.01 us
    all_to_all x1, blocking collectives: 21.4 us -> 22.9 us  [shards(): gathered = lax.all_to_all(spread, 'gx', 0, 0, tiled=True)]
    all_to_all x1, blocking collectives: 25.3 us -> 24 us  [shards(): gathered = lax.all_to_all(spread, 'gy', 0, 0, tiled=True)]
    ppermute x4 -> x5, starting transfers between devices: 17 us -> 16.5 us  [swap(): return lax.ppermute(values, axis, pairs + [(j, i) for i, j in pairs])]
  transfers between devices with their start and end apart: 4 -> 5, of which waited for: 0 -> 2; matrix products, arithmetic and copies ran while one was open for 0% -> 0% of each run, Pallas kernels for 5% -> 2%
where the time goes in v11:
time: 89.4 us; the launch traced here: 89.1 us
  blocking collectives  46.9 us (52%)
  starting transfers between devices  16.5 us (18%)
  Pallas kernels  12.5 us (14%)
  waiting for transfers between devices  12.3 us (14%)
    all_to_all x1, blocking collectives, shards(): gathered = lax.all_to_all(spread, 'gy', 0, 0, tiled=True)  24 us
    all_to_all x1, blocking collectives, shards(): gathered = lax.all_to_all(spread, 'gx', 0, 0, tiled=True)  22.9 us
    ppermute x5, starting transfers between devices, swap(): return lax.ppermute(values, axis, pairs + [(j, i) for i, j in pairs])  16.5 us
    ppermute x5, waiting for transfers between devices, swap(): return lax.ppermute(values, axis, pairs + [(j, i) for i, j in pairs])  12.3 us
    pallas_call x1, Pallas kernels, shards(): call(bottom, [(4, 4, 256)], [(17, 16, 128)] + [(16, 16, 128)] * 7, n_in=4)  3.12 us
    pallas_call x1, Pallas kernels, shards(): call(pack_y, [(8 * NROWS, 512)] * 2 + [(OWN_ROWS, 512)], [(64, 512)] * 3...  2.04 us
    pallas_call x1, Pallas kernels, shards(): call(mate_side, [(4, 8, 512), (8, 16, 256)], scratch, n_in=14, cost=pl.Co...  1.8 us
    pallas_call x1, Pallas kernels, shards(): call(other_side, [(4, 8, 512), (8, 16, 256)], scratch, n_in=15)  1.79 us
  transfers between devices with their start and end apart: 5, of which 2 were waited for; matrix products, arithmetic and copies ran while one was open for 0% of the time, Pallas kernels for 2%

profile of v11, /device:TPU:1, one launch (start us, length us, event | category | flops | bytes accessed | tf_op | source)
XLA Modules:
  0.0 89.1 jit_solution(16781551696198474096)
XLA Ops:
  0.6 0.0 copy-start
  0.6 0.0 copy-start.1
  0.6 0.0 copy-start.2
  0.7 2.0 %shard_map.51 = (f32[160,512]{1,0:T(8,128)}, f32[160,512]{1,0:T(8,128)}, f32[168,512]{1,0:T(8,128)}) custom-call(f32[64,512]{1,0:T(8,128)} %bitcast.16, f32[64,512]{1,0:T(8,128)} %bitcast.18, f32[64,512]{1,0:T(8,128)} %bitcast.20), custom_call_target="tpu_custom_call" | custom-call | tf_op jit(solution)/shard_map/pallas_call | solution.py:571
  2.7 4.5 %collective-permute-start = (f32[168,512]{1,0:T(8,128)}, f32[168,512]{1,0:T(8,128)S(1)}, u32[]{:S(2)}, u32[]{:S(2)}) collective-permute-start(f32[168,512]{1,0:T(8,128)} %get-tuple-element.36), channel_id=1, source_target_pairs={{16,32},{48,64},{80,96},{112,128},{144,160},{176,192},{208,224},{2... | collective-permute-start | bytes 1032200 | tf_op jit(solution)/shard_map/ppermute | solution.py:566
  7.2 0.7 collective-permute-start.1
  7.9 6.4 %collective-permute-start.2 = (f32[160,512]{1,0:T(8,128)}, f32[160,512]{1,0:T(8,128)S(1)}, u32[]{:S(2)}, u32[]{:S(2)}) collective-permute-start(f32[160,512]{1,0:T(8,128)} %get-tuple-element.38), channel_id=1, source_target_pairs={{0,1},{2,3},{4,5},{6,7},{8,9},{10,11},{12,13},{14,15},{1,0},{3,2},... | collective-permute-start | bytes 983048 | tf_op jit(solution)/shard_map/ppermute | solution.py:566
  14.3 0.0 copy-done
  14.3 0.0 copy-done.1
  14.4 0.0 copy-done.2
  14.4 0.0 collective-permute-done.1.far
  14.4 8.0 %collective-permute-done.2.near = f32[160,512]{1,0:T(8,128)S(1)} collective-permute-done((f32[160,512]{1,0:T(8,128)}, f32[160,512]{1,0:T(8,128)S(1)}, u32[]{:S(2)}, u32[]{:S(2)}) %collective-permute-start.2) | collective-permute-done | bytes 327712 | tf_op jit(solution)/shard_map/ppermute | solution.py:566
  22.4 0.0 collective-permute-done._own_end.refs_13_
  22.4 0.4 shard_map.52
  22.9 2.7 %collective-permute-start.3 = (f32[320,512]{1,0:T(8,128)S(1)}, f32[320,512]{1,0:T(8,128)S(1)}, u32[]{:S(2)}, u32[]{:S(2)}) collective-permute-start(f32[320,512]{1,0:T(8,128)S(1)} %get-tuple-element.51), channel_id=1, source_target_pairs={{0,16},{32,48},{64,80},{96,112},{128,144},{160,176},{192,208},{224... | collective-permute-start | bytes 1966088 | tf_op jit(solution)/shard_map/ppermute | solution.py:566
  25.6 2.2 %collective-permute-start.4 = (f32[152,512]{1,0:T(8,128)S(1)}, f32[152,512]{1,0:T(8,128)S(1)}, u32[]{:S(2)}, u32[]{:S(2)}) collective-permute-start(f32[152,512]{1,0:T(8,128)S(1)} %get-tuple-element.52), channel_id=1, source_target_pairs={{16,32},{48,64},{80,96},{112,128},{144,160},{176,192},{208,224},{2... | collective-permute-start | bytes 933896 | tf_op jit(solution)/shard_map/ppermute | solution.py:566
  27.8 1.7 %shard_map.53 = (f32[2,3,24,512]{3,2,1,0:T(8,128)S(1)}, f32[1,24,512]{2,1,0:T(8,128)S(1)}, f32[2,4,24,512]{3,2,1,0:T(8,128)S(1)}, f32[2,4,24,512]{3,2,1,0:T(8,12...) custom-call(f32[8,24,512]{2,1,0:T(8,128)S(1)} %bitcast.7, ...), custom_call_target="tpu_custom_call" | custom-call | flops 16000000 | bytes 4000000 | tf_op jit(solution)/shard_map/pallas_call | solution.py:587
  29.5 4.3 %collective-permute-done.4.refs_13_.refs_12_ = f32[152,512]{1,0:T(8,128)S(1)} collective-permute-done((f32[152,512]{1,0:T(8,128)S(1)}, f32[152,512]{1,0:T(8,128)S(1)}, u32[]{:S(2)}, u32[]{:S(2)}) %collective-permute-start.4) | collective-permute-done | bytes 311328 | tf_op jit(solution)/shard_map/ppermute | solution.py:566
  33.8 0.0 collective-permute-done.3.refs_12_
  33.8 1.8 %shard_map.54 = (f32[4,8,512]{2,1,0:T(8,128)S(1)}, f32[8,16,256]{2,1,0:T(8,128)S(1)}) custom-call(f32[8,24,512]{2,1,0:T(8,128)S(1)} %bitcast.8, f32[8,24,512]{2,1,0:T(8,128)S(1)} %bitcast.11, f32[8,24,512]{2,1,0:T(8,128)S(1)} %bitcast.14, f32[2,3,24,512]{3,2,1,0:T(8,128)S(1)} %get-tuple-element.42.refs_3_, f32[1,24,512]{2,1,0:T(8,128)S(1)} %get-tuple-element.43.refs_4_, ...), custom_call_target="tpu_custom_call" | custom-call | flops 1000 | bytes 1000 | tf_op jit(solution)/shard_map/pallas_call | solution.py:594
  35.6 1.8 %shard_map.55 = (f32[4,8,512]{2,1,0:T(8,128)S(1)}, f32[8,16,256]{2,1,0:T(8,128)S(1)}) custom-call(f32[8,24,512]{2,1,0:T(8,128)S(1)} %bitcast.9, f32[8,24,512]{2,1,0:T(8,128)S(1)} %bitcast.12, f32[8,24,512]{2,1,0:T(8,128)S(1)} %bitcast.15, f32[2,3,24,512]{3,2,1,0:T(8,128)S(1)} %get-tuple-element.42.refs_3_, f32[1,24,512]{2,1,0:T(8,128)S(1)} %get-tuple-element.43.refs_4_, ...), custom_call_target="tpu_custom_call" | custom-call | tf_op jit(solution)/shard_map/pallas_call | solution.py:598
  37.4 1.0 %shard_map.56 = (f32[8,8,512]{2,1,0:T(8,128)}, f32[4,4,256]{2,1,0:T(4,128)S(1)}, f32[16,16,128]{2,1,0:T(8,128)S(1)}) custom-call(f32[8,16,256]{2,1,0:T(8,128)S(1)} %get-tuple-element.53.mate, f32[8,16,256]{2,1,0:T(8,128)S(1)} %get-tuple-element.55.other, f32[4,16,256]{2,1,0:T(8,128)S(1)} %get-tuple-element.56.cmid, ...), custom_call_target="tpu_custom_call" | custom-call | tf_op jit(solution)/shard_map/pallas_call | solution.py:600
  38.4 24.0 %all_to_all.10 = f32[16,16,128]{2,1,0:T(8,128)S(1)} all-to-all(f32[16,16,128]{2,1,0:T(8,128)S(1)} %get-tuple-element.59), channel_id=1, replica_groups=mesh['gx'=32,'gy'=16] {'gy'}, dimensions={0} | all-to-all | bytes 262144 | tf_op jit(solution)/shard_map/all_to_all | solution.py:603
  62.4 0.6 shard_map.57
  63.0 22.9 %all_to_all.11.gathered = f32[32,32,128]{2,1,0:T(8,128)S(1)} all-to-all(f32[32,32,128]{2,1,0:T(8,128)S(1)} %get-tuple-element.60), channel_id=1, replica_groups=mesh['gx'=32,'gy'=16] {'gx'}, dimensions={0} | all-to-all | bytes 1048576 | tf_op jit(solution)/shard_map/all_to_all | solution.py:606
  85.9 3.1 %shard_map.58 = f32[4,4,256]{2,1,0:T(4,128)} custom-call(f32[32,32,128]{2,1,0:T(8,128)S(1)} %all_to_all.11.gathered, f32[8,128]{1,0:T(8,128)S(1)} %get-tuple-element.61.elow, f32[16,128]{1,0:T(8,128)S(1)} %get-tuple-element.62.cnear, f32[4,4,256]{2,1,0:T(4,128)S(1)} %get-tuple-element.63.emid), custom_call_target="tpu_custom_call" | custom-call | tf_op jit(solution)/shard_map/pallas_call | solution.py:607
  (1 shorter events, 0.0 us)
Async XLA Ops:
  0.6 13.7 %copy-start = (f32[8,8,512]{2,1,0:T(8,128)S(1)}, f32[8,8,512]{2,1,0:T(8,128)}, u32[]{:S(2)}) copy-start(f32[8,8,512]{2,1,0:T(8,128)} %param.3) | copy-start | bytes 393220
  0.6 13.7 %copy-start.1 = (f32[8,8,512]{2,1,0:T(8,128)S(1)}, f32[8,8,512]{2,1,0:T(8,128)}, u32[]{:S(2)}) copy-start(f32[8,8,512]{2,1,0:T(8,128)} %param.4) | copy-start | bytes 393220
  0.6 13.7 %copy-start.2 = (f32[8,8,512]{2,1,0:T(8,128)S(1)}, f32[8,8,512]{2,1,0:T(8,128)}, u32[]{:S(2)}) copy-start(f32[8,8,512]{2,1,0:T(8,128)} %param.5) | copy-start | bytes 393220
  2.7 19.7 %collective-permute-start = (f32[168,512]{1,0:T(8,128)}, f32[168,512]{1,0:T(8,128)S(1)}, u32[]{:S(2)}, u32[]{:S(2)}) collective-permute-start(f32[168,512]{1,0:T(8,128)} %get-tuple-element.36), channel_id=1, source_target_pairs={{16,32},{48,64},{80,96},{112,128},{144,160},{176,192},{208,224},{2... | collective-permute-start | bytes 1032200 | tf_op jit(solution)/shard_map/ppermute | solution.py:566
  7.2 7.2 %collective-permute-start.1 = (f32[160,512]{1,0:T(8,128)}, f32[160,512]{1,0:T(8,128)S(1)}, u32[]{:S(2)}, u32[]{:S(2)}) collective-permute-start(f32[160,512]{1,0:T(8,128)} %get-tuple-element.37), channel_id=1, source_target_pairs={{1,2},{3,4},{5,6},{7,8},{9,10},{11,12},{13,14},{2,1},{4,3},{6,5},{... | collective-permute-start | bytes 983048 | tf_op jit(solution)/shard_map/ppermute | solution.py:566
  7.9 14.5 %collective-permute-start.2 = (f32[160,512]{1,0:T(8,128)}, f32[160,512]{1,0:T(8,128)S(1)}, u32[]{:S(2)}, u32[]{:S(2)}) collective-permute-start(f32[160,512]{1,0:T(8,128)} %get-tuple-element.38), channel_id=1, source_target_pairs={{0,1},{2,3},{4,5},{6,7},{8,9},{10,11},{12,13},{14,15},{1,0},{3,2},... | collective-permute-start | bytes 983048 | tf_op jit(solution)/shard_map/ppermute | solution.py:566
  22.9 10.9 %collective-permute-start.3 = (f32[320,512]{1,0:T(8,128)S(1)}, f32[320,512]{1,0:T(8,128)S(1)}, u32[]{:S(2)}, u32[]{:S(2)}) collective-permute-start(f32[320,512]{1,0:T(8,128)S(1)} %get-tuple-element.51), channel_id=1, source_target_pairs={{0,16},{32,48},{64,80},{96,112},{128,144},{160,176},{192,208},{224... | collective-permute-start | bytes 1966088 | tf_op jit(solution)/shard_map/ppermute | solution.py:566
  25.6 8.2 %collective-permute-start.4 = (f32[152,512]{1,0:T(8,128)S(1)}, f32[152,512]{1,0:T(8,128)S(1)}, u32[]{:S(2)}, u32[]{:S(2)}) collective-permute-start(f32[152,512]{1,0:T(8,128)S(1)} %get-tuple-element.52), channel_id=1, source_target_pairs={{16,32},{48,64},{80,96},{112,128},{144,160},{176,192},{208,224},{2... | collective-permute-start | bytes 933896 | tf_op jit(solution)/shard_map/ppermute | solution.py:566
